TPU v7x, 32 devices: a whole 2x2x4 slice. The times are simulated.
32 devices in a mesh: grp: 2 (over x), tsec: 1, lat: 16 (over z, y, core).
Axes of the slice: x: 2, y: 2, z: 4, core: 2. Of those that a mesh axis runs over, the one named last changes fastest.
Arguments:
- sources: bfloat16 [2048, 1792], P(('grp', 'lat'), 'tsec'), parts along dimension 0, may hold values from -6 to 6
- errors: bfloat16 [1, 2048, 1792], P('tsec', ('grp', 'lat')), parts along dimension 1, may hold values from -6 to 6
- enc_weight: bfloat16 [1792, 8192], P('tsec', 'lat'), may hold values from -0.125 to 0.125
- enc_bias: float32 [8192], P('lat'), may hold values from -3 to 3
- dec_weight: bfloat16 [1, 8192, 1792], P('tsec', 'lat'), may hold values from -0.1875 to 0.1875
- active: int32 [2048, 8192], P('grp', 'lat'), parts along dimension 0, may hold values 0 or 1
Outputs:
- code_grad: float32 [2048, 8192], P(('grp', 'tsec'), 'lat'), parts along dimension 0
- dec_grad: float32 [1, 16384, 1792], P('tsec', ('grp', 'lat')), parts along dimension 1
- enc_grad: float32 [3584, 8192], P(('grp', 'tsec'), 'lat'), parts along dimension 0
- input_grad: float32 [2048, 1792], P(('grp', 'lat'), 'tsec'), parts along dimension 0
There are 2 independent parts, one for each index of `grp`. A program takes and returns all parts, laid end to end along the dimension named above; an argument that names none is the same for every part. Nothing has to cross between parts.
All inputs are finite; a program needn't handle non-finite values. No bound on the sum of `active` on one device may be relied on, other than what follows from the above.
Results may differ from a plain program's by a relative error of at most 0.0029.
Values may be sent and summed in bfloat16 or wider, within the bound.
No kernel may reach another device: no remote copies, remote signals or barrier semaphores. Data moves between devices by JAX's collectives and lax.ppermute only.
A program may use at most 64 MiB of HBM per device.

v0:
```python
import jax
import jax.numpy as jnp
from jax import lax
from jax.sharding import PartitionSpec as P


def local(sources, errors, enc_weight, enc_bias, dec_weight, active):
    mine = lax.axis_index("tsec")
    rows_all = lax.all_gather(sources, "lat", axis=0, tiled=True)
    flags = active.astype(jnp.float32)
    share = rows_all.shape[0] // lax.axis_size("tsec")
    partial_value = jnp.dot(rows_all, enc_weight, preferred_element_type=jnp.float32)
    pre = lax.psum(partial_value, "tsec") + enc_bias
    codes = (pre * flags).astype(jnp.bfloat16)
    targets = lax.all_gather(errors, "lat", axis=1, tiled=True)
    dec_grad = jnp.einsum("rl,trd->tld", codes, targets, preferred_element_type=jnp.float32)
    partial_code = jnp.einsum(
        "trd,tld->rl", targets, dec_weight, preferred_element_type=jnp.float32
    )
    total = lax.psum(partial_code, "tsec")
    pre_grad = (total * flags).astype(jnp.bfloat16)
    code_grad = lax.dynamic_slice_in_dim(total, mine * share, share, 0)
    enc_grad = jnp.einsum("rd,rl->dl", rows_all, pre_grad, preferred_element_type=jnp.float32)
    input_grad = lax.psum_scatter(
        jnp.einsum("rl,dl->rd", pre_grad, enc_weight, preferred_element_type=jnp.float32),
        "lat",
        scatter_dimension=0,
        tiled=True,
    )
    return (code_grad, dec_grad, enc_grad, input_grad)


def solution(mesh):
    return jax.shard_map(
        local,
        mesh=mesh,
        in_specs=(
            P(("grp", "lat"), "tsec"),
            P("tsec", ("grp", "lat"), None),
            P("tsec", "lat"),
            P("lat"),
            P("tsec", "lat", None),
            P("grp", "lat"),
        ),
        out_specs=(
            P(("grp", "tsec"), "lat"),
            P("tsec", ("grp", "lat"), None),
            P(("grp", "tsec"), "lat"),
            P(("grp", "lat"), "tsec"),
        ),
        check_vma=False,
    )
```

profile of v0, /device:TPU:0, one launch (start us, length us, event | category | flops | bytes accessed | tf_op | source)
XLA Modules:
  0.0 211.3 jit_solution(12799400764702491249)
XLA Ops:
  7.2 0.0 copy-start
  7.2 0.0 all-gather.3.cloned.1.call-start
  7.2 0.7 all-gather.3.cloned.1.call-update
  7.9 0.0 all-gather.5.cloned.1.call-start
  8.0 0.7 all-gather.5.cloned.1.call-update
  8.7 0.0 reduce-scatter.2.cloned.1.call-start
  8.7 51.8 %all-gather.3.cloned.1.call-done = bf16[1,1024,1792]{2,1,0:T(8,128)(2,1)} async-done(((bf16[1,64,1792]{2,1,0:T(8,128)(2,1)}), bf16[1,1024,1792]{2,1,0:T(8,128)(2,1)}) %all-gather.3.cloned.1.call-update) | async-done | bytes 3670032 | tf_op jit(solution)/shard_map/all_gather | solution.py:15
  60.5 6.6 %multiply_convert_fusion = (bf16[1024,512]{1,0:T(8,128)(2,1)S(1)}, f32[1024,512]{1,0:T(8,128)}) fusion(s32[1024,512]{1,0:T(8,128)} %param.11, bf16[1,512,1792]{2,1,0:T(8,128)(2,1)} %param.10, bf16[1,1024,1792]{2,1,0:T(8,128)(2,1)} %all-gather.3.cloned.1.call-done), kind=kOutput, calls=%fused_computation.6 | convolution fusion | flops 1880621056 | bytes 10747904 | tf_op jit(solution)/shard_map/trd,tld->rl/dot_general | solution.py:17
  67.2 0.0 copy-done
  67.2 5.0 %fusion.8 = f32[1024,1792]{1,0:T(8,128)} fusion(bf16[1024,512]{1,0:T(8,128)(2,1)S(1)} %get-tuple-element.8, bf16[1792,512]{1,0:T(8,128)(2,1)S(1)} %copy-done), kind=kOutput, calls=%fused_computation.9 | convolution fusion | flops 1879048192 | bytes 10223616 | tf_op jit(solution)/shard_map/rl,dl->rd/dot_general | solution.py:25
  72.2 0.0 reduce-scatter.2.cloned.1.call-update
  72.2 37.2 %all-gather.5.cloned.1.call-done = bf16[1024,1792]{1,0:T(8,128)(2,1)} async-done(((bf16[64,1792]{1,0:T(8,128)(2,1)}), bf16[1024,1792]{1,0:T(8,128)(2,1)}) %all-gather.5.cloned.1.call-update) | async-done | bytes 3670032 | tf_op jit(solution)/shard_map/all_gather | solution.py:9
  109.4 6.0 %convolution_bitcast_fusion = f32[1792,512]{0,1:T(8,128)} fusion(bf16[1024,512]{1,0:T(8,128)(2,1)S(1)} %get-tuple-element.8, bf16[1024,1792]{1,0:T(8,128)(2,1)} %all-gather.5.cloned.1.call-done), kind=kOutput, calls=%fused_computation.5 | convolution fusion | flops 1879048192 | bytes 8388608 | tf_op jit(solution)/shard_map/rd,rl->dl/dot_general | solution.py:23
  115.4 0.0 copy-start.1
  115.4 5.2 %copy.10 = f32[1792,512]{1,0:T(8,128)} copy(f32[1792,512]{0,1:T(8,128)} %convolution_bitcast_fusion) | data formatting | bytes 7340032
  120.5 0.0 copy-done.1
  120.5 10.8 %fusion.4 = f32[1,512,1792]{2,1,0:T(8,128)} fusion(bf16[1,1024,1792]{2,1,0:T(8,128)(2,1)} %all-gather.3.cloned.1.call-done, s32[1024,512]{1,0:T(8,128)} %param.11, bf16[1024,1792]{1,0:T(8,128)(2,1)} %all-gather.5.cloned.1.call-done, bf16[1792,512]{1,0:T(8,128)(2,1)S(1)} %copy-done, f32[512]{0:T(512)S(1)} %copy-done.1), kind=kOutput, calls=%fused_computation.4 | convolution fusion | flops 3760193536 | bytes 14944256 | tf_op jit(solution)/shard_map/rl,trd->tld/dot_general | solution.py:16
  131.3 73.4 %reduce-scatter.2.cloned.1.call-done = f32[64,1792]{1,0:T(8,128)} async-done(((f32[1024,1792]{1,0:T(8,128)}), f32[64,1792]{1,0:T(8,128)}) %reduce-scatter.2.cloned.1.call-update) | async-done | bytes 458768 | tf_op jit(solution)/shard_map/reduce_scatter | solution.py:24
Async XLA Ops:
  7.2 60.0 %copy-start = (bf16[1792,512]{1,0:T(8,128)(2,1)S(1)}, bf16[1792,512]{1,0:T(8,128)(2,1)}, u32[]{:S(2)}) copy-start(bf16[1792,512]{1,0:T(8,128)(2,1)} %param.8) | copy-start | bytes 5505028
  7.2 53.4 %all-gather.3.cloned.1.call-start = ((), (), s32[]{:S(2)}) async-start(), calls=%async_computation.1 | async-start | bytes 3899392 | tf_op jit(solution)/shard_map/all_gather | solution.py:15
  7.9 101.5 %all-gather.5.cloned.1.call-start = ((), (), s32[]{:S(2)}) async-start(), calls=%async_computation.2 | async-start | bytes 3899392 | tf_op jit(solution)/shard_map/all_gather | solution.py:9
  8.7 196.1 %reduce-scatter.2.cloned.1.call-start = ((), (), s32[]{:S(2)}) async-start(), calls=%async_computation.3 | async-start | bytes 7798784 | tf_op jit(solution)/shard_map/reduce_scatter | solution.py:24
  115.4 5.2 %copy-start.1 = (f32[512]{0:T(512)S(1)}, f32[512]{0:T(512)}, u32[]{:S(2)}) copy-start(f32[512]{0:T(512)} %param.9) | copy-start | bytes 6148
Sparse Core Ops, SparseCore 0:
  10.3 50.1 all-gather.2
  62.8 46.5 all-gather.4
  114.0 90.7 reduce-scatter.1
where the time goes:
time: 212 us; the launch traced here: 211 us
  waiting for transfers between devices  164 us (77%)
  matrix products  28.5 us (13%)
  between operations  13.8 us (7%)
  local copies, waits for them, and re-layouts  5.18 us (2%)
    reduce_scatter x1, waiting for transfers between devices, local(): lax.psum_scatter(jnp.einsum('rl,dl->rd', pre_grad, enc_weight, preferred_...  73.4 us
    all_gather x1, waiting for transfers between devices, local(): targets = lax.all_gather(errors, 'lat', axis=1, tiled=True)  51.8 us
    all_gather x1, waiting for transfers between devices, local(): rows_all = lax.all_gather(sources, 'lat', axis=0, tiled=True)  37.2 us
    dot_general x1, matrix products, local(): jnp.einsum('rl,trd->tld', codes, targets, preferred_element_type=jnp.floa...  10.8 us
    dot_general x1, matrix products, local(): jnp.einsum('trd,tld->rl', targets, dec_weight, preferred_element_type=jnp...  6.64 us
    dot_general x1, matrix products, local(): jnp.einsum('rd,rl->dl', rows_all, pre_grad, preferred_element_type=jnp.fl...  5.97 us
    unnamed x5, local copies, waits for them, and re-layouts  5.18 us
    dot_general x1, matrix products, local(): jnp.einsum('rl,dl->rd', pre_grad, enc_weight, preferred_element_type=jnp....  5.04 us
  transfers between devices with their start and end apart: 3, of which 3 were waited for; matrix products, arithmetic and copies ran while one was open for 16% of the time, Pallas kernels for 0%

commit v1 on v0

v1 whole, which is shorter than its diff:
```python
import jax
import jax.numpy as jnp
from jax import lax
from jax.sharding import PartitionSpec as P

BF = jnp.bfloat16
F32 = jnp.float32


def general(sources, errors, enc_weight, enc_bias, dec_weight, active):
    mine = lax.axis_index("tsec")
    rows_all = lax.all_gather(sources, "lat", axis=0, tiled=True)
    flags = active.astype(F32)
    share = rows_all.shape[0] // lax.axis_size("tsec")
    partial_value = jnp.dot(rows_all, enc_weight, preferred_element_type=F32)
    pre = lax.psum(partial_value, "tsec") + enc_bias
    codes = (pre * flags).astype(BF)
    targets = lax.all_gather(errors, "lat", axis=1, tiled=True)
    dec_grad = jnp.einsum("rl,trd->tld", codes, targets, preferred_element_type=F32)
    partial_code = jnp.einsum("trd,tld->rl", targets, dec_weight, preferred_element_type=F32)
    total = lax.psum(partial_code, "tsec")
    pre_grad = (total * flags).astype(BF)
    code_grad = lax.dynamic_slice_in_dim(total, mine * share, share, 0)
    enc_grad = jnp.einsum("rd,rl->dl", rows_all, pre_grad, preferred_element_type=F32)
    input_grad = lax.psum_scatter(
        jnp.einsum("rl,dl->rd", pre_grad, enc_weight, preferred_element_type=F32),
        "lat",
        scatter_dimension=0,
        tiled=True,
    )
    return (code_grad, dec_grad, enc_grad, input_grad)


NZ, NY, NC = 4, 2, 2


def swap(x, partner):
    pairs = []
    for z in range(NZ):
        for y in range(NY):
            for c in range(NC):
                pz, py, pc = partner(z, y, c)
                pairs.append(((z * NY + y) * NC + c, (pz * NY + py) * NC + pc))
    return lax.ppermute(x, "lat", pairs)


def over_core(x):
    return swap(x, lambda z, y, c: (z, y, 1 - c))


def over_y(x):
    return swap(x, lambda z, y, c: (z, 1 - y, c))


def over_mirror(x):
    return swap(x, lambda z, y, c: (NZ - 1 - z, y, c))


def over_pair(x):
    return swap(x, lambda z, y, c: (z ^ 1, y, c))


def gather(x):
    m = over_mirror(x)
    p = over_pair(x)
    q = over_pair(m)
    blocks = []
    for v in (x, m, p, q):
        half = jnp.concatenate([v, over_y(v)], 0)
        blocks.append(jnp.concatenate([half, over_core(half)], 0))
    return blocks


def grid(sources, errors, enc_weight, enc_bias, dec_weight, active):
    rows = sources.shape[0]
    i = lax.axis_index("lat")
    z, y, c = i // (NY * NC), (i // NC) % NY, i % NC
    zs = (z, NZ - 1 - z, z ^ 1, NZ - 1 - (z ^ 1))
    parts = ((y, c), (1 - y, c), (y, 1 - c), (1 - y, 1 - c))
    place = [[((zz * NY + yy) * NC + cc) * rows for yy, cc in parts] for zz in zs]

    weight_peer = over_core(enc_weight)
    errs = gather(errors[0])
    srcs = gather(sources)
    code_grad = jnp.zeros(active.shape, F32)
    grads, flags, keeps, sends = [], [], [], []
    for j in range(NZ):
        total = lax.dot_general(
            errs[j], dec_weight[0], (((1,), (1,)), ((), ())), preferred_element_type=F32
        )
        act = jnp.concatenate(
            [lax.dynamic_slice_in_dim(active, r, rows, 0) for r in place[j]], 0
        ).astype(F32)
        flags.append(act)
        for n, r in enumerate(place[j]):
            code_grad = lax.dynamic_update_slice_in_dim(
                code_grad, total[n * rows : (n + 1) * rows], r, 0
            )
        grad = (total * act).astype(BF)
        grads.append(grad)
        peer = over_core(grad[2 * rows :])
        nt = (((1,), (1,)), ((), ()))
        term = lax.dot_general(
            grad[: 2 * rows], enc_weight, nt, preferred_element_type=F32
        ) + lax.dot_general(peer, weight_peer, nt, preferred_element_type=F32)
        keeps.append(term[:rows] + over_y(term[rows:].astype(BF)).astype(F32))
    own = keeps[0] + over_pair(keeps[2].astype(BF)).astype(F32)
    far = keeps[1] + over_pair(keeps[3].astype(BF)).astype(F32)
    input_grad = own + over_mirror(far.astype(BF)).astype(F32)

    src = jnp.concatenate(srcs, 0)
    pre = jnp.dot(src, enc_weight, preferred_element_type=F32) + enc_bias
    codes = (pre * jnp.concatenate(flags, 0)).astype(BF)
    tn = (((0,), (0,)), ((), ()))
    dec_grad = lax.dot_general(
        codes, jnp.concatenate(errs, 0), tn, preferred_element_type=F32
    )
    enc_grad = lax.dot_general(
        src, jnp.concatenate(grads, 0), tn, preferred_element_type=F32
    )
    return code_grad, dec_grad[None], enc_grad, input_grad


def solution(mesh):
    on_grid = mesh.shape["lat"] == NZ * NY * NC and mesh.shape["tsec"] == 1
    return jax.shard_map(
        grid if on_grid else general,
        mesh=mesh,
        in_specs=(
            P(("grp", "lat"), "tsec"),
            P("tsec", ("grp", "lat"), None),
            P("tsec", "lat"),
            P("lat"),
            P("tsec", "lat", None),
            P("grp", "lat"),
        ),
        out_specs=(
            P(("grp", "tsec"), "lat"),
            P("tsec", ("grp", "lat"), None),
            P(("grp", "tsec"), "lat"),
            P(("grp", "lat"), "tsec"),
        ),
        check_vma=False,
    )
```

time: 212 us -> 140 us (0.66)
  waiting for transfers between devices: 164 us -> 43 us
  starting transfers between devices: 0.11 us -> 35.3 us
  between operations: 13.8 us -> 1.18 us
  local copies, waits for them, and re-layouts: 5.18 us -> 17.7 us
  matrix products: 28.5 us -> 39.2 us
  other arithmetic: 0 us -> 3.48 us
    all_gather x2 -> x0, waiting for transfers between devices: 89 us -> none  [the longest x1 51.8 us: local(): targets = lax.all_gather(errors, 'lat', axis=1, tiled=True)]
    reduce_scatter x1 -> x0, waiting for transfers between devices: 73.4 us -> none  [local(): lax.psum_scatter(jnp.einsum('rl,dl->rd', pre_grad, enc_weight, preferred_...]
    ppermute x0 -> x34, waiting for transfers between devices: none -> 43 us  [swap(): return lax.ppermute(x, 'lat', pairs)]
    ppermute x0 -> x34, starting transfers between devices: none -> 35.3 us  [swap(): return lax.ppermute(x, 'lat', pairs)]
    dot_general x4 -> x14, matrix products: 28.5 us -> 39.2 us  [the longest x4 12.4 us: grid(): lax.dot_general(grad[:2 * rows], enc_weight, nt, preferred_element_type=F32)]
    dynamic_update_slice x0 -> x16, local copies, waits for them, and re-layouts: none -> 10.7 us  [grid(): lax.dynamic_update_slice_in_dim(code_grad, total[n * rows:(n + 1) * rows]...]
    unnamed x5 -> x40, local copies, waits for them, and re-layouts: 5.18 us -> 2.14 us
    convert_element_type x0 -> x5, other arithmetic: none -> 2.36 us  [the longest x2 2.21 us: grid(): act = jnp.concatenate([lax.dynamic_slice_in_dim(active, r, rows, 0) for r...]
  transfers between devices with their start and end apart: 3 -> 34, of which waited for: 3 -> 9; matrix products, arithmetic and copies ran while one was open for 16% -> 43% of each run, Pallas kernels for 0% -> 0%
where the time goes in v1:
time: 140 us
  waiting for transfers between devices  43 us (31%)
  matrix products  39.2 us (28%)
  starting transfers between devices  35.3 us (25%)
  local copies, waits for them, and re-layouts  17.7 us (13%)
  other arithmetic  3.48 us (2%)
    ppermute x34, waiting for transfers between devices, swap(): return lax.ppermute(x, 'lat', pairs)  43 us
    ppermute x34, starting transfers between devices, swap(): return lax.ppermute(x, 'lat', pairs)  35.3 us
    dot_general x4, matrix products, grid(): lax.dot_general(grad[:2 * rows], enc_weight, nt, preferred_element_type=F32)  12.4 us
    dot_general x1, matrix products, grid(): lax.dot_general(codes, jnp.concatenate(errs, 0), tn, preferred_element_ty...  10.7 us
    dynamic_update_slice x16, local copies, waits for them, and re-layouts, grid(): lax.dynamic_update_slice_in_dim(code_grad, total[n * rows:(n + 1) * rows]...  10.7 us
    dot_general x4, matrix products, grid(): lax.dot_general(peer, weight_peer, nt, preferred_element_type=F32)  9.48 us
    dot_general x1, matrix products, grid(): lax.dot_general(src, jnp.concatenate(grads, 0), tn, preferred_element_typ...  3.98 us
  transfers between devices with their start and end apart: 34, of which 9 were waited for; matrix products, arithmetic and copies ran while one was open for 43% of the time, Pallas kernels for 0%

profile of v1, /device:TPU:0, one launch (start us, length us, event | category | flops | bytes accessed | tf_op | source)
XLA Modules:
  0.0 139.9 jit_solution(194879594060007884)
XLA Ops:
  0.6 3.0 %collective-permute-start = (bf16[64,1792]{1,0:T(8,128)(2,1)}, bf16[64,1792]{1,0:T(8,128)(2,1)S(1)}, u32[]{:S(2)}, u32[]{:S(2)}) collective-permute-start(bf16[64,1792]{1,0:T(8,128)(2,1)} %bitcast.37), channel_id=1, source_target_pairs={{0,2},{1,3},{2,0},{3,1},{4,6},{5,7},{6,4},{7,5},{8,10},{9,11},{10,... | collective-permute-start | bytes 688136 | tf_op jit(solution)/shard_map/ppermute | solution.py:44
  3.7 3.6 %collective-permute-start.2 = (bf16[64,1792]{1,0:T(8,128)(2,1)}, bf16[64,1792]{1,0:T(8,128)(2,1)S(1)}, u32[]{:S(2)}, u32[]{:S(2)}) collective-permute-start(bf16[64,1792]{1,0:T(8,128)(2,1)} %bitcast.38), channel_id=1, source_target_pairs={{0,12},{1,13},{2,14},{3,15},{4,8},{5,9},{6,10},{7,11},{8,4},{9,5},... | collective-permute-start | bytes 688136 | tf_op jit(solution)/shard_map/ppermute | solution.py:44
  8.7 1.6 %constant_dynamic-update-slice_fusion.23 = bf16[1024,1792]{1,0:T(8,128)(2,1)} fusion(bf16[1,64,1792]{2,1,0:T(8,128)(2,1)} %param.7), kind=kLoop, calls=%fused_computation.120 | loop fusion | bytes 458752
  10.3 1.8 %constant_dynamic-slice_fusion.15 = (s32[64,512]{1,0:T(8,128)S(1)}, s32[64,512]{1,0:T(8,128)S(1)}, s32[64,512]{1,0:T(8,128)S(1)}, s32[64,512]{1,0:T(8,128)S(1)},...) fusion(s32[1024,512]{1,0:T(8,128)} %param.11, ...), kind=kLoop, calls=%fused_computation.136 | loop fusion | bytes 4194368 | tf_op jit(solution)/shard_map/dynamic_slice | solution.py:92
  15.8 1.6 %collective-permute-start.3 = (bf16[64,1792]{1,0:T(8,128)(2,1)S(1)}, bf16[64,1792]{1,0:T(8,128)(2,1)S(1)}, u32[]{:S(2)}, u32[]{:S(2)}) collective-permute-start(bf16[64,1792]{1,0:T(8,128)(2,1)S(1)} %collective-permute-done.2), channel_id=1, source_target_pairs={{0,2},{1,3},{2,0},{3,1},{4,6},{5,7},{6,4},{7,5},{8,10},{9,11},{10,... | collective-permute-start | bytes 688136 | tf_op jit(solution)/shard_map/ppermute | solution.py:44
  17.4 2.3 %collective-permute-done.5 = bf16[64,1792]{1,0:T(8,128)(2,1)S(1)} collective-permute-done((bf16[64,1792]{1,0:T(8,128)(2,1)}, bf16[64,1792]{1,0:T(8,128)(2,1)S(1)}, u32[]{:S(2)}, u32[]{:S(2)}) %collective-permute-start.5) | collective-permute-done | bytes 229408 | tf_op jit(solution)/shard_map/ppermute | solution.py:44
  19.7 4.0 %collective-permute-done.3 = bf16[64,1792]{1,0:T(8,128)(2,1)S(1)} collective-permute-done((bf16[64,1792]{1,0:T(8,128)(2,1)S(1)}, bf16[64,1792]{1,0:T(8,128)(2,1)S(1)}, u32[]{:S(2)}, u32[]{:S(2)}) %collective-permute-start.3) | collective-permute-done | bytes 229408 | tf_op jit(solution)/shard_map/ppermute | solution.py:44
  23.8 1.5 %collective-permute-start.6 = (bf16[64,1792]{1,0:T(8,128)(2,1)S(1)}, bf16[64,1792]{1,0:T(8,128)(2,1)S(1)}, u32[]{:S(2)}, u32[]{:S(2)}) collective-permute-start(bf16[64,1792]{1,0:T(8,128)(2,1)S(1)} %collective-permute-done.5), channel_id=1, source_target_pairs={{0,2},{1,3},{2,0},{3,1},{4,6},{5,7},{6,4},{7,5},{8,10},{9,11},{10,... | collective-permute-start | bytes 688136 | tf_op jit(solution)/shard_map/ppermute | solution.py:44
  25.4 5.5 %collective-permute-done.6 = bf16[64,1792]{1,0:T(8,128)(2,1)S(1)} collective-permute-done((bf16[64,1792]{1,0:T(8,128)(2,1)S(1)}, bf16[64,1792]{1,0:T(8,128)(2,1)S(1)}, u32[]{:S(2)}, u32[]{:S(2)}) %collective-permute-start.6) | collective-permute-done | bytes 229408 | tf_op jit(solution)/shard_map/ppermute | solution.py:44
  30.9 1.5 %collective-permute-start.14 = (bf16[64,1792]{1,0:T(8,128)(2,1)S(1)}, bf16[64,1792]{1,0:T(8,128)(2,1)S(1)}, u32[]{:S(2)}, u32[]{:S(2)}) collective-permute-start(bf16[64,1792]{1,0:T(8,128)(2,1)S(1)} %collective-permute-done.13), channel_id=1, source_target_pairs={{0,2},{1,3},{2,0},{3,1},{4,6},{5,7},{6,4},{7,5},{8,10},{9,11},{10,... | collective-permute-start | bytes 688136 | tf_op jit(solution)/shard_map/ppermute | solution.py:44
  32.5 5.5 %collective-permute-start.8 = (bf16[64,1792]{1,0:T(8,128)(2,1)S(1)}, bf16[64,1792]{1,0:T(8,128)(2,1)S(1)}, u32[]{:S(2)}, u32[]{:S(2)}) collective-permute-start(bf16[64,1792]{1,0:T(8,128)(2,1)S(1)} %collective-permute-done.2), channel_id=1, source_target_pairs={{0,4},{1,5},{2,6},{3,7},{4,0},{5,1},{6,2},{7,3},{8,12},{9,13},{10,... | collective-permute-start | bytes 688136 | tf_op jit(solution)/shard_map/ppermute | solution.py:44
  37.9 1.5 %collective-permute-start.17 = (bf16[64,1792]{1,0:T(8,128)(2,1)S(1)}, bf16[64,1792]{1,0:T(8,128)(2,1)S(1)}, u32[]{:S(2)}, u32[]{:S(2)}) collective-permute-start(bf16[64,1792]{1,0:T(8,128)(2,1)S(1)} %collective-permute-done.16), channel_id=1, source_target_pairs={{0,2},{1,3},{2,0},{3,1},{4,6},{5,7},{6,4},{7,5},{8,10},{9,11},{10,... | collective-permute-start | bytes 688136 | tf_op jit(solution)/shard_map/ppermute | solution.py:44
  39.5 4.4 %collective-permute-done.17 = bf16[64,1792]{1,0:T(8,128)(2,1)S(1)} collective-permute-done((bf16[64,1792]{1,0:T(8,128)(2,1)S(1)}, bf16[64,1792]{1,0:T(8,128)(2,1)S(1)}, u32[]{:S(2)}, u32[]{:S(2)}) %collective-permute-start.17) | collective-permute-done | bytes 229408 | tf_op jit(solution)/shard_map/ppermute | solution.py:44
  44.0 5.7 %collective-permute-start.19 = (bf16[64,1792]{1,0:T(8,128)(2,1)S(1)}, bf16[64,1792]{1,0:T(8,128)(2,1)S(1)}, u32[]{:S(2)}, u32[]{:S(2)}) collective-permute-start(bf16[64,1792]{1,0:T(8,128)(2,1)S(1)} %collective-permute-done.13), channel_id=1, source_target_pairs={{0,4},{1,5},{2,6},{3,7},{4,0},{5,1},{6,2},{7,3},{8,12},{9,13},{10,... | collective-permute-start | bytes 688136 | tf_op jit(solution)/shard_map/ppermute | solution.py:44
  51.3 1.6 %broadcast_in_dim.7 = f32[1024,512]{1,0:T(8,128)} broadcast(f32[]{:T(128)} %constant.42.clone.1), dimensions={} | broadcast | bytes 2097156 | tf_op jit(solution)/shard_map/broadcast_in_dim | solution.py:85
  55.6 2.3 %collective-permute-done.9 = bf16[64,1792]{1,0:T(8,128)(2,1)S(1)} collective-permute-done((bf16[64,1792]{1,0:T(8,128)(2,1)S(1)}, bf16[64,1792]{1,0:T(8,128)(2,1)S(1)}, u32[]{:S(2)}, u32[]{:S(2)}) %collective-permute-start.9) | collective-permute-done | bytes 229408 | tf_op jit(solution)/shard_map/ppermute | solution.py:44
  59.3 6.8 %collective-permute-done.20 = bf16[64,1792]{1,0:T(8,128)(2,1)S(1)} collective-permute-done((bf16[64,1792]{1,0:T(8,128)(2,1)S(1)}, bf16[64,1792]{1,0:T(8,128)(2,1)S(1)}, u32[]{:S(2)}, u32[]{:S(2)}) %collective-permute-start.20) | collective-permute-done | bytes 229408 | tf_op jit(solution)/shard_map/ppermute | solution.py:44
  66.2 2.2 %fusion.49 = f32[128,1792]{1,0:T(8,128)S(1)} fusion(bf16[1792,512]{1,0:T(8,128)(2,1)} %param.8, bf16[256,512]{1,0:T(8,128)(2,1)S(1)} %get-tuple-element.26), kind=kOutput, calls=%fused_computation.79 | convolution fusion | flops 234881024 | bytes 2883584 | tf_op jit(solution)/shard_map/dot_general | solution.py:103
  77.2 3.2 %fusion.45 = f32[128,1792]{1,0:T(8,128)} fusion(bf16[1792,512]{1,0:T(8,128)(2,1)} %param.8, bf16[256,512]{1,0:T(8,128)(2,1)S(1)} %get-tuple-element.24), kind=kOutput, calls=%fused_computation.75 | convolution fusion | flops 234881024 | bytes 2883584 | tf_op jit(solution)/shard_map/dot_general | solution.py:103
  80.5 3.2 %fusion.47 = f32[128,1792]{1,0:T(8,128)} fusion(bf16[1792,512]{1,0:T(8,128)(2,1)} %param.8, bf16[256,512]{1,0:T(8,128)(2,1)S(1)} %get-tuple-element.22), kind=kOutput, calls=%fused_computation.77 | convolution fusion | flops 234881024 | bytes 2883584 | tf_op jit(solution)/shard_map/dot_general | solution.py:103
  87.0 3.8 %fusion.43 = f32[128,1792]{1,0:T(8,128)} fusion(bf16[1792,512]{1,0:T(8,128)(2,1)} %param.8, bf16[256,512]{1,0:T(8,128)(2,1)S(1)} %get-tuple-element.20), kind=kOutput, calls=%fused_computation.73 | convolution fusion | flops 234881024 | bytes 2883584 | tf_op jit(solution)/shard_map/dot_general | solution.py:103
  90.8 4.0 %fusion.9 = f32[1792,512]{1,0:T(8,128)} fusion(bf16[1024,1792]{1,0:T(8,128)(2,1)S(1)} %constant_dynamic-update-slice_fusion, bf16[256,512]{1,0:T(8,128)(2,1)S(1)} %get-tuple-element.20, bf16[256,512]{1,0:T(8,128)(2,1)S(1)} %get-tuple-element.22, bf16[256,512]{1,0:T(8,128)(2,1)S(1)} %get-tuple-element.24, bf16[256,512]{1,0:T(8,128)(2,1)S(1)} %get-tuple-element.26), kind=kOutput, calls=%fused_computation.15 | convolution fusion | flops 1883242496 | bytes 8388608 | tf_op jit(solution)/shard_map/dot_general | solution.py:118
  94.8 10.7 %convolution_bitcast_fusion = f32[1,512,1792]{2,1,0:T(8,128)} fusion(bf16[1024,1792]{1,0:T(8,128)(2,1)} %copy-done.6, f32[256,512]{1,0:T(8,128)} %get-tuple-element.31, f32[256,512]{1,0:T(8,128)} %get-tuple-element.30, f32[256,512]{1,0:T(8,128)} %get-tuple-element.29, f32[256,512]{1,0:T(8,128)} %get-tuple-element.28, bf16[1024,1792]{1,0:T(8,128)(2,1)} %copy-done.7, ...), kind=kOutput, calls=%fused_computation | convolution fusion | flops 3761242112 | bytes 14944256 | tf_op jit(solution)/shard_map/dot_general | solution.py:115
  106.2 2.6 %convolution_add_fusion = f32[128,1792]{1,0:T(8,128)S(1)} fusion(f32[128,1792]{1,0:T(8,128)} %fusion.43, bf16[128,512]{1,0:T(8,128)(2,1)} %collective-permute-done.30, bf16[1792,512]{1,0:T(8,128)(2,1)} %collective-permute-done.23), kind=kOutput, calls=%fused_computation.1 | convolution fusion | flops 235110400 | bytes 3801088 | tf_op jit(solution)/shard_map/dot_general | solution.py:105
  109.7 2.3 %convolution_add_fusion.1 = f32[128,1792]{1,0:T(8,128)S(1)} fusion(f32[128,1792]{1,0:T(8,128)S(1)} %copy-done.1, bf16[128,512]{1,0:T(8,128)(2,1)} %collective-permute-done.28, bf16[1792,512]{1,0:T(8,128)(2,1)} %collective-permute-done.23), kind=kOutput, calls=%fused_computation.2 | convolution fusion | flops 235110400 | bytes 3801088 | tf_op jit(solution)/shard_map/dot_general | solution.py:105
  112.0 1.4 collective-permute-start.29
  113.4 2.3 %convolution_add_fusion.2 = f32[128,1792]{1,0:T(8,128)S(1)} fusion(f32[128,1792]{1,0:T(8,128)S(1)} %copy-done.2, bf16[128,512]{1,0:T(8,128)(2,1)} %collective-permute-done.25, bf16[1792,512]{1,0:T(8,128)(2,1)} %collective-permute-done.23), kind=kOutput, calls=%fused_computation.3 | convolution fusion | flops 235110400 | bytes 3801088 | tf_op jit(solution)/shard_map/dot_general | solution.py:105
  116.5 2.3 %convolution_add_fusion.3 = f32[128,1792]{1,0:T(8,128)S(1)} fusion(f32[128,1792]{1,0:T(8,128)S(1)} %fusion.49, bf16[128,512]{1,0:T(8,128)(2,1)} %collective-permute-done.22, bf16[1792,512]{1,0:T(8,128)(2,1)} %collective-permute-done.23), kind=kOutput, calls=%fused_computation.4 | convolution fusion | flops 235110400 | bytes 3801088 | tf_op jit(solution)/shard_map/dot_general | solution.py:105
  118.8 1.4 collective-permute-start.24
  120.4 6.8 %collective-permute-done.26 = bf16[64,1792]{1,0:T(8,128)(2,1)S(1)} collective-permute-done((bf16[64,1792]{1,0:T(8,128)(2,1)S(1)}, bf16[64,1792]{1,0:T(8,128)(2,1)S(1)}, u32[]{:S(2)}, u32[]{:S(2)}) %collective-permute-start.26) | collective-permute-done | bytes 229408 | tf_op jit(solution)/shard_map/ppermute | solution.py:44
  128.3 3.3 %collective-permute-done.24 = bf16[64,1792]{1,0:T(8,128)(2,1)S(1)} collective-permute-done((bf16[64,1792]{1,0:T(8,128)(2,1)S(1)}, bf16[64,1792]{1,0:T(8,128)(2,1)S(1)}, u32[]{:S(2)}, u32[]{:S(2)}) %collective-permute-start.24) | collective-permute-done | bytes 229408 | tf_op jit(solution)/shard_map/ppermute | solution.py:44
  131.7 7.3 %collective-permute-done.27 = bf16[64,1792]{1,0:T(8,128)(2,1)S(1)} collective-permute-done((bf16[64,1792]{1,0:T(8,128)(2,1)S(1)}, bf16[64,1792]{1,0:T(8,128)(2,1)S(1)}, u32[]{:S(2)}, u32[]{:S(2)}) %collective-permute-start.27) | collective-permute-done | bytes 229408 | tf_op jit(solution)/shard_map/ppermute | solution.py:44
  (132 shorter events, 27.5 us)
Async XLA Ops:
  0.6 13.7 %collective-permute-start = (bf16[64,1792]{1,0:T(8,128)(2,1)}, bf16[64,1792]{1,0:T(8,128)(2,1)S(1)}, u32[]{:S(2)}, u32[]{:S(2)}) collective-permute-start(bf16[64,1792]{1,0:T(8,128)(2,1)} %bitcast.37), channel_id=1, source_target_pairs={{0,2},{1,3},{2,0},{3,1},{4,6},{5,7},{6,4},{7,5},{8,10},{9,11},{10,... | collective-permute-start | bytes 688136 | tf_op jit(solution)/shard_map/ppermute | solution.py:44
  3.7 12.0 %collective-permute-start.2 = (bf16[64,1792]{1,0:T(8,128)(2,1)}, bf16[64,1792]{1,0:T(8,128)(2,1)S(1)}, u32[]{:S(2)}, u32[]{:S(2)}) collective-permute-start(bf16[64,1792]{1,0:T(8,128)(2,1)} %bitcast.38), channel_id=1, source_target_pairs={{0,12},{1,13},{2,14},{3,15},{4,8},{5,9},{6,10},{7,11},{8,4},{9,5},... | collective-permute-start | bytes 688136 | tf_op jit(solution)/shard_map/ppermute | solution.py:44
  7.3 12.4 %collective-permute-start.5 = (bf16[64,1792]{1,0:T(8,128)(2,1)}, bf16[64,1792]{1,0:T(8,128)(2,1)S(1)}, u32[]{:S(2)}, u32[]{:S(2)}) collective-permute-start(bf16[64,1792]{1,0:T(8,128)(2,1)} %bitcast.39), channel_id=1, source_target_pairs={{0,4},{1,5},{2,6},{3,7},{4,0},{5,1},{6,2},{7,3},{8,12},{9,13},{10,... | collective-permute-start | bytes 688136 | tf_op jit(solution)/shard_map/ppermute | solution.py:44
  7.3 8.5 %collective-permute-start.11 = (bf16[64,1792]{1,0:T(8,128)(2,1)}, bf16[64,1792]{1,0:T(8,128)(2,1)S(1)}, u32[]{:S(2)}, u32[]{:S(2)}) collective-permute-start(bf16[64,1792]{1,0:T(8,128)(2,1)} %param.6), channel_id=1, source_target_pairs={{0,2},{1,3},{2,0},{3,1},{4,6},{5,7},{6,4},{7,5},{8,10},{9,11},{10,... | collective-permute-start | bytes 688136 | tf_op jit(solution)/shard_map/ppermute | solution.py:44
  7.8 17.5 %collective-permute-start.13 = (bf16[64,1792]{1,0:T(8,128)(2,1)}, bf16[64,1792]{1,0:T(8,128)(2,1)S(1)}, u32[]{:S(2)}, u32[]{:S(2)}) collective-permute-start(bf16[64,1792]{1,0:T(8,128)(2,1)} %param.6), channel_id=1, source_target_pairs={{0,12},{1,13},{2,14},{3,15},{4,8},{5,9},{6,10},{7,11},{8,4},{9,5},... | collective-permute-start | bytes 688136 | tf_op jit(solution)/shard_map/ppermute | solution.py:44
  14.4 18.1 %collective-permute-start.16 = (bf16[64,1792]{1,0:T(8,128)(2,1)S(1)}, bf16[64,1792]{1,0:T(8,128)(2,1)S(1)}, u32[]{:S(2)}, u32[]{:S(2)}) collective-permute-start(bf16[64,1792]{1,0:T(8,128)(2,1)S(1)} %copy-done.3), channel_id=1, source_target_pairs={{0,4},{1,5},{2,6},{3,7},{4,0},{5,1},{6,2},{7,3},{8,12},{9,13},{10,... | collective-permute-start | bytes 688136 | tf_op jit(solution)/shard_map/ppermute | solution.py:44
  15.7 90.6 %collective-permute-start.23 = (bf16[1792,512]{1,0:T(8,128)(2,1)}, bf16[1792,512]{1,0:T(8,128)(2,1)}, u32[]{:S(2)}, u32[]{:S(2)}) collective-permute-start(bf16[1792,512]{1,0:T(8,128)(2,1)} %param.8), channel_id=1, source_target_pairs={{0,1},{1,0},{2,3},{3,2},{4,5},{5,4},{6,7},{7,6},{8,9},{9,8},{10,11... | collective-permute-start | bytes 5505032 | tf_op jit(solution)/shard_map/ppermute | solution.py:44
  15.8 8.0 %collective-permute-start.3 = (bf16[64,1792]{1,0:T(8,128)(2,1)S(1)}, bf16[64,1792]{1,0:T(8,128)(2,1)S(1)}, u32[]{:S(2)}, u32[]{:S(2)}) collective-permute-start(bf16[64,1792]{1,0:T(8,128)(2,1)S(1)} %collective-permute-done.2), channel_id=1, source_target_pairs={{0,2},{1,3},{2,0},{3,1},{4,6},{5,7},{6,4},{7,5},{8,10},{9,11},{10,... | collective-permute-start | bytes 688136 | tf_op jit(solution)/shard_map/ppermute | solution.py:44
  19.7 30.1 %collective-permute-start.1 = (bf16[128,1792]{1,0:T(8,128)(2,1)S(1)}, bf16[128,1792]{1,0:T(8,128)(2,1)S(1)}, u32[]{:S(2)}, u32[]{:S(2)}) collective-permute-start(bf16[128,1792]{1,0:T(8,128)(2,1)S(1)} %pad_maximum_fusion), channel_id=1, source_target_pairs={{0,1},{1,0},{2,3},{3,2},{4,5},{5,4},{6,7},{7,6},{8,9},{9,8},{10,11... | collective-permute-start | bytes 1376264 | tf_op jit(solution)/shard_map/ppermute | solution.py:44
  23.8 7.2 %collective-permute-start.6 = (bf16[64,1792]{1,0:T(8,128)(2,1)S(1)}, bf16[64,1792]{1,0:T(8,128)(2,1)S(1)}, u32[]{:S(2)}, u32[]{:S(2)}) collective-permute-start(bf16[64,1792]{1,0:T(8,128)(2,1)S(1)} %collective-permute-done.5), channel_id=1, source_target_pairs={{0,2},{1,3},{2,0},{3,1},{4,6},{5,7},{6,4},{7,5},{8,10},{9,11},{10,... | collective-permute-start | bytes 688136 | tf_op jit(solution)/shard_map/ppermute | solution.py:44
  25.3 33.2 %collective-permute-start.12 = (bf16[128,1792]{1,0:T(8,128)(2,1)S(1)}, bf16[128,1792]{1,0:T(8,128)(2,1)S(1)}, u32[]{:S(2)}, u32[]{:S(2)}) collective-permute-start(bf16[128,1792]{1,0:T(8,128)(2,1)S(1)} %pad_maximum_fusion.4), channel_id=1, source_target_pairs={{0,1},{1,0},{2,3},{3,2},{4,5},{5,4},{6,7},{7,6},{8,9},{9,8},{10,11... | collective-permute-start | bytes 1376264 | tf_op jit(solution)/shard_map/ppermute | solution.py:44
  32.5 17.3 %collective-permute-start.8 = (bf16[64,1792]{1,0:T(8,128)(2,1)S(1)}, bf16[64,1792]{1,0:T(8,128)(2,1)S(1)}, u32[]{:S(2)}, u32[]{:S(2)}) collective-permute-start(bf16[64,1792]{1,0:T(8,128)(2,1)S(1)} %collective-permute-done.2), channel_id=1, source_target_pairs={{0,4},{1,5},{2,6},{3,7},{4,0},{5,1},{6,2},{7,3},{8,12},{9,13},{10,... | collective-permute-start | bytes 688136 | tf_op jit(solution)/shard_map/ppermute | solution.py:44
  44.0 14.0 %collective-permute-start.19 = (bf16[64,1792]{1,0:T(8,128)(2,1)S(1)}, bf16[64,1792]{1,0:T(8,128)(2,1)S(1)}, u32[]{:S(2)}, u32[]{:S(2)}) collective-permute-start(bf16[64,1792]{1,0:T(8,128)(2,1)S(1)} %collective-permute-done.13), channel_id=1, source_target_pairs={{0,4},{1,5},{2,6},{3,7},{4,0},{5,1},{6,2},{7,3},{8,12},{9,13},{10,... | collective-permute-start | bytes 688136 | tf_op jit(solution)/shard_map/ppermute | solution.py:44
  49.7 18.7 %collective-permute-start.4 = (bf16[128,1792]{1,0:T(8,128)(2,1)S(1)}, bf16[128,1792]{1,0:T(8,128)(2,1)S(1)}, u32[]{:S(2)}, u32[]{:S(2)}) collective-permute-start(bf16[128,1792]{1,0:T(8,128)(2,1)S(1)} %pad_maximum_fusion.1), channel_id=1, source_target_pairs={{0,1},{1,0},{2,3},{3,2},{4,5},{5,4},{6,7},{7,6},{8,9},{9,8},{10,11... | collective-permute-start | bytes 1376264 | tf_op jit(solution)/shard_map/ppermute | solution.py:44
  49.8 8.0 %collective-permute-start.9 = (bf16[64,1792]{1,0:T(8,128)(2,1)S(1)}, bf16[64,1792]{1,0:T(8,128)(2,1)S(1)}, u32[]{:S(2)}, u32[]{:S(2)}) collective-permute-start(bf16[64,1792]{1,0:T(8,128)(2,1)S(1)} %collective-permute-done.8), channel_id=1, source_target_pairs={{0,2},{1,3},{2,0},{3,1},{4,6},{5,7},{6,4},{7,5},{8,10},{9,11},{10,... | collective-permute-start | bytes 688136 | tf_op jit(solution)/shard_map/ppermute | solution.py:44
  57.8 14.5 %collective-permute-start.7 = (bf16[128,1792]{1,0:T(8,128)(2,1)S(1)}, bf16[128,1792]{1,0:T(8,128)(2,1)S(1)}, u32[]{:S(2)}, u32[]{:S(2)}) collective-permute-start(bf16[128,1792]{1,0:T(8,128)(2,1)S(1)} %pad_maximum_fusion.2), channel_id=1, source_target_pairs={{0,1},{1,0},{2,3},{3,2},{4,5},{5,4},{6,7},{7,6},{8,9},{9,8},{10,11... | collective-permute-start | bytes 1376264 | tf_op jit(solution)/shard_map/ppermute | solution.py:44
  58.0 18.6 %collective-permute-start.15 = (bf16[128,1792]{1,0:T(8,128)(2,1)S(1)}, bf16[128,1792]{1,0:T(8,128)(2,1)S(1)}, u32[]{:S(2)}, u32[]{:S(2)}) collective-permute-start(bf16[128,1792]{1,0:T(8,128)(2,1)S(1)} %pad_maximum_fusion.5), channel_id=1, source_target_pairs={{0,1},{1,0},{2,3},{3,2},{4,5},{5,4},{6,7},{7,6},{8,9},{9,8},{10,11... | collective-permute-start | bytes 1376264 | tf_op jit(solution)/shard_map/ppermute | solution.py:44
  58.6 7.6 %collective-permute-start.20 = (bf16[64,1792]{1,0:T(8,128)(2,1)S(1)}, bf16[64,1792]{1,0:T(8,128)(2,1)S(1)}, u32[]{:S(2)}, u32[]{:S(2)}) collective-permute-start(bf16[64,1792]{1,0:T(8,128)(2,1)S(1)} %collective-permute-done.19), channel_id=1, source_target_pairs={{0,2},{1,3},{2,0},{3,1},{4,6},{5,7},{6,4},{7,5},{8,10},{9,11},{10,... | collective-permute-start | bytes 688136 | tf_op jit(solution)/shard_map/ppermute | solution.py:44
  66.2 14.3 %collective-permute-start.18 = (bf16[128,1792]{1,0:T(8,128)(2,1)S(1)}, bf16[128,1792]{1,0:T(8,128)(2,1)S(1)}, u32[]{:S(2)}, u32[]{:S(2)}) collective-permute-start(bf16[128,1792]{1,0:T(8,128)(2,1)S(1)} %pad_maximum_fusion.6), channel_id=1, source_target_pairs={{0,1},{1,0},{2,3},{3,2},{4,5},{5,4},{6,7},{7,6},{8,9},{9,8},{10,11... | collective-permute-start | bytes 1376264 | tf_op jit(solution)/shard_map/ppermute | solution.py:44
  68.5 15.2 %collective-permute-start.10 = (bf16[128,1792]{1,0:T(8,128)(2,1)S(1)}, bf16[128,1792]{1,0:T(8,128)(2,1)S(1)}, u32[]{:S(2)}, u32[]{:S(2)}) collective-permute-start(bf16[128,1792]{1,0:T(8,128)(2,1)S(1)} %pad_maximum_fusion.3), channel_id=1, source_target_pairs={{0,1},{1,0},{2,3},{3,2},{4,5},{5,4},{6,7},{7,6},{8,9},{9,8},{10,11... | collective-permute-start | bytes 1376264 | tf_op jit(solution)/shard_map/ppermute | solution.py:44
  72.4 18.4 %collective-permute-start.21 = (bf16[128,1792]{1,0:T(8,128)(2,1)S(1)}, bf16[128,1792]{1,0:T(8,128)(2,1)S(1)}, u32[]{:S(2)}, u32[]{:S(2)}) collective-permute-start(bf16[128,1792]{1,0:T(8,128)(2,1)S(1)} %pad_maximum_fusion.7), channel_id=1, source_target_pairs={{0,1},{1,0},{2,3},{3,2},{4,5},{5,4},{6,7},{7,6},{8,9},{9,8},{10,11... | collective-permute-start | bytes 1376264 | tf_op jit(solution)/shard_map/ppermute | solution.py:44
  76.6 39.9 %collective-permute-start.22 = (bf16[128,512]{1,0:T(8,128)(2,1)S(1)}, bf16[128,512]{1,0:T(8,128)(2,1)}, u32[]{:S(2)}, u32[]{:S(2)}) collective-permute-start(bf16[128,512]{1,0:T(8,128)(2,1)S(1)} %slice.149), channel_id=1, source_target_pairs={{0,1},{1,0},{2,3},{3,2},{4,5},{5,4},{6,7},{7,6},{8,9},{9,8},{10,11... | collective-permute-start | bytes 393224 | tf_op jit(solution)/shard_map/ppermute | solution.py:44
  80.4 29.2 %collective-permute-start.28 = (bf16[128,512]{1,0:T(8,128)(2,1)}, bf16[128,512]{1,0:T(8,128)(2,1)}, u32[]{:S(2)}, u32[]{:S(2)}) collective-permute-start(bf16[128,512]{1,0:T(8,128)(2,1)} %slice.157), channel_id=1, source_target_pairs={{0,1},{1,0},{2,3},{3,2},{4,5},{5,4},{6,7},{7,6},{8,9},{9,8},{10,11... | collective-permute-start | bytes 393224 | tf_op jit(solution)/shard_map/ppermute | solution.py:44
  83.7 29.7 %collective-permute-start.25 = (bf16[128,512]{1,0:T(8,128)(2,1)S(1)}, bf16[128,512]{1,0:T(8,128)(2,1)}, u32[]{:S(2)}, u32[]{:S(2)}) collective-permute-start(bf16[128,512]{1,0:T(8,128)(2,1)S(1)} %slice.153), channel_id=1, source_target_pairs={{0,1},{1,0},{2,3},{3,2},{4,5},{5,4},{6,7},{7,6},{8,9},{9,8},{10,11... | collective-permute-start | bytes 393224 | tf_op jit(solution)/shard_map/ppermute | solution.py:44
  90.8 15.5 %collective-permute-start.30 = (bf16[128,512]{1,0:T(8,128)(2,1)}, bf16[128,512]{1,0:T(8,128)(2,1)}, u32[]{:S(2)}, u32[]{:S(2)}) collective-permute-start(bf16[128,512]{1,0:T(8,128)(2,1)} %slice.161), channel_id=1, source_target_pairs={{0,1},{1,0},{2,3},{3,2},{4,5},{5,4},{6,7},{7,6},{8,9},{9,8},{10,11... | collective-permute-start | bytes 393224 | tf_op jit(solution)/shard_map/ppermute | solution.py:44
  108.9 11.4 %collective-permute-start.31 = (bf16[64,1792]{1,0:T(8,128)(2,1)S(1)}, bf16[64,1792]{1,0:T(8,128)(2,1)S(1)}, u32[]{:S(2)}, u32[]{:S(2)}) collective-permute-start(bf16[64,1792]{1,0:T(8,128)(2,1)S(1)} %slice.208), channel_id=1, source_target_pairs={{0,2},{1,3},{2,0},{3,1},{4,6},{5,7},{6,4},{7,5},{8,10},{9,11},{10,... | collective-permute-start | bytes 688136 | tf_op jit(solution)/shard_map/ppermute | solution.py:44
  112.0 15.3 %collective-permute-start.29 = (bf16[64,1792]{1,0:T(8,128)(2,1)S(1)}, bf16[64,1792]{1,0:T(8,128)(2,1)S(1)}, u32[]{:S(2)}, u32[]{:S(2)}) collective-permute-start(bf16[64,1792]{1,0:T(8,128)(2,1)S(1)} %slice.209), channel_id=1, source_target_pairs={{0,2},{1,3},{2,0},{3,1},{4,6},{5,7},{6,4},{7,5},{8,10},{9,11},{10,... | collective-permute-start | bytes 688136 | tf_op jit(solution)/shard_map/ppermute | solution.py:44
  115.7 11.4 %collective-permute-start.26 = (bf16[64,1792]{1,0:T(8,128)(2,1)S(1)}, bf16[64,1792]{1,0:T(8,128)(2,1)S(1)}, u32[]{:S(2)}, u32[]{:S(2)}) collective-permute-start(bf16[64,1792]{1,0:T(8,128)(2,1)S(1)} %slice.210), channel_id=1, source_target_pairs={{0,2},{1,3},{2,0},{3,1},{4,6},{5,7},{6,4},{7,5},{8,10},{9,11},{10,... | collective-permute-start | bytes 688136 | tf_op jit(solution)/shard_map/ppermute | solution.py:44
  118.8 12.8 %collective-permute-start.24 = (bf16[64,1792]{1,0:T(8,128)(2,1)S(1)}, bf16[64,1792]{1,0:T(8,128)(2,1)S(1)}, u32[]{:S(2)}, u32[]{:S(2)}) collective-permute-start(bf16[64,1792]{1,0:T(8,128)(2,1)S(1)} %slice.211), channel_id=1, source_target_pairs={{0,2},{1,3},{2,0},{3,1},{4,6},{5,7},{6,4},{7,5},{8,10},{9,11},{10,... | collective-permute-start | bytes 688136 | tf_op jit(solution)/shard_map/ppermute | solution.py:44
  120.3 7.0 %collective-permute-start.32 = (bf16[64,1792]{1,0:T(8,128)(2,1)S(1)}, bf16[64,1792]{1,0:T(8,128)(2,1)S(1)}, u32[]{:S(2)}, u32[]{:S(2)}) collective-permute-start(bf16[64,1792]{1,0:T(8,128)(2,1)S(1)} %fusion.37), channel_id=1, source_target_pairs={{0,4},{1,5},{2,6},{3,7},{4,0},{5,1},{6,2},{7,3},{8,12},{9,13},{10,... | collective-permute-start | bytes 688136 | tf_op jit(solution)/shard_map/ppermute | solution.py:44
  127.2 11.8 %collective-permute-start.27 = (bf16[64,1792]{1,0:T(8,128)(2,1)S(1)}, bf16[64,1792]{1,0:T(8,128)(2,1)S(1)}, u32[]{:S(2)}, u32[]{:S(2)}) collective-permute-start(bf16[64,1792]{1,0:T(8,128)(2,1)S(1)} %fusion.40), channel_id=1, source_target_pairs={{0,4},{1,5},{2,6},{3,7},{4,0},{5,1},{6,2},{7,3},{8,12},{9,13},{10,... | collective-permute-start | bytes 688136 | tf_op jit(solution)/shard_map/ppermute | solution.py:44
  127.4 11.6 %collective-permute-start.33 = (bf16[64,1792]{1,0:T(8,128)(2,1)S(1)}, bf16[64,1792]{1,0:T(8,128)(2,1)S(1)}, u32[]{:S(2)}, u32[]{:S(2)}) collective-permute-start(bf16[64,1792]{1,0:T(8,128)(2,1)S(1)} %fusion.39), channel_id=1, source_target_pairs={{0,12},{1,13},{2,14},{3,15},{4,8},{5,9},{6,10},{7,11},{8,4},{9,5},... | collective-permute-start | bytes 688136 | tf_op jit(solution)/shard_map/ppermute | solution.py:44
  (11 other events, 96.8 us)

commit v2 on v1

v2 whole, which is shorter than its diff:
```python
import jax
import jax.numpy as jnp
from jax import lax
from jax.experimental import pallas as pl
from jax.experimental.pallas import tpu as pltpu
from jax.sharding import PartitionSpec as P

BF = jnp.bfloat16
F32 = jnp.float32


def general(sources, errors, enc_weight, enc_bias, dec_weight, active):
    mine = lax.axis_index("tsec")
    rows_all = lax.all_gather(sources, "lat", axis=0, tiled=True)
    flags = active.astype(F32)
    share = rows_all.shape[0] // lax.axis_size("tsec")
    partial_value = jnp.dot(rows_all, enc_weight, preferred_element_type=F32)
    pre = lax.psum(partial_value, "tsec") + enc_bias
    codes = (pre * flags).astype(BF)
    targets = lax.all_gather(errors, "lat", axis=1, tiled=True)
    dec_grad = jnp.einsum("rl,trd->tld", codes, targets, preferred_element_type=F32)
    partial_code = jnp.einsum("trd,tld->rl", targets, dec_weight, preferred_element_type=F32)
    total = lax.psum(partial_code, "tsec")
    pre_grad = (total * flags).astype(BF)
    code_grad = lax.dynamic_slice_in_dim(total, mine * share, share, 0)
    enc_grad = jnp.einsum("rd,rl->dl", rows_all, pre_grad, preferred_element_type=F32)
    input_grad = lax.psum_scatter(
        jnp.einsum("rl,dl->rd", pre_grad, enc_weight, preferred_element_type=F32),
        "lat",
        scatter_dimension=0,
        tiled=True,
    )
    return (code_grad, dec_grad, enc_grad, input_grad)


NZ, NY, NC = 4, 2, 2


def swap(x, partner):
    pairs = []
    for z in range(NZ):
        for y in range(NY):
            for c in range(NC):
                pz, py, pc = partner(z, y, c)
                pairs.append(((z * NY + y) * NC + c, (pz * NY + py) * NC + pc))
    return lax.ppermute(x, "lat", pairs)


def over_core(x):
    return swap(x, lambda z, y, c: (z, y, 1 - c))


def over_y(x):
    return swap(x, lambda z, y, c: (z, 1 - y, c))


def over_mirror(x):
    return swap(x, lambda z, y, c: (NZ - 1 - z, y, c))


def over_pair(x):
    return swap(x, lambda z, y, c: (z ^ 1, y, c))


VMEM = pl.BlockSpec(memory_space=pltpu.VMEM)
ANY = pl.BlockSpec(memory_space=pl.ANY)
PARAMS = pltpu.CompilerParams(vmem_limit_bytes=40 * 2**20)
NT = (((1,), (1,)), ((), ()))
NN = (((1,), (0,)), ((), ()))
TN = (((0,), (0,)), ((), ()))


def dot(a, b, dims):
    return lax.dot_general(a, b, dims, preferred_element_type=F32)


def like(shape, kind):
    return jax.ShapeDtypeStruct(shape, kind)


def call(kernel, outs, flops, *args, **options):
    moved = sum(a.size * a.dtype.itemsize for a in args)
    return pl.pallas_call(
        kernel,
        out_shape=outs,
        in_specs=options.pop("in_specs", [VMEM] * len(args)),
        out_specs=options.pop("out_specs", [VMEM] * len(outs)),
        compiler_params=PARAMS,
        cost_estimate=pl.CostEstimate(flops=1, bytes_accessed=1, transcendentals=0),
        **options,
    )(*args)


def flags_kernel(rows, place, active, flags, stage, sems):
    copies = [
        pltpu.make_async_copy(
            active.at[pl.ds(pl.multiple_of(place[n], rows), rows)],
            stage.at[pl.ds(n * rows, rows)],
            sems.at[n],
        )
        for n in range(NZ * NY * NC)
    ]
    for copy in copies:
        copy.start()
    for n, copy in enumerate(copies):
        copy.wait()
        span = pl.ds(n * rows, rows)
        flags[span] = stage[span].astype(F32)


def make_flags(place, active, rows):
    n = NZ * NY * NC
    return call(
        lambda *refs: flags_kernel(rows, *refs),
        [like(active.shape, F32)],
        active.size,
        place,
        active,
        in_specs=[pl.BlockSpec(memory_space=pltpu.SMEM), ANY],
        scratch_shapes=[pltpu.VMEM(active.shape, active.dtype), pltpu.SemaphoreType.DMA((n,))],
    )[0]


def place_kernel(rows, place, *refs):
    totals, out, sems = refs[:NZ], refs[NZ], refs[NZ + 1]
    copies = []
    for n in range(NZ * NY * NC):
        j, k = divmod(n, NY * NC)
        copies.append(
            pltpu.make_async_copy(
                totals[j].at[pl.ds(k * rows, rows)],
                out.at[pl.ds(pl.multiple_of(place[n], rows), rows)],
                sems.at[n],
            )
        )
    for copy in copies:
        copy.start()
    for copy in copies:
        copy.wait()


def place_rows(place, totals, rows):
    n = NZ * NY * NC
    return call(
        lambda *refs: place_kernel(rows, *refs),
        [like((n * rows, totals[0].shape[1]), F32)],
        0,
        place,
        *totals,
        in_specs=[pl.BlockSpec(memory_space=pltpu.SMEM)] + [VMEM] * NZ,
        out_specs=[ANY],
        scratch_shapes=[pltpu.SemaphoreType.DMA((n,))],
    )[0]


def code_kernel(j, half, *refs):
    *others, weight, flags, errs, total, grad = refs
    n = half.shape[0]
    errs[:n] = half[...]
    row = n
    for other in others:
        errs[row : row + other.shape[0]] = other[...]
        row += other.shape[0]
    value = dot(errs[...], weight[...], NT)
    total[...] = value
    grad[...] = (value * flags[pl.ds(j * 2 * n, 2 * n)]).astype(BF)


def code_step(j, half, others, weight, flags):
    n, d = half.shape
    lat = weight.shape[0]
    return call(
        lambda *refs: code_kernel(j, *refs),
        [like((2 * n, d), BF), like((2 * n, lat), F32), like((2 * n, lat), BF)],
        4 * n * d * lat,
        half,
        *others,
        weight,
        flags,
    )


def term_kernel(grad, peer, weight, weight_peer, keep, send):
    n = peer.shape[0]
    term = dot(grad[:n], weight[...], NT) + dot(peer[...], weight_peer[...], NT)
    keep[...] = term[: n // 2]
    send[...] = term[n // 2 :].astype(BF)


def term_step(grad, peer, weight, weight_peer):
    n, lat = peer.shape
    d = weight.shape[0]
    return call(
        term_kernel,
        [like((n // 2, d), F32), like((n // 2, d), BF)],
        4 * n * d * lat,
        grad,
        peer,
        weight,
        weight_peer,
    )


def pre_kernel(j, half, *refs):
    *others, weight, bias, flags, srcs, codes = refs
    n = half.shape[0]
    srcs[:n] = half[...]
    row = n
    for other in others:
        srcs[row : row + other.shape[0]] = other[...]
        row += other.shape[0]
    value = dot(srcs[...], weight[...], NN) + bias[...]
    codes[...] = (value * flags[pl.ds(j * 2 * n, 2 * n)]).astype(BF)


def pre_step(j, half, others, weight, bias, flags):
    n, d = half.shape
    lat = weight.shape[1]
    return call(
        lambda *refs: pre_kernel(j, *refs),
        [like((2 * n, d), BF), like((2 * n, lat), BF)],
        4 * n * d * lat,
        half,
        *others,
        weight,
        bias,
        flags,
    )


def tokens_kernel(*refs):
    codes, errs, srcs, grads = (refs[NZ * k : NZ * k + NZ] for k in range(4))
    dec_grad, enc_grad, token, turned = refs[4 * NZ + 1 :]
    token[...] = jnp.zeros_like(token)
    n, tile = codes[0].shape[0], enc_grad.shape[0]

    @pl.when(pl.program_id(0) == 0)
    def _():
        for j in range(NZ):
            turned[:, j * n : (j + 1) * n] = codes[j][...].T

    cols = pl.ds(pl.multiple_of(pl.program_id(0) * tile, tile), tile)
    dec_grad[...] = sum(
        dot(turned[:, j * n : (j + 1) * n], errs[j][:, cols], NN) for j in range(NZ)
    )
    enc_grad[...] = sum(dot(srcs[j][:, cols], grads[j][...], TN) for j in range(NZ))


def tokens_step(codes, errs, srcs, grads, last, tile=256):
    n, lat = codes[0].shape
    d = errs[0].shape[1]
    return call(
        tokens_kernel,
        [like((lat, d), F32), like((d, lat), F32), like((8, 128), F32)],
        4 * NZ * n * d * lat,
        *codes,
        *errs,
        *srcs,
        *grads,
        last,
        grid=(d // tile,),
        out_specs=[
            pl.BlockSpec((lat, tile), lambda t: (0, t)),
            pl.BlockSpec((tile, lat), lambda t: (t, 0)),
            VMEM,
        ],
        scratch_shapes=[pltpu.VMEM((lat, NZ * n), BF)],
    )


def after_kernel(x, *refs):
    refs[-1][...] = x[...]


def after(x, *others):
    return call(after_kernel, [like(x.shape, x.dtype)], 0, x, *others)[0]


def finish_kernel(keep, back, pair, top, bottom, token, out):
    n = top.shape[0]
    own = keep[...] + back[...].astype(F32) + pair[...].astype(F32)
    out[:n] = own[:n] + top[...].astype(F32)
    out[n:] = own[n:] + bottom[...].astype(F32)


def pack_kernel(count, *refs):
    row = 0
    for part in refs[:count]:
        n = part.shape[0]
        refs[-1][row : row + n] = part[...]
        row += n


def pack(parts, *others):
    n = sum(part.shape[0] for part in parts)
    out = like((n, parts[0].shape[1]), parts[0].dtype)
    return call(lambda *refs: pack_kernel(len(parts), *refs), [out], 0, *parts, *others)[0]


def pieces(send, x, count=2):
    n = x.shape[0] // count
    return [send(x[k * n : (k + 1) * n]) for k in range(count)]


def grid(sources, errors, enc_weight, enc_bias, dec_weight, active):
    rows = sources.shape[0]
    i = lax.axis_index("lat")
    z, y, c = i // (NY * NC), (i // NC) % NY, i % NC
    zs = (z, NZ - 1 - z, z ^ 1, NZ - 1 - (z ^ 1))
    parts = ((y, c), (1 - y, c), (y, 1 - c), (1 - y, 1 - c))
    place = jnp.stack([((zz * NY + yy) * NC + cc) * rows for zz in zs for yy, cc in parts])
    bias = enc_bias[None]
    flags = make_flags(place, active, rows)

    def code(j, half, others):
        return code_step(j, half, others, dec_weight[0], flags)

    def across(grad):
        return over_core(grad[2 * rows :])

    def term(grad, peer):
        return term_step(grad, peer, enc_weight, weight_peer)

    def plus(keep, *backs):
        n = keep.shape[0] // len(backs[0])
        return [
            keep[k * n : (k + 1) * n] + sum(back[k].astype(F32) for back in backs)
            for k in range(len(backs[0]))
        ]

    def pre(j, half, others):
        return pre_step(j, half, others, enc_weight, bias, flags)

    x, s = errors[0], sources
    y0, m, p = over_y(x), over_mirror(x), over_pair(x)
    s_y0, s_m = over_y(s), over_mirror(s)
    weight_peer = over_core(enc_weight)
    m = after(m, y0, p, flags, weight_peer)
    y1, q = pieces(over_y, m), pieces(over_pair, m)
    half0 = pack([x, y0], m, s_y0)
    other0 = pieces(over_core, half0)
    s_x = pack([s, s_y0], half0)
    s_other0 = pieces(over_core, s_x)
    errs0, total0, grad0 = code(0, half0, other0)
    q1 = [over_pair(after(part, grad0)) for part in y1]
    p = after(p, y1[0], grad0)
    y2 = pieces(over_y, p)
    half1 = pack([m, *y1], grad0, *q)
    other1, peer0 = pieces(over_core, half1, 4), across(after(grad0, half1))
    errs1, total1, grad1 = code(1, half1, other1)
    keep0, send0 = term(grad0, peer0)
    srcs0, codes0 = pre(0, s_x, [after(s_other0[0], grad1), s_other0[1]])
    half3 = pack([*q, *q1], send0, codes0, s_m)
    half2 = pack([p, *y2], half3)
    other3, other2 = pieces(over_core, half3), pieces(over_core, half2)
    back0, peer1 = over_y(after(send0, half3)), across(after(grad1, half3))
    s_m = after(s_m, half3)
    s_y1, s_q = over_y(s_m), over_pair(s_m)
    s_p = over_pair(after(s_x, half3))
    errs3, total3, grad3 = code(3, half3, other3)
    peer3 = across(grad3)
    errs2, total2, grad2 = code(2, after(half2, grad3), other2)
    peer2 = across(grad2)
    keep3, send3 = term(grad3, after(peer3, grad2))
    back3 = pieces(over_y, send3)
    keep1, send1 = term(after(grad1, send3), peer1)
    back1 = pieces(over_y, send1)
    keep2, send2 = term(after(grad2, send1, back0), peer2)
    back2 = over_y(send2)
    s_q = after(s_q, send2)
    s_y3 = over_y(s_q)
    s_m = pack([s_m, s_y1], send2)
    s_other1 = pieces(over_core, s_m)
    sum3 = [after(part.astype(BF), send2) for part in plus(keep3, back3)]
    pair3 = [over_pair(part) for part in sum3]
    s_p = after(s_p, *sum3)
    s_other2 = pieces(over_core, s_p)
    srcs1, codes1 = pre(1, s_m, [after(s_other1[0], *sum3), s_other1[1]])
    srcs2, codes2 = pre(2, s_p, s_other2)
    far = [part.astype(BF) for part in plus(keep1, back1, pair3)]
    far = [after(part, codes1, codes2) for part in far]
    far_in = [over_mirror(part) for part in far]
    sum2 = (keep2 + back2.astype(F32)).astype(BF)
    pair2 = over_pair(sum2)
    s_q = pack([s_q, s_y3], *far)
    srcs3, codes3 = pre(3, s_q, pieces(over_core, s_q))
    code_grad = place_rows(
        place, (total0, total1, total2, after(total3, *far)), rows
    )
    dec_grad, enc_grad, token = tokens_step(
        (codes0, codes1, codes2, codes3),
        (errs0, errs1, errs2, errs3),
        (srcs0, srcs1, srcs2, srcs3),
        (grad0, grad1, grad2, grad3),
        far[1],
    )
    input_grad = call(
        finish_kernel, [like(x.shape, F32)], 0, keep0, back0, pair2, *far_in, token
    )[0]
    return code_grad, dec_grad[None], enc_grad, input_grad


def solution(mesh):
    on_grid = mesh.shape["lat"] == NZ * NY * NC and mesh.shape["tsec"] == 1
    return jax.shard_map(
        grid if on_grid else general,
        mesh=mesh,
        in_specs=(
            P(("grp", "lat"), "tsec"),
            P("tsec", ("grp", "lat"), None),
            P("tsec", "lat"),
            P("lat"),
            P("tsec", "lat", None),
            P("grp", "lat"),
        ),
        out_specs=(
            P(("grp", "tsec"), "lat"),
            P("tsec", ("grp", "lat"), None),
            P(("grp", "tsec"), "lat"),
            P(("grp", "lat"), "tsec"),
        ),
        check_vma=False,
    )
```

time: 140 us -> 98.4 us (0.70)
  matrix products: 39.2 us -> 0 us
  Pallas kernels: 0 us -> 24.6 us
  local copies, waits for them, and re-layouts: 17.7 us -> 2.26 us
  waiting for transfers between devices: 43 us -> 30.8 us
  starting transfers between devices: 35.3 us -> 39.2 us
  other arithmetic: 3.48 us -> 0.16 us
    dot_general x14 -> x0, matrix products: 39.2 us -> none  [the longest x4 12.4 us: grid(): lax.dot_general(grad[:2 * rows], enc_weight, nt, preferred_element_type=F32)]
    pallas_call x0 -> x45, Pallas kernels: none -> 24.6 us  [call(): pl.pallas_call(kernel, out_shape=outs, in_specs=options.pop('in_specs', [...]
    ppermute x34 -> x51, waiting for transfers between devices: 43 us -> 30.8 us  [swap(): return lax.ppermute(x, 'lat', pairs)]
    dynamic_update_slice x16 -> x0, local copies, waits for them, and re-layouts: 10.7 us -> none  [grid(): lax.dynamic_update_slice_in_dim(code_grad, total[n * rows:(n + 1) * rows]...]
    ppermute x34 -> x51, starting transfers between devices: 35.3 us -> 39.2 us  [swap(): return lax.ppermute(x, 'lat', pairs)]
    convert_element_type x5 -> x3, other arithmetic: 2.36 us -> 0.16 us  [the longest x1 0.08 us: grid(): far = [part.astype(BF) for part in plus(keep1, back1, pair3)]]
    dynamic_slice x1 -> x0, local copies, waits for them, and re-layouts: 1.77 us -> none  [grid(): lax.dynamic_slice_in_dim(active, r, rows, 0)]
    broadcast_in_dim x1 -> x0, local copies, waits for them, and re-layouts: 1.58 us -> none  [grid(): code_grad = jnp.zeros(active.shape, F32)]
  transfers between devices with their start and end apart: 34 -> 51, of which waited for: 9 -> 14; matrix products, arithmetic and copies ran while one was open for 43% -> 1% of each run, Pallas kernels for 0% -> 24%
where the time goes in v2:
time: 98.4 us; the launch traced here: 98.3 us
  starting transfers between devices  39.2 us (40%)
  waiting for transfers between devices  30.8 us (31%)
  Pallas kernels  24.6 us (25%)
  local copies, waits for them, and re-layouts  2.26 us (2%)
  between operations  1.35 us (1%)
    ppermute x51, starting transfers between devices, swap(): return lax.ppermute(x, 'lat', pairs)  39.2 us
    ppermute x51, waiting for transfers between devices, swap(): return lax.ppermute(x, 'lat', pairs)  30.8 us
    pallas_call x45, Pallas kernels, call(): pl.pallas_call(kernel, out_shape=outs, in_specs=options.pop('in_specs', [...  24.6 us
  transfers between devices with their start and end apart: 51, of which 14 were waited for; matrix products, arithmetic and copies ran while one was open for 1% of the time, Pallas kernels for 24%

profile of v2, /device:TPU:0, one launch (start us, length us, event | category | flops | bytes accessed | tf_op | source)
XLA Modules:
  0.0 98.3 jit_solution(10334537916464211850)
XLA Ops:
  1.1 2.6 %collective-permute-start = (bf16[64,1792]{1,0:T(8,128)(2,1)}, bf16[64,1792]{1,0:T(8,128)(2,1)S(1)}, u32[]{:S(2)}, u32[]{:S(2)}) collective-permute-start(bf16[64,1792]{1,0:T(8,128)(2,1)} %bitcast.24), channel_id=1, source_target_pairs={{0,2},{1,3},{2,0},{3,1},{4,6},{5,7},{6,4},{7,5},{8,10},{9,11},{10,... | collective-permute-start | bytes 688136 | tf_op jit(solution)/shard_map/ppermute | solution.py:46
  3.7 1.6 %collective-permute-start.2 = (bf16[64,1792]{1,0:T(8,128)(2,1)}, bf16[64,1792]{1,0:T(8,128)(2,1)S(1)}, u32[]{:S(2)}, u32[]{:S(2)}) collective-permute-start(bf16[64,1792]{1,0:T(8,128)(2,1)} %bitcast.25), channel_id=1, source_target_pairs={{0,4},{1,5},{2,6},{3,7},{4,0},{5,1},{6,2},{7,3},{8,12},{9,13},{10,... | collective-permute-start | bytes 688136 | tf_op jit(solution)/shard_map/ppermute | solution.py:46
  5.3 2.5 %collective-permute-start.1 = (bf16[64,1792]{1,0:T(8,128)(2,1)}, bf16[64,1792]{1,0:T(8,128)(2,1)S(1)}, u32[]{:S(2)}, u32[]{:S(2)}) collective-permute-start(bf16[64,1792]{1,0:T(8,128)(2,1)} %bitcast.26), channel_id=1, source_target_pairs={{0,12},{1,13},{2,14},{3,15},{4,8},{5,9},{6,10},{7,11},{8,4},{9,5},... | collective-permute-start | bytes 688136 | tf_op jit(solution)/shard_map/ppermute | solution.py:46
  8.4 1.6 %copy-done.2 = s32[1024,512]{1,0:T(8,128)S(1)} copy-done((s32[1024,512]{1,0:T(8,128)S(1)}, s32[1024,512]{1,0:T(8,128)}, u32[]{:S(2)}) %copy-start.2) | copy-done | bytes 2097176
  10.0 3.6 %shard_map.93.refs_2_.refs_4_.refs_6_.refs_5_ = f32[1024,512]{1,0:T(8,128)S(1)} custom-call(s32[16]{0:T(128)S(1)} %stack.67.refs_0_, s32[1024,512]{1,0:T(8,128)S(1)} %copy-done.2), custom_call_target="tpu_custom_call" | custom-call | flops 1 | bytes 1 | tf_op jit(solution)/shard_map/pallas_call | solution.py:83
  13.6 5.1 %collective-permute-done.1.x = bf16[64,1792]{1,0:T(8,128)(2,1)S(1)} collective-permute-done((bf16[64,1792]{1,0:T(8,128)(2,1)}, bf16[64,1792]{1,0:T(8,128)(2,1)S(1)}, u32[]{:S(2)}, u32[]{:S(2)}) %collective-permute-start.1) | collective-permute-done | bytes 229408 | tf_op jit(solution)/shard_map/ppermute | solution.py:46
  20.1 1.5 %collective-permute-start.7 = (bf16[32,1792]{1,0:T(8,128)(2,1)S(1)}, bf16[32,1792]{1,0:T(8,128)(2,1)S(1)}, u32[]{:S(2)}, u32[]{:S(2)}) collective-permute-start(bf16[32,1792]{1,0:T(8,128)(2,1)S(1)} %get-tuple-element.95), channel_id=1, source_target_pairs={{0,2},{1,3},{2,0},{3,1},{4,6},{5,7},{6,4},{7,5},{8,10},{9,11},{10,... | collective-permute-start | bytes 344072 | tf_op jit(solution)/shard_map/ppermute | solution.py:46
  21.6 1.4 %collective-permute-start.9 = (bf16[32,1792]{1,0:T(8,128)(2,1)S(1)}, bf16[32,1792]{1,0:T(8,128)(2,1)S(1)}, u32[]{:S(2)}, u32[]{:S(2)}) collective-permute-start(bf16[32,1792]{1,0:T(8,128)(2,1)S(1)} %get-tuple-element.95), channel_id=1, source_target_pairs={{0,4},{1,5},{2,6},{3,7},{4,0},{5,1},{6,2},{7,3},{8,12},{9,13},{10,... | collective-permute-start | bytes 344072 | tf_op jit(solution)/shard_map/ppermute | solution.py:46
  23.2 1.4 %collective-permute-done.6.refs_2_ = bf16[64,1792]{1,0:T(8,128)(2,1)S(1)} collective-permute-done((bf16[64,1792]{1,0:T(8,128)(2,1)S(1)}, bf16[64,1792]{1,0:T(8,128)(2,1)S(1)}, u32[]{:S(2)}, u32[]{:S(2)}) %collective-permute-start.6) | collective-permute-done | bytes 229408 | tf_op jit(solution)/shard_map/ppermute | solution.py:46
  25.5 1.8 %collective-permute-done.7.refs_1_.refs_0_.x = bf16[32,1792]{1,0:T(8,128)(2,1)S(1)} collective-permute-done((bf16[32,1792]{1,0:T(8,128)(2,1)S(1)}, bf16[32,1792]{1,0:T(8,128)(2,1)S(1)}, u32[]{:S(2)}, u32[]{:S(2)}) %collective-permute-start.7) | collective-permute-done | bytes 114720 | tf_op jit(solution)/shard_map/ppermute | solution.py:46
  28.6 2.7 %collective-permute-start.22 = (bf16[64,1792]{1,0:T(8,128)(2,1)S(1)}, bf16[64,1792]{1,0:T(8,128)(2,1)S(1)}, u32[]{:S(2)}, u32[]{:S(2)}) collective-permute-start(bf16[64,1792]{1,0:T(8,128)(2,1)S(1)} %copy-done.4), channel_id=1, source_target_pairs={{0,12},{1,13},{2,14},{3,15},{4,8},{5,9},{6,10},{7,11},{8,4},{9,5},... | collective-permute-start | bytes 688136 | tf_op jit(solution)/shard_map/ppermute | solution.py:46
  31.8 2.0 %collective-permute-start.17 = (bf16[32,1792]{1,0:T(8,128)(2,1)S(1)}, bf16[32,1792]{1,0:T(8,128)(2,1)S(1)}, u32[]{:S(2)}, u32[]{:S(2)}) collective-permute-start(bf16[32,1792]{1,0:T(8,128)(2,1)S(1)} %shard_map.100), channel_id=1, source_target_pairs={{0,4},{1,5},{2,6},{3,7},{4,0},{5,1},{6,2},{7,3},{8,12},{9,13},{10,... | collective-permute-start | bytes 344072 | tf_op jit(solution)/shard_map/ppermute | solution.py:46
  36.0 1.4 %collective-permute-start.16 = (bf16[32,1792]{1,0:T(8,128)(2,1)S(1)}, bf16[32,1792]{1,0:T(8,128)(2,1)S(1)}, u32[]{:S(2)}, u32[]{:S(2)}) collective-permute-start(bf16[32,1792]{1,0:T(8,128)(2,1)S(1)} %get-tuple-element.92), channel_id=1, source_target_pairs={{0,2},{1,3},{2,0},{3,1},{4,6},{5,7},{6,4},{7,5},{8,10},{9,11},{10,... | collective-permute-start | bytes 344072 | tf_op jit(solution)/shard_map/ppermute | solution.py:46
  37.4 1.3 %shard_map.103 = (f32[64,1792]{1,0:T(8,128)S(1)}, bf16[64,1792]{1,0:T(8,128)(2,1)S(1)}) custom-call(bf16[256,512]{1,0:T(8,128)(2,1)S(1)} %get-tuple-element.36.refs_3_.refs_1_.refs_0_.x.grad.refs_12_, bf16[128,512]{1,0:T(8,128)(2,1)S(1)} %collective-permute-done.19.peer, bf16[1792,512]{1,0:T(8,128)(2,1)S(1)} %copy-done, ...), custom_call_target="tpu_custom_call" | custom-call | flops 1 | bytes 1 | tf_op jit(solution)/shard_map/pallas_call | solution.py:83
  39.0 1.7 %collective-permute-done.18.refs_3_ = bf16[32,1792]{1,0:T(8,128)(2,1)S(1)} collective-permute-done((bf16[32,1792]{1,0:T(8,128)(2,1)S(1)}, bf16[32,1792]{1,0:T(8,128)(2,1)S(1)}, u32[]{:S(2)}, u32[]{:S(2)}) %collective-permute-start.18) | collective-permute-done | bytes 114720 | tf_op jit(solution)/shard_map/ppermute | solution.py:46
  40.7 2.4 %collective-permute-done.17.refs_2_ = bf16[32,1792]{1,0:T(8,128)(2,1)S(1)} collective-permute-done((bf16[32,1792]{1,0:T(8,128)(2,1)S(1)}, bf16[32,1792]{1,0:T(8,128)(2,1)S(1)}, u32[]{:S(2)}, u32[]{:S(2)}) %collective-permute-start.17) | collective-permute-done | bytes 114720 | tf_op jit(solution)/shard_map/ppermute | solution.py:46
  48.1 1.6 %collective-permute-start.34 = (bf16[64,1792]{1,0:T(8,128)(2,1)S(1)}, bf16[64,1792]{1,0:T(8,128)(2,1)S(1)}, u32[]{:S(2)}, u32[]{:S(2)}) collective-permute-start(bf16[64,1792]{1,0:T(8,128)(2,1)S(1)} %shard_map.121.refs_0_), channel_id=1, source_target_pairs={{0,2},{1,3},{2,0},{3,1},{4,6},{5,7},{6,4},{7,5},{8,10},{9,11},{10,... | collective-permute-start | bytes 688136 | tf_op jit(solution)/shard_map/ppermute | solution.py:46
  49.7 1.3 %shard_map.113 = (f32[64,1792]{1,0:T(8,128)S(1)}, bf16[64,1792]{1,0:T(8,128)(2,1)S(1)}) custom-call(bf16[256,512]{1,0:T(8,128)(2,1)S(1)} %get-tuple-element.41.refs_0_.grad.refs_15_, bf16[128,512]{1,0:T(8,128)(2,1)S(1)} %shard_map.112.peer, bf16[1792,512]{1,0:T(8,128)(2,1)S(1)} %copy-done, bf16[1792,512]{1,0:T(8,128)(2,1)S(1)} %collective-permute-done.3.refs_3_.weight_peer), custom_call_target="tpu_custom_call" | custom-call | flops 1 | bytes 1 | tf_op jit(solution)/shard_map/pallas_call | solution.py:83
  51.0 1.3 %collective-permute-start.38 = (bf16[128,1792]{1,0:T(8,128)(2,1)S(1)}, bf16[128,1792]{1,0:T(8,128)(2,1)S(1)}, u32[]{:S(2)}, u32[]{:S(2)}) collective-permute-start(bf16[128,1792]{1,0:T(8,128)(2,1)S(1)} %shard_map.126), channel_id=1, source_target_pairs={{0,4},{1,5},{2,6},{3,7},{4,0},{5,1},{6,2},{7,3},{8,12},{9,13},{10,... | collective-permute-start | bytes 1376264 | tf_op jit(solution)/shard_map/ppermute | solution.py:46
  52.4 1.3 %shard_map.116 = (f32[64,1792]{1,0:T(8,128)S(1)}, bf16[64,1792]{1,0:T(8,128)(2,1)S(1)}) custom-call(bf16[256,512]{1,0:T(8,128)(2,1)S(1)} %shard_map.114.grad, bf16[128,512]{1,0:T(8,128)(2,1)S(1)} %collective-permute-done.28.peer, bf16[1792,512]{1,0:T(8,128)(2,1)S(1)} %copy-done, bf16[1792,512]{1,0:T(8,128)(2,1)S(1)} %collective-permute-done.3.refs_3_.weight_peer), custom_call_target="tpu_custom_call" | custom-call | flops 1 | bytes 1 | tf_op jit(solution)/shard_map/pallas_call | solution.py:83
  53.7 1.3 %shard_map.119 = (f32[64,1792]{1,0:T(8,128)S(1)}, bf16[64,1792]{1,0:T(8,128)(2,1)S(1)}) custom-call(bf16[256,512]{1,0:T(8,128)(2,1)S(1)} %shard_map.118.grad, bf16[128,512]{1,0:T(8,128)(2,1)S(1)} %collective-permute-done.32.peer, bf16[1792,512]{1,0:T(8,128)(2,1)S(1)} %copy-done, bf16[1792,512]{1,0:T(8,128)(2,1)S(1)} %collective-permute-done.3.refs_3_.weight_peer), custom_call_target="tpu_custom_call" | custom-call | flops 1 | bytes 1 | tf_op jit(solution)/shard_map/pallas_call | solution.py:83
  55.7 1.6 %collective-permute-start.30 = (bf16[32,1792]{1,0:T(8,128)(2,1)S(1)}, bf16[32,1792]{1,0:T(8,128)(2,1)S(1)}, u32[]{:S(2)}, u32[]{:S(2)}) collective-permute-start(bf16[32,1792]{1,0:T(8,128)(2,1)S(1)} %get-tuple-element.91), channel_id=1, source_target_pairs={{0,2},{1,3},{2,0},{3,1},{4,6},{5,7},{6,4},{7,5},{8,10},{9,11},{10,... | collective-permute-start | bytes 344072 | tf_op jit(solution)/shard_map/ppermute | solution.py:46
  57.9 1.6 %collective-permute-start.29 = (bf16[32,1792]{1,0:T(8,128)(2,1)S(1)}, bf16[32,1792]{1,0:T(8,128)(2,1)S(1)}, u32[]{:S(2)}, u32[]{:S(2)}) collective-permute-start(bf16[32,1792]{1,0:T(8,128)(2,1)S(1)} %get-tuple-element.89), channel_id=1, source_target_pairs={{0,2},{1,3},{2,0},{3,1},{4,6},{5,7},{6,4},{7,5},{8,10},{9,11},{10,... | collective-permute-start | bytes 344072 | tf_op jit(solution)/shard_map/ppermute | solution.py:46
  59.5 6.6 %collective-permute-done.30 = bf16[32,1792]{1,0:T(8,128)(2,1)S(1)} collective-permute-done((bf16[32,1792]{1,0:T(8,128)(2,1)S(1)}, bf16[32,1792]{1,0:T(8,128)(2,1)S(1)}, u32[]{:S(2)}, u32[]{:S(2)}) %collective-permute-start.30) | collective-permute-done | bytes 114720 | tf_op jit(solution)/shard_map/ppermute | solution.py:46
  66.6 2.0 %collective-permute-done.36 = bf16[32,1792]{1,0:T(8,128)(2,1)S(1)} collective-permute-done((bf16[32,1792]{1,0:T(8,128)(2,1)S(1)}, bf16[32,1792]{1,0:T(8,128)(2,1)S(1)}, u32[]{:S(2)}, u32[]{:S(2)}) %collective-permute-start.36) | collective-permute-done | bytes 114720 | tf_op jit(solution)/shard_map/ppermute | solution.py:46
  69.5 1.3 %collective-permute-start.42 = (bf16[32,1792]{1,0:T(8,128)(2,1)S(1)}, bf16[32,1792]{1,0:T(8,128)(2,1)S(1)}, u32[]{:S(2)}, u32[]{:S(2)}) collective-permute-start(bf16[32,1792]{1,0:T(8,128)(2,1)S(1)} %shard_map.123.refs_1_), channel_id=1, source_target_pairs={{0,4},{1,5},{2,6},{3,7},{4,0},{5,1},{6,2},{7,3},{8,12},{9,13},{10,... | collective-permute-start | bytes 344072 | tf_op jit(solution)/shard_map/ppermute | solution.py:46
  71.0 1.4 %collective-permute-done.41 = bf16[32,1792]{1,0:T(8,128)(2,1)S(1)} collective-permute-done((bf16[32,1792]{1,0:T(8,128)(2,1)S(1)}, bf16[32,1792]{1,0:T(8,128)(2,1)S(1)}, u32[]{:S(2)}, u32[]{:S(2)}) %collective-permute-start.41) | collective-permute-done | bytes 114720 | tf_op jit(solution)/shard_map/ppermute | solution.py:46
  77.5 5.3 %collective-permute-done.47 = bf16[64,1792]{1,0:T(8,128)(2,1)S(1)} collective-permute-done((bf16[64,1792]{1,0:T(8,128)(2,1)S(1)}, bf16[64,1792]{1,0:T(8,128)(2,1)S(1)}, u32[]{:S(2)}, u32[]{:S(2)}) %collective-permute-start.47) | collective-permute-done | bytes 229408 | tf_op jit(solution)/shard_map/ppermute | solution.py:46
  83.8 2.4 %collective-permute-start.50 = (bf16[32,1792]{1,0:T(8,128)(2,1)S(1)}, bf16[32,1792]{1,0:T(8,128)(2,1)S(1)}, u32[]{:S(2)}, u32[]{:S(2)}) collective-permute-start(bf16[32,1792]{1,0:T(8,128)(2,1)S(1)} %shard_map.130.refs_1_.refs_3_.refs_16_), channel_id=1, source_target_pairs={{0,12},{1,13},{2,14},{3,15},{4,8},{5,9},{6,10},{7,11},{8,4},{9,5},... | collective-permute-start | bytes 344072 | tf_op jit(solution)/shard_map/ppermute | solution.py:46
  86.2 1.4 %collective-permute-start.49 = (bf16[32,1792]{1,0:T(8,128)(2,1)S(1)}, bf16[32,1792]{1,0:T(8,128)(2,1)S(1)}, u32[]{:S(2)}, u32[]{:S(2)}) collective-permute-start(bf16[32,1792]{1,0:T(8,128)(2,1)S(1)} %shard_map.129.refs_0_.refs_2_), channel_id=1, source_target_pairs={{0,12},{1,13},{2,14},{3,15},{4,8},{5,9},{6,10},{7,11},{8,4},{9,5},... | collective-permute-start | bytes 344072 | tf_op jit(solution)/shard_map/ppermute | solution.py:46
  87.7 2.0 %shard_map.132 = f32[1024,512]{1,0:T(8,128)} custom-call(s32[16]{0:T(128)S(1)} %stack.67.refs_0_, f32[256,512]{1,0:T(8,128)S(1)} %get-tuple-element.35.refs_1_, f32[256,512]{1,0:T(8,128)S(1)} %get-tuple-element.37.refs_2_, f32[256,512]{1,0:T(8,128)S(1)} %get-tuple-element.42.refs_3_, f32[256,512]{1,0:T(8,128)S(1)} %shard_map.131.refs_4_), custom_call_target="tpu_custom_call" | custom-call | flops 1 | bytes 1 | tf_op jit(solution)/shard_map/pallas_call | solution.py:83
  90.3 7.1 %shard_map.136 = (f32[512,1792]{1,0:T(8,128)}, f32[1792,512]{1,0:T(8,128)}, f32[8,128]{1,0:T(8,128)S(1)}) custom-call(bf16[256,512]{1,0:T(8,128)(2,1)S(1)} %get-tuple-element.40.refs_5_.refs_0_, bf16[256,512]{1,0:T(8,128)(2,1)S(1)} %get-tuple-element.50.refs_0_.refs_1_, bf16[256,512]{1,0:T(8,128)(2,1)S(1)} %get-tuple-element.51.refs_1_.refs_2_, ...), custom_call_target="tpu_custom_call" | custom-call | flops 1 | bytes 1 | tf_op jit(solution)/shard_map/pallas_call | solution.py:83
  (147 shorter events, 22.9 us)
Async XLA Ops:
  0.6 18.0 %collective-permute-start.3 = (bf16[1792,512]{1,0:T(8,128)(2,1)}, bf16[1792,512]{1,0:T(8,128)(2,1)S(1)}, u32[]{:S(2)}, u32[]{:S(2)}) collective-permute-start(bf16[1792,512]{1,0:T(8,128)(2,1)} %refs_3_.7), channel_id=1, source_target_pairs={{0,1},{1,0},{2,3},{3,2},{4,5},{5,4},{6,7},{7,6},{8,9},{9,8},{10,11... | collective-permute-start | bytes 5505032 | tf_op jit(solution)/shard_map/ppermute | solution.py:46
  1.1 12.4 %collective-permute-start = (bf16[64,1792]{1,0:T(8,128)(2,1)}, bf16[64,1792]{1,0:T(8,128)(2,1)S(1)}, u32[]{:S(2)}, u32[]{:S(2)}) collective-permute-start(bf16[64,1792]{1,0:T(8,128)(2,1)} %bitcast.24), channel_id=1, source_target_pairs={{0,2},{1,3},{2,0},{3,1},{4,6},{5,7},{6,4},{7,5},{8,10},{9,11},{10,... | collective-permute-start | bytes 688136 | tf_op jit(solution)/shard_map/ppermute | solution.py:46
  3.7 9.9 %collective-permute-start.2 = (bf16[64,1792]{1,0:T(8,128)(2,1)}, bf16[64,1792]{1,0:T(8,128)(2,1)S(1)}, u32[]{:S(2)}, u32[]{:S(2)}) collective-permute-start(bf16[64,1792]{1,0:T(8,128)(2,1)} %bitcast.25), channel_id=1, source_target_pairs={{0,4},{1,5},{2,6},{3,7},{4,0},{5,1},{6,2},{7,3},{8,12},{9,13},{10,... | collective-permute-start | bytes 688136 | tf_op jit(solution)/shard_map/ppermute | solution.py:46
  5.3 13.4 %collective-permute-start.1 = (bf16[64,1792]{1,0:T(8,128)(2,1)}, bf16[64,1792]{1,0:T(8,128)(2,1)S(1)}, u32[]{:S(2)}, u32[]{:S(2)}) collective-permute-start(bf16[64,1792]{1,0:T(8,128)(2,1)} %bitcast.26), channel_id=1, source_target_pairs={{0,12},{1,13},{2,14},{3,15},{4,8},{5,9},{6,10},{7,11},{8,4},{9,5},... | collective-permute-start | bytes 688136 | tf_op jit(solution)/shard_map/ppermute | solution.py:46
  7.8 10.9 %collective-permute-start.4 = (bf16[64,1792]{1,0:T(8,128)(2,1)}, bf16[64,1792]{1,0:T(8,128)(2,1)S(1)}, u32[]{:S(2)}, u32[]{:S(2)}) collective-permute-start(bf16[64,1792]{1,0:T(8,128)(2,1)} %refs_0_.1), channel_id=1, source_target_pairs={{0,2},{1,3},{2,0},{3,1},{4,6},{5,7},{6,4},{7,5},{8,10},{9,11},{10,... | collective-permute-start | bytes 688136 | tf_op jit(solution)/shard_map/ppermute | solution.py:46
  18.9 6.5 %collective-permute-start.10 = (bf16[32,1792]{1,0:T(8,128)(2,1)S(1)}, bf16[32,1792]{1,0:T(8,128)(2,1)S(1)}, u32[]{:S(2)}, u32[]{:S(2)}) collective-permute-start(bf16[32,1792]{1,0:T(8,128)(2,1)S(1)} %get-tuple-element.94), channel_id=1, source_target_pairs={{0,4},{1,5},{2,6},{3,7},{4,0},{5,1},{6,2},{7,3},{8,12},{9,13},{10,... | collective-permute-start | bytes 344072 | tf_op jit(solution)/shard_map/ppermute | solution.py:46
  19.6 7.7 %collective-permute-start.8 = (bf16[32,1792]{1,0:T(8,128)(2,1)S(1)}, bf16[32,1792]{1,0:T(8,128)(2,1)S(1)}, u32[]{:S(2)}, u32[]{:S(2)}) collective-permute-start(bf16[32,1792]{1,0:T(8,128)(2,1)S(1)} %get-tuple-element.94), channel_id=1, source_target_pairs={{0,2},{1,3},{2,0},{3,1},{4,6},{5,7},{6,4},{7,5},{8,10},{9,11},{10,... | collective-permute-start | bytes 344072 | tf_op jit(solution)/shard_map/ppermute | solution.py:46
  20.1 7.2 %collective-permute-start.7 = (bf16[32,1792]{1,0:T(8,128)(2,1)S(1)}, bf16[32,1792]{1,0:T(8,128)(2,1)S(1)}, u32[]{:S(2)}, u32[]{:S(2)}) collective-permute-start(bf16[32,1792]{1,0:T(8,128)(2,1)S(1)} %get-tuple-element.95), channel_id=1, source_target_pairs={{0,2},{1,3},{2,0},{3,1},{4,6},{5,7},{6,4},{7,5},{8,10},{9,11},{10,... | collective-permute-start | bytes 344072 | tf_op jit(solution)/shard_map/ppermute | solution.py:46
  21.6 5.7 %collective-permute-start.9 = (bf16[32,1792]{1,0:T(8,128)(2,1)S(1)}, bf16[32,1792]{1,0:T(8,128)(2,1)S(1)}, u32[]{:S(2)}, u32[]{:S(2)}) collective-permute-start(bf16[32,1792]{1,0:T(8,128)(2,1)S(1)} %get-tuple-element.95), channel_id=1, source_target_pairs={{0,4},{1,5},{2,6},{3,7},{4,0},{5,1},{6,2},{7,3},{8,12},{9,13},{10,... | collective-permute-start | bytes 344072 | tf_op jit(solution)/shard_map/ppermute | solution.py:46
  28.6 10.4 %collective-permute-start.22 = (bf16[64,1792]{1,0:T(8,128)(2,1)S(1)}, bf16[64,1792]{1,0:T(8,128)(2,1)S(1)}, u32[]{:S(2)}, u32[]{:S(2)}) collective-permute-start(bf16[64,1792]{1,0:T(8,128)(2,1)S(1)} %copy-done.4), channel_id=1, source_target_pairs={{0,12},{1,13},{2,14},{3,15},{4,8},{5,9},{6,10},{7,11},{8,4},{9,5},... | collective-permute-start | bytes 688136 | tf_op jit(solution)/shard_map/ppermute | solution.py:46
  31.8 8.9 %collective-permute-start.18 = (bf16[32,1792]{1,0:T(8,128)(2,1)S(1)}, bf16[32,1792]{1,0:T(8,128)(2,1)S(1)}, u32[]{:S(2)}, u32[]{:S(2)}) collective-permute-start(bf16[32,1792]{1,0:T(8,128)(2,1)S(1)} %shard_map.101), channel_id=1, source_target_pairs={{0,4},{1,5},{2,6},{3,7},{4,0},{5,1},{6,2},{7,3},{8,12},{9,13},{10,... | collective-permute-start | bytes 344072 | tf_op jit(solution)/shard_map/ppermute | solution.py:46
  31.8 11.3 %collective-permute-start.17 = (bf16[32,1792]{1,0:T(8,128)(2,1)S(1)}, bf16[32,1792]{1,0:T(8,128)(2,1)S(1)}, u32[]{:S(2)}, u32[]{:S(2)}) collective-permute-start(bf16[32,1792]{1,0:T(8,128)(2,1)S(1)} %shard_map.100), channel_id=1, source_target_pairs={{0,4},{1,5},{2,6},{3,7},{4,0},{5,1},{6,2},{7,3},{8,12},{9,13},{10,... | collective-permute-start | bytes 344072 | tf_op jit(solution)/shard_map/ppermute | solution.py:46
  34.6 9.1 %collective-permute-start.15 = (bf16[32,1792]{1,0:T(8,128)(2,1)S(1)}, bf16[32,1792]{1,0:T(8,128)(2,1)S(1)}, u32[]{:S(2)}, u32[]{:S(2)}) collective-permute-start(bf16[32,1792]{1,0:T(8,128)(2,1)S(1)} %get-tuple-element.93), channel_id=1, source_target_pairs={{0,2},{1,3},{2,0},{3,1},{4,6},{5,7},{6,4},{7,5},{8,10},{9,11},{10,... | collective-permute-start | bytes 344072 | tf_op jit(solution)/shard_map/ppermute | solution.py:46
  36.0 7.7 %collective-permute-start.16 = (bf16[32,1792]{1,0:T(8,128)(2,1)S(1)}, bf16[32,1792]{1,0:T(8,128)(2,1)S(1)}, u32[]{:S(2)}, u32[]{:S(2)}) collective-permute-start(bf16[32,1792]{1,0:T(8,128)(2,1)S(1)} %get-tuple-element.92), channel_id=1, source_target_pairs={{0,2},{1,3},{2,0},{3,1},{4,6},{5,7},{6,4},{7,5},{8,10},{9,11},{10,... | collective-permute-start | bytes 344072 | tf_op jit(solution)/shard_map/ppermute | solution.py:46
  44.4 9.3 %collective-permute-start.31 = (bf16[64,1792]{1,0:T(8,128)(2,1)S(1)}, bf16[64,1792]{1,0:T(8,128)(2,1)S(1)}, u32[]{:S(2)}, u32[]{:S(2)}) collective-permute-start(bf16[64,1792]{1,0:T(8,128)(2,1)S(1)} %shard_map.117), channel_id=1, source_target_pairs={{0,2},{1,3},{2,0},{3,1},{4,6},{5,7},{6,4},{7,5},{8,10},{9,11},{10,... | collective-permute-start | bytes 688136 | tf_op jit(solution)/shard_map/ppermute | solution.py:46
  45.0 10.0 %collective-permute-start.43 = (bf16[64,1792]{1,0:T(8,128)(2,1)S(1)}, bf16[64,1792]{1,0:T(8,128)(2,1)S(1)}, u32[]{:S(2)}, u32[]{:S(2)}) collective-permute-start(bf16[64,1792]{1,0:T(8,128)(2,1)S(1)} %shard_map.121.refs_0_), channel_id=1, source_target_pairs={{0,4},{1,5},{2,6},{3,7},{4,0},{5,1},{6,2},{7,3},{8,12},{9,13},{10,... | collective-permute-start | bytes 688136 | tf_op jit(solution)/shard_map/ppermute | solution.py:46
  48.0 5.8 %collective-permute-start.32 = (bf16[128,512]{1,0:T(8,128)(2,1)S(1)}, bf16[128,512]{1,0:T(8,128)(2,1)S(1)}, u32[]{:S(2)}, u32[]{:S(2)}) collective-permute-start(bf16[128,512]{1,0:T(8,128)(2,1)S(1)} %slice.127), channel_id=1, source_target_pairs={{0,1},{1,0},{2,3},{3,2},{4,5},{5,4},{6,7},{7,6},{8,9},{9,8},{10,11... | collective-permute-start | bytes 393224 | tf_op jit(solution)/shard_map/ppermute | solution.py:46
  48.1 9.6 %collective-permute-start.34 = (bf16[64,1792]{1,0:T(8,128)(2,1)S(1)}, bf16[64,1792]{1,0:T(8,128)(2,1)S(1)}, u32[]{:S(2)}, u32[]{:S(2)}) collective-permute-start(bf16[64,1792]{1,0:T(8,128)(2,1)S(1)} %shard_map.121.refs_0_), channel_id=1, source_target_pairs={{0,2},{1,3},{2,0},{3,1},{4,6},{5,7},{6,4},{7,5},{8,10},{9,11},{10,... | collective-permute-start | bytes 688136 | tf_op jit(solution)/shard_map/ppermute | solution.py:46
  51.0 18.4 %collective-permute-start.38 = (bf16[128,1792]{1,0:T(8,128)(2,1)S(1)}, bf16[128,1792]{1,0:T(8,128)(2,1)S(1)}, u32[]{:S(2)}, u32[]{:S(2)}) collective-permute-start(bf16[128,1792]{1,0:T(8,128)(2,1)S(1)} %shard_map.126), channel_id=1, source_target_pairs={{0,4},{1,5},{2,6},{3,7},{4,0},{5,1},{6,2},{7,3},{8,12},{9,13},{10,... | collective-permute-start | bytes 1376264 | tf_op jit(solution)/shard_map/ppermute | solution.py:46
  55.1 21.8 %collective-permute-start.44 = (bf16[64,1792]{1,0:T(8,128)(2,1)S(1)}, bf16[64,1792]{1,0:T(8,128)(2,1)S(1)}, u32[]{:S(2)}, u32[]{:S(2)}) collective-permute-start(bf16[64,1792]{1,0:T(8,128)(2,1)S(1)} %shard_map.133.refs_0_), channel_id=1, source_target_pairs={{0,2},{1,3},{2,0},{3,1},{4,6},{5,7},{6,4},{7,5},{8,10},{9,11},{10,... | collective-permute-start | bytes 688136 | tf_op jit(solution)/shard_map/ppermute | solution.py:46
  55.7 10.4 %collective-permute-start.30 = (bf16[32,1792]{1,0:T(8,128)(2,1)S(1)}, bf16[32,1792]{1,0:T(8,128)(2,1)S(1)}, u32[]{:S(2)}, u32[]{:S(2)}) collective-permute-start(bf16[32,1792]{1,0:T(8,128)(2,1)S(1)} %get-tuple-element.91), channel_id=1, source_target_pairs={{0,2},{1,3},{2,0},{3,1},{4,6},{5,7},{6,4},{7,5},{8,10},{9,11},{10,... | collective-permute-start | bytes 344072 | tf_op jit(solution)/shard_map/ppermute | solution.py:46
  57.3 11.3 %collective-permute-start.36 = (bf16[32,1792]{1,0:T(8,128)(2,1)S(1)}, bf16[32,1792]{1,0:T(8,128)(2,1)S(1)}, u32[]{:S(2)}, u32[]{:S(2)}) collective-permute-start(bf16[32,1792]{1,0:T(8,128)(2,1)S(1)} %get-tuple-element.90), channel_id=1, source_target_pairs={{0,2},{1,3},{2,0},{3,1},{4,6},{5,7},{6,4},{7,5},{8,10},{9,11},{10,... | collective-permute-start | bytes 344072 | tf_op jit(solution)/shard_map/ppermute | solution.py:46
  57.9 13.1 %collective-permute-start.29 = (bf16[32,1792]{1,0:T(8,128)(2,1)S(1)}, bf16[32,1792]{1,0:T(8,128)(2,1)S(1)}, u32[]{:S(2)}, u32[]{:S(2)}) collective-permute-start(bf16[32,1792]{1,0:T(8,128)(2,1)S(1)} %get-tuple-element.89), channel_id=1, source_target_pairs={{0,2},{1,3},{2,0},{3,1},{4,6},{5,7},{6,4},{7,5},{8,10},{9,11},{10,... | collective-permute-start | bytes 344072 | tf_op jit(solution)/shard_map/ppermute | solution.py:46
  66.1 6.3 %collective-permute-start.41 = (bf16[32,1792]{1,0:T(8,128)(2,1)S(1)}, bf16[32,1792]{1,0:T(8,128)(2,1)S(1)}, u32[]{:S(2)}, u32[]{:S(2)}) collective-permute-start(bf16[32,1792]{1,0:T(8,128)(2,1)S(1)} %get-tuple-element.88), channel_id=1, source_target_pairs={{0,2},{1,3},{2,0},{3,1},{4,6},{5,7},{6,4},{7,5},{8,10},{9,11},{10,... | collective-permute-start | bytes 344072 | tf_op jit(solution)/shard_map/ppermute | solution.py:46
  68.6 4.9 %collective-permute-start.33 = (bf16[32,1792]{1,0:T(8,128)(2,1)S(1)}, bf16[32,1792]{1,0:T(8,128)(2,1)S(1)}, u32[]{:S(2)}, u32[]{:S(2)}) collective-permute-start(bf16[32,1792]{1,0:T(8,128)(2,1)S(1)} %shard_map.120.refs_0_), channel_id=1, source_target_pairs={{0,4},{1,5},{2,6},{3,7},{4,0},{5,1},{6,2},{7,3},{8,12},{9,13},{10,... | collective-permute-start | bytes 344072 | tf_op jit(solution)/shard_map/ppermute | solution.py:46
  69.5 5.3 %collective-permute-start.42 = (bf16[32,1792]{1,0:T(8,128)(2,1)S(1)}, bf16[32,1792]{1,0:T(8,128)(2,1)S(1)}, u32[]{:S(2)}, u32[]{:S(2)}) collective-permute-start(bf16[32,1792]{1,0:T(8,128)(2,1)S(1)} %shard_map.123.refs_1_), channel_id=1, source_target_pairs={{0,4},{1,5},{2,6},{3,7},{4,0},{5,1},{6,2},{7,3},{8,12},{9,13},{10,... | collective-permute-start | bytes 344072 | tf_op jit(solution)/shard_map/ppermute | solution.py:46
  74.8 8.1 %collective-permute-start.47 = (bf16[64,1792]{1,0:T(8,128)(2,1)S(1)}, bf16[64,1792]{1,0:T(8,128)(2,1)S(1)}, u32[]{:S(2)}, u32[]{:S(2)}) collective-permute-start(bf16[64,1792]{1,0:T(8,128)(2,1)S(1)} %get-tuple-element.49.refs_0_.refs_2_), channel_id=1, source_target_pairs={{0,2},{1,3},{2,0},{3,1},{4,6},{5,7},{6,4},{7,5},{8,10},{9,11},{10,... | collective-permute-start | bytes 688136 | tf_op jit(solution)/shard_map/ppermute | solution.py:46
  77.0 12.7 %collective-permute-start.45 = (bf16[64,1792]{1,0:T(8,128)(2,1)S(1)}, bf16[64,1792]{1,0:T(8,128)(2,1)S(1)}, u32[]{:S(2)}, u32[]{:S(2)}) collective-permute-start(bf16[64,1792]{1,0:T(8,128)(2,1)S(1)} %get-tuple-element.67), channel_id=1, source_target_pairs={{0,1},{1,0},{2,3},{3,2},{4,5},{5,4},{6,7},{7,6},{8,9},{9,8},{10,11... | collective-permute-start | bytes 688136 | tf_op jit(solution)/shard_map/ppermute | solution.py:46
  77.2 12.5 %collective-permute-start.46 = (bf16[64,1792]{1,0:T(8,128)(2,1)S(1)}, bf16[64,1792]{1,0:T(8,128)(2,1)S(1)}, u32[]{:S(2)}, u32[]{:S(2)}) collective-permute-start(bf16[64,1792]{1,0:T(8,128)(2,1)S(1)} %get-tuple-element.66), channel_id=1, source_target_pairs={{0,1},{1,0},{2,3},{3,2},{4,5},{5,4},{6,7},{7,6},{8,9},{9,8},{10,11... | collective-permute-start | bytes 688136 | tf_op jit(solution)/shard_map/ppermute | solution.py:46
  82.9 14.5 %collective-permute-start.48 = (bf16[64,1792]{1,0:T(8,128)(2,1)S(1)}, bf16[64,1792]{1,0:T(8,128)(2,1)S(1)}, u32[]{:S(2)}, u32[]{:S(2)}) collective-permute-start(bf16[64,1792]{1,0:T(8,128)(2,1)S(1)} %add_convert_fusion), channel_id=1, source_target_pairs={{0,4},{1,5},{2,6},{3,7},{4,0},{5,1},{6,2},{7,3},{8,12},{9,13},{10,... | collective-permute-start | bytes 688136 | tf_op jit(solution)/shard_map/ppermute | solution.py:46
  83.8 13.6 %collective-permute-start.50 = (bf16[32,1792]{1,0:T(8,128)(2,1)S(1)}, bf16[32,1792]{1,0:T(8,128)(2,1)S(1)}, u32[]{:S(2)}, u32[]{:S(2)}) collective-permute-start(bf16[32,1792]{1,0:T(8,128)(2,1)S(1)} %shard_map.130.refs_1_.refs_3_.refs_16_), channel_id=1, source_target_pairs={{0,12},{1,13},{2,14},{3,15},{4,8},{5,9},{6,10},{7,11},{8,4},{9,5},... | collective-permute-start | bytes 344072 | tf_op jit(solution)/shard_map/ppermute | solution.py:46
  86.2 11.1 %collective-permute-start.49 = (bf16[32,1792]{1,0:T(8,128)(2,1)S(1)}, bf16[32,1792]{1,0:T(8,128)(2,1)S(1)}, u32[]{:S(2)}, u32[]{:S(2)}) collective-permute-start(bf16[32,1792]{1,0:T(8,128)(2,1)S(1)} %shard_map.129.refs_0_.refs_2_), channel_id=1, source_target_pairs={{0,12},{1,13},{2,14},{3,15},{4,8},{5,9},{6,10},{7,11},{8,4},{9,5},... | collective-permute-start | bytes 344072 | tf_op jit(solution)/shard_map/ppermute | solution.py:46
  (25 other events, 80.5 us)

commit v3 on v2

--- a/solution.py
+++ b/solution.py
@@ -64,7 +64,7 @@
 
 VMEM = pl.BlockSpec(memory_space=pltpu.VMEM)
 ANY = pl.BlockSpec(memory_space=pl.ANY)
-PARAMS = pltpu.CompilerParams(vmem_limit_bytes=40 * 2**20)
+PARAMS = pltpu.CompilerParams(vmem_limit_bytes=16 * 2**20)
 NT = (((1,), (1,)), ((), ()))
 NN = (((1,), (0,)), ((), ()))
 TN = (((0,), (0,)), ((), ()))
@@ -228,43 +228,79 @@
     )
 
 
-def tokens_kernel(*refs):
-    codes, errs, srcs, grads = (refs[NZ * k : NZ * k + NZ] for k in range(4))
-    dec_grad, enc_grad, token, turned = refs[4 * NZ + 1 :]
-    token[...] = jnp.zeros_like(token)
-    n, tile = codes[0].shape[0], enc_grad.shape[0]
-
-    @pl.when(pl.program_id(0) == 0)
-    def _():
-        for j in range(NZ):
-            turned[:, j * n : (j + 1) * n] = codes[j][...].T
-
-    cols = pl.ds(pl.multiple_of(pl.program_id(0) * tile, tile), tile)
-    dec_grad[...] = sum(
-        dot(turned[:, j * n : (j + 1) * n], errs[j][:, cols], NN) for j in range(NZ)
-    )
-    enc_grad[...] = sum(dot(srcs[j][:, cols], grads[j][...], TN) for j in range(NZ))
-
-
-def tokens_step(codes, errs, srcs, grads, last, tile=256):
+def early_kernel(*refs):
+    count = (len(refs) - 3) // 4
+    codes, errs, srcs, grads = (refs[count * k : count * (k + 1)] for k in range(4))
+    dec_grad, enc_grad, turned = refs[4 * count :]
+    n, tile = codes[0].shape[0], 256
+    for j in range(count):
+        turned[:, j * n : (j + 1) * n] = codes[j][...].T
+
+    @pl.loop(0, errs[0].shape[1] // tile)
+    def _(t):
+        cols = pl.ds(pl.multiple_of(t * tile, tile), tile)
+        dec_grad[:, cols] = sum(
+            dot(turned[:, j * n : (j + 1) * n], errs[j][:, cols], NN) for j in range(count)
+        )
+        enc_grad[cols, :] = sum(dot(srcs[j][:, cols], grads[j][...], TN) for j in range(count))
+
+
+def early_step(codes, errs, srcs, grads):
     n, lat = codes[0].shape
     d = errs[0].shape[1]
     return call(
-        tokens_kernel,
-        [like((lat, d), F32), like((d, lat), F32), like((8, 128), F32)],
-        4 * NZ * n * d * lat,
+        early_kernel,
+        [like((lat, d), F32), like((d, lat), F32)],
+        1,
         *codes,
         *errs,
         *srcs,
         *grads,
-        last,
+        scratch_shapes=[pltpu.VMEM((lat, len(codes) * n), BF)],
+    )
+
+
+def late_kernel(*refs):
+    count = (len(refs) - 6) // 4
+    codes, errs, srcs, grads = (refs[count * k : count * (k + 1)] for k in range(4))
+    dec_part, enc_part, dec_grad, enc_grad, token, turned = refs[4 * count :]
+    token[...] = jnp.zeros_like(token)
+    n, tile = codes[0].shape[0], enc_grad.shape[0]
+
+    @pl.when(pl.program_id(0) == 0)
+    def _():
+        for j in range(count):
+            turned[:, j * n : (j + 1) * n] = codes[j][...].T
+
+    cols = pl.ds(pl.multiple_of(pl.program_id(0) * tile, tile), tile)
+    dec_grad[...] = dec_part[:, cols] + sum(
+        dot(turned[:, j * n : (j + 1) * n], errs[j][:, cols], NN) for j in range(count)
+    )
+    enc_grad[...] = enc_part[cols, :] + sum(
+        dot(srcs[j][:, cols], grads[j][...], TN) for j in range(count)
+    )
+
+
+def late_step(codes, errs, srcs, grads, dec_part, enc_part, tile=256):
+    n, lat = codes[0].shape
+    d = errs[0].shape[1]
+    return call(
+        late_kernel,
+        [like((lat, d), F32), like((d, lat), F32), like((8, 128), F32)],
+        1,
+        *codes,
+        *errs,
+        *srcs,
+        *grads,
+        dec_part,
+        enc_part,
         grid=(d // tile,),
         out_specs=[
             pl.BlockSpec((lat, tile), lambda t: (0, t)),
             pl.BlockSpec((tile, lat), lambda t: (t, 0)),
             VMEM,
         ],
-        scratch_shapes=[pltpu.VMEM((lat, NZ * n), BF)],
+        scratch_shapes=[pltpu.VMEM((lat, len(codes) * n), BF)],
     )
 
 
@@ -276,25 +312,32 @@
     return call(after_kernel, [like(x.shape, x.dtype)], 0, x, *others)[0]
 
 
-def finish_kernel(keep, back, pair, top, bottom, token, out):
-    n = top.shape[0]
-    own = keep[...] + back[...].astype(F32) + pair[...].astype(F32)
-    out[:n] = own[:n] + top[...].astype(F32)
-    out[n:] = own[n:] + bottom[...].astype(F32)
-
-
-def pack_kernel(count, *refs):
+def add_kernel(keep, back, *refs):
+    refs[-1][...] = (keep[...] + back[...].astype(F32)).astype(refs[-1].dtype)
+
+
+def add(keep, back, kind, *others):
+    return call(add_kernel, [like(keep.shape, kind)], 0, keep, back, *others)[0]
+
+
+def finish_kernel(own, pair, far, token, out):
+    out[...] = own[...] + pair[...].astype(F32) + far[...].astype(F32)
+
+
+def pack_kernel(spans, *refs):
     row = 0
-    for part in refs[:count]:
-        n = part.shape[0]
-        refs[-1][row : row + n] = part[...]
+    for ref, (start, n) in zip(refs, spans):
+        refs[-1][row : row + n] = ref[start : start + n]
         row += n
 
 
 def pack(parts, *others):
-    n = sum(part.shape[0] for part in parts)
-    out = like((n, parts[0].shape[1]), parts[0].dtype)
-    return call(lambda *refs: pack_kernel(len(parts), *refs), [out], 0, *parts, *others)[0]
+    parts = [part if isinstance(part, tuple) else (part, 0, part.shape[0]) for part in parts]
+    spans = [part[1:] for part in parts]
+    first = parts[0][0]
+    out = like((sum(n for _, n in spans), first.shape[1]), first.dtype)
+    arrays = [part[0] for part in parts]
+    return call(lambda *refs: pack_kernel(spans, *refs), [out], 0, *arrays, *others)[0]
 
 
 def pieces(send, x, count=2):
@@ -332,70 +375,63 @@
         return pre_step(j, half, others, enc_weight, bias, flags)
 
     x, s = errors[0], sources
-    y0, m, p = over_y(x), over_mirror(x), over_pair(x)
-    s_y0, s_m = over_y(s), over_mirror(s)
+    m, p = over_mirror(x), over_pair(x)
+    y0, s_y0 = over_y(x), over_y(s)
     weight_peer = over_core(enc_weight)
     m = after(m, y0, p, flags, weight_peer)
-    y1, q = pieces(over_y, m), pieces(over_pair, m)
-    half0 = pack([x, y0], m, s_y0)
-    other0 = pieces(over_core, half0)
-    s_x = pack([s, s_y0], half0)
-    s_other0 = pieces(over_core, s_x)
-    errs0, total0, grad0 = code(0, half0, other0)
-    q1 = [over_pair(after(part, grad0)) for part in y1]
-    p = after(p, y1[0], grad0)
-    y2 = pieces(over_y, p)
-    half1 = pack([m, *y1], grad0, *q)
-    other1, peer0 = pieces(over_core, half1, 4), across(after(grad0, half1))
-    errs1, total1, grad1 = code(1, half1, other1)
-    keep0, send0 = term(grad0, peer0)
-    srcs0, codes0 = pre(0, s_x, [after(s_other0[0], grad1), s_other0[1]])
-    half3 = pack([*q, *q1], send0, codes0, s_m)
-    half2 = pack([p, *y2], half3)
-    other3, other2 = pieces(over_core, half3), pieces(over_core, half2)
-    back0, peer1 = over_y(after(send0, half3)), across(after(grad1, half3))
+    y1, q = over_y(m), over_pair(m)
+    s = after(s, m)
+    s_p, s_m = over_pair(s), over_mirror(s)
+    q1, y2 = over_pair(y1), over_y(after(p, y1))
+    s_y2 = over_y(s_p)
+    half0 = pack([x, y0, s, s_y0], y1)
+    half3 = pack([q, q1], s_m, s_y2, y2)
+    other3 = over_core(half3)
+    halves = pack([half0, m, y1, p, y2], half3)
+    others = over_core(halves)
     s_m = after(s_m, half3)
     s_y1, s_q = over_y(s_m), over_pair(s_m)
-    s_p = over_pair(after(s_x, half3))
-    errs3, total3, grad3 = code(3, half3, other3)
+    errs3, total3, grad3 = code(3, half3, [other3])
     peer3 = across(grad3)
-    errs2, total2, grad2 = code(2, after(half2, grad3), other2)
-    peer2 = across(grad2)
-    keep3, send3 = term(grad3, after(peer3, grad2))
-    back3 = pieces(over_y, send3)
+    errs1, total1, grad1 = code(1, halves[4 * rows : 6 * rows], [after(others[4 * rows : 6 * rows], grad3)])
+    keep3, send3 = term(grad3, after(peer3, grad1, s_y1, s_q))
+    back3 = over_y(send3)
+    errs2, total2, grad2 = code(2, halves[6 * rows :], [after(others[6 * rows :], send3)])
+    peer1, peer2 = across(grad1), across(grad2)
     keep1, send1 = term(after(grad1, send3), peer1)
-    back1 = pieces(over_y, send1)
-    keep2, send2 = term(after(grad2, send1, back0), peer2)
+    back1 = over_y(send1)
+    keep2, send2 = term(after(grad2, send1), peer2)
     back2 = over_y(send2)
-    s_q = after(s_q, send2)
+    sum3 = after((keep3 + back3.astype(F32)).astype(BF), send1)
+    pair3 = over_pair(sum3)
+    s_q = after(s_q, sum3)
     s_y3 = over_y(s_q)
-    s_m = pack([s_m, s_y1], send2)
-    s_other1 = pieces(over_core, s_m)
-    sum3 = [after(part.astype(BF), send2) for part in plus(keep3, back3)]
-    pair3 = [over_pair(part) for part in sum3]
-    s_p = after(s_p, *sum3)
-    s_other2 = pieces(over_core, s_p)
-    srcs1, codes1 = pre(1, s_m, [after(s_other1[0], *sum3), s_other1[1]])
-    srcs2, codes2 = pre(2, s_p, s_other2)
-    far = [part.astype(BF) for part in plus(keep1, back1, pair3)]
-    far = [after(part, codes1, codes2) for part in far]
-    far_in = [over_mirror(part) for part in far]
-    sum2 = (keep2 + back2.astype(F32)).astype(BF)
+    s_mp = pack([s_m, s_y1, s_p, s_y2], sum3)
+    s_other = over_core(s_mp)
+    errs0, total0, grad0 = code(0, halves[: 2 * rows], [after(others[: 2 * rows], sum3)])
+    keep0, send0 = term(grad0, across(grad0))
+    back0 = over_y(send0)
+    far = pack([(keep1 + back1.astype(F32) + pair3.astype(F32)).astype(BF)], send2)
+    far_in = over_mirror(far)
+    srcs0, codes0 = pre(0, halves[2 * rows : 4 * rows], [after(others[2 * rows : 4 * rows], far)])
+    srcs1, codes1 = pre(1, s_mp[: 2 * rows], [after(s_other[: 2 * rows], far)])
+    srcs2, codes2 = pre(2, s_mp[2 * rows :], [after(s_other[2 * rows :], far)])
+    dec_part, enc_part = early_step(
+        (codes0, codes1, codes2), (errs0, errs1, errs2), (srcs0, srcs1, srcs2), (grad0, grad1, grad2)
+    )
+    sum2 = add(keep2, back2, BF, codes1)
     pair2 = over_pair(sum2)
-    s_q = pack([s_q, s_y3], *far)
-    srcs3, codes3 = pre(3, s_q, pieces(over_core, s_q))
-    code_grad = place_rows(
-        place, (total0, total1, total2, after(total3, *far)), rows
-    )
-    dec_grad, enc_grad, token = tokens_step(
-        (codes0, codes1, codes2, codes3),
-        (errs0, errs1, errs2, errs3),
-        (srcs0, srcs1, srcs2, srcs3),
-        (grad0, grad1, grad2, grad3),
-        far[1],
+    own = add(keep0, back0, F32, dec_part)
+    s_q = pack([s_q, s_y3], dec_part)
+    cuts = (0, 3 * rows // 4, 3 * rows // 2, 2 * rows)
+    q_other = [over_core(s_q[a:b]) for a, b in zip(cuts, cuts[1:])]
+    srcs3, codes3 = pre(3, s_q, q_other)
+    code_grad = place_rows(place, (total0, total1, total2, after(total3, dec_part)), rows)
+    dec_grad, enc_grad, token = late_step(
+        (codes3,), (errs3,), (srcs3,), (grad3,), dec_part, enc_part
     )
     input_grad = call(
-        finish_kernel, [like(x.shape, F32)], 0, keep0, back0, pair2, *far_in, token
+        finish_kernel, [like(x.shape, F32)], 0, own, pair2, far_in, token
     )[0]
     return code_grad, dec_grad[None], enc_grad, input_grad
 

time: 98.4 us -> 86.4 us (0.88)
  starting transfers between devices: 39.2 us -> 26.3 us
  Pallas kernels: 24.6 us -> 27.3 us
  waiting for transfers between devices: 30.8 us -> 29.2 us
    ppermute x51 -> x32, starting transfers between devices: 39.2 us -> 26.3 us  [swap(): return lax.ppermute(x, 'lat', pairs)]
    pallas_call x45 -> x41, Pallas kernels: 24.6 us -> 27.3 us  [call(): pl.pallas_call(kernel, out_shape=outs, in_specs=options.pop('in_specs', [...]
    ppermute x51 -> x32, waiting for transfers between devices: 30.8 us -> 29.2 us  [swap(): return lax.ppermute(x, 'lat', pairs)]
  transfers between devices with their start and end apart: 51 -> 32, of which waited for: 14 -> 13; matrix products, arithmetic and copies ran while one was open for 1% -> 1% of each run, Pallas kernels for 24% -> 29%
where the time goes in v3:
time: 86.4 us; the launch traced here: 86.2 us
  waiting for transfers between devices  29.2 us (34%)
  Pallas kernels  27.3 us (32%)
  starting transfers between devices  26.3 us (30%)
  local copies, waits for them, and re-layouts  2.14 us (2%)
  between operations  1.19 us (1%)
    ppermute x32, waiting for transfers between devices, swap(): return lax.ppermute(x, 'lat', pairs)  29.2 us
    pallas_call x41, Pallas kernels, call(): pl.pallas_call(kernel, out_shape=outs, in_specs=options.pop('in_specs', [...  27.3 us
    ppermute x32, starting transfers between devices, swap(): return lax.ppermute(x, 'lat', pairs)  26.3 us
  transfers between devices with their start and end apart: 32, of which 13 were waited for; matrix products, arithmetic and copies ran while one was open for 1% of the time, Pallas kernels for 29%

profile of v3, /device:TPU:0, one launch (start us, length us, event | category | flops | bytes accessed | tf_op | source)
XLA Modules:
  0.0 86.2 jit_solution(9594320605089311426)
XLA Ops:
  1.1 2.7 %collective-permute-start.2 = (bf16[64,1792]{1,0:T(8,128)(2,1)}, bf16[64,1792]{1,0:T(8,128)(2,1)S(1)}, u32[]{:S(2)}, u32[]{:S(2)}) collective-permute-start(bf16[64,1792]{1,0:T(8,128)(2,1)} %bitcast.24), channel_id=1, source_target_pairs={{0,4},{1,5},{2,6},{3,7},{4,0},{5,1},{6,2},{7,3},{8,12},{9,13},{10,... | collective-permute-start | bytes 688136 | tf_op jit(solution)/shard_map/ppermute | solution.py:46
  3.8 2.5 %collective-permute-start.1 = (bf16[64,1792]{1,0:T(8,128)(2,1)}, bf16[64,1792]{1,0:T(8,128)(2,1)S(1)}, u32[]{:S(2)}, u32[]{:S(2)}) collective-permute-start(bf16[64,1792]{1,0:T(8,128)(2,1)} %bitcast.25), channel_id=1, source_target_pairs={{0,12},{1,13},{2,14},{3,15},{4,8},{5,9},{6,10},{7,11},{8,4},{9,5},... | collective-permute-start | bytes 688136 | tf_op jit(solution)/shard_map/ppermute | solution.py:46
  6.3 1.5 %collective-permute-start = (bf16[64,1792]{1,0:T(8,128)(2,1)}, bf16[64,1792]{1,0:T(8,128)(2,1)S(1)}, u32[]{:S(2)}, u32[]{:S(2)}) collective-permute-start(bf16[64,1792]{1,0:T(8,128)(2,1)} %bitcast.26), channel_id=1, source_target_pairs={{0,2},{1,3},{2,0},{3,1},{4,6},{5,7},{6,4},{7,5},{8,10},{9,11},{10,... | collective-permute-start | bytes 688136 | tf_op jit(solution)/shard_map/ppermute | solution.py:46
  7.9 1.6 %copy-done.2 = s32[1024,512]{1,0:T(8,128)S(1)} copy-done((s32[1024,512]{1,0:T(8,128)S(1)}, s32[1024,512]{1,0:T(8,128)}, u32[]{:S(2)}) %copy-start.2) | copy-done | bytes 2097176
  9.5 3.6 %shard_map.93.refs_2_.refs_3_.refs_4_.refs_6_ = f32[1024,512]{1,0:T(8,128)S(1)} custom-call(s32[16]{0:T(128)S(1)} %stack.67.refs_0_, s32[1024,512]{1,0:T(8,128)S(1)} %copy-done.2), custom_call_target="tpu_custom_call" | custom-call | flops 1 | bytes 1 | tf_op jit(solution)/shard_map/pallas_call | solution.py:83
  13.1 4.3 %collective-permute-done.1.x = bf16[64,1792]{1,0:T(8,128)(2,1)S(1)} collective-permute-done((bf16[64,1792]{1,0:T(8,128)(2,1)}, bf16[64,1792]{1,0:T(8,128)(2,1)S(1)}, u32[]{:S(2)}, u32[]{:S(2)}) %collective-permute-start.1) | collective-permute-done | bytes 229408 | tf_op jit(solution)/shard_map/ppermute | solution.py:46
  17.5 1.6 %collective-permute-start.5 = (bf16[64,1792]{1,0:T(8,128)(2,1)S(1)}, bf16[64,1792]{1,0:T(8,128)(2,1)S(1)}, u32[]{:S(2)}, u32[]{:S(2)}) collective-permute-start(bf16[64,1792]{1,0:T(8,128)(2,1)S(1)} %shard_map.94.refs_0_.refs_1_), channel_id=1, source_target_pairs={{0,2},{1,3},{2,0},{3,1},{4,6},{5,7},{6,4},{7,5},{8,10},{9,11},{10,... | collective-permute-start | bytes 688136 | tf_op jit(solution)/shard_map/ppermute | solution.py:46
  20.2 2.6 %collective-permute-start.9 = (bf16[64,1792]{1,0:T(8,128)(2,1)S(1)}, bf16[64,1792]{1,0:T(8,128)(2,1)S(1)}, u32[]{:S(2)}, u32[]{:S(2)}) collective-permute-start(bf16[64,1792]{1,0:T(8,128)(2,1)S(1)} %shard_map.95.refs_2_), channel_id=1, source_target_pairs={{0,12},{1,13},{2,14},{3,15},{4,8},{5,9},{6,10},{7,11},{8,4},{9,5},... | collective-permute-start | bytes 688136 | tf_op jit(solution)/shard_map/ppermute | solution.py:46
  22.9 3.2 %collective-permute-done.5.refs_4_.refs_0_.refs_2_ = bf16[64,1792]{1,0:T(8,128)(2,1)S(1)} collective-permute-done((bf16[64,1792]{1,0:T(8,128)(2,1)S(1)}, bf16[64,1792]{1,0:T(8,128)(2,1)S(1)}, u32[]{:S(2)}, u32[]{:S(2)}) %collective-permute-start.5) | collective-permute-done | bytes 229408 | tf_op jit(solution)/shard_map/ppermute | solution.py:46
  26.1 1.6 %collective-permute-start.6 = (bf16[64,1792]{1,0:T(8,128)(2,1)S(1)}, bf16[64,1792]{1,0:T(8,128)(2,1)S(1)}, u32[]{:S(2)}, u32[]{:S(2)}) collective-permute-start(bf16[64,1792]{1,0:T(8,128)(2,1)S(1)} %shard_map.97), channel_id=1, source_target_pairs={{0,2},{1,3},{2,0},{3,1},{4,6},{5,7},{6,4},{7,5},{8,10},{9,11},{10,... | collective-permute-start | bytes 688136 | tf_op jit(solution)/shard_map/ppermute | solution.py:46
  27.7 3.7 %collective-permute-done.10.refs_2_ = bf16[64,1792]{1,0:T(8,128)(2,1)S(1)} collective-permute-done((bf16[64,1792]{1,0:T(8,128)(2,1)S(1)}, bf16[64,1792]{1,0:T(8,128)(2,1)S(1)}, u32[]{:S(2)}, u32[]{:S(2)}) %collective-permute-start.10) | collective-permute-done | bytes 229408 | tf_op jit(solution)/shard_map/ppermute | solution.py:46
  31.4 2.4 %collective-permute-done.9.refs_2_.x = bf16[64,1792]{1,0:T(8,128)(2,1)S(1)} collective-permute-done((bf16[64,1792]{1,0:T(8,128)(2,1)S(1)}, bf16[64,1792]{1,0:T(8,128)(2,1)S(1)}, u32[]{:S(2)}, u32[]{:S(2)}) %collective-permute-start.9) | collective-permute-done | bytes 229408 | tf_op jit(solution)/shard_map/ppermute | solution.py:46
  33.8 3.7 %collective-permute-done.7.refs_0_ = bf16[64,1792]{1,0:T(8,128)(2,1)S(1)} collective-permute-done((bf16[64,1792]{1,0:T(8,128)(2,1)S(1)}, bf16[64,1792]{1,0:T(8,128)(2,1)S(1)}, u32[]{:S(2)}, u32[]{:S(2)}) %collective-permute-start.7) | collective-permute-done | bytes 229408 | tf_op jit(solution)/shard_map/ppermute | solution.py:46
  37.5 1.9 %collective-permute-done.11.refs_3_ = bf16[64,1792]{1,0:T(8,128)(2,1)S(1)} collective-permute-done((bf16[64,1792]{1,0:T(8,128)(2,1)S(1)}, bf16[64,1792]{1,0:T(8,128)(2,1)S(1)}, u32[]{:S(2)}, u32[]{:S(2)}) %collective-permute-start.11) | collective-permute-done | bytes 229408 | tf_op jit(solution)/shard_map/ppermute | solution.py:46
  39.4 1.3 %collective-permute-done.8.refs_1_ = bf16[64,1792]{1,0:T(8,128)(2,1)S(1)} collective-permute-done((bf16[64,1792]{1,0:T(8,128)(2,1)S(1)}, bf16[64,1792]{1,0:T(8,128)(2,1)S(1)}, u32[]{:S(2)}, u32[]{:S(2)}) %collective-permute-start.8) | collective-permute-done | bytes 229408 | tf_op jit(solution)/shard_map/ppermute | solution.py:46
  42.0 3.4 %collective-permute-done.13.refs_1_ = bf16[128,1792]{1,0:T(8,128)(2,1)S(1)} collective-permute-done((bf16[128,1792]{1,0:T(8,128)(2,1)S(1)}, bf16[128,1792]{1,0:T(8,128)(2,1)S(1)}, u32[]{:S(2)}, u32[]{:S(2)}) %collective-permute-start.13) | collective-permute-done | bytes 458784 | tf_op jit(solution)/shard_map/ppermute | solution.py:46
  46.5 0.7 shard_map.102
  47.2 1.9 %collective-permute-done.16.refs_2_.x = bf16[64,1792]{1,0:T(8,128)(2,1)S(1)} collective-permute-done((bf16[64,1792]{1,0:T(8,128)(2,1)S(1)}, bf16[64,1792]{1,0:T(8,128)(2,1)S(1)}, u32[]{:S(2)}, u32[]{:S(2)}) %collective-permute-start.16) | collective-permute-done | bytes 229408 | tf_op jit(solution)/shard_map/ppermute | solution.py:46
  49.2 1.3 %shard_map.105 = (f32[64,1792]{1,0:T(8,128)S(1)}, bf16[64,1792]{1,0:T(8,128)(2,1)S(1)}) custom-call(bf16[256,512]{1,0:T(8,128)(2,1)S(1)} %get-tuple-element.37.refs_0_.grad.refs_3_, bf16[128,512]{1,0:T(8,128)(2,1)S(1)} %shard_map.104.peer, bf16[1792,512]{1,0:T(8,128)(2,1)S(1)} %copy-done, bf16[1792,512]{1,0:T(8,128)(2,1)S(1)} %collective-permute-done.3.refs_3_.weight_peer), custom_call_target="tpu_custom_call" | custom-call | flops 1 | bytes 1 | tf_op jit(solution)/shard_map/pallas_call | solution.py:83
  52.5 1.3 %shard_map.107 = (f32[64,1792]{1,0:T(8,128)S(1)}, bf16[64,1792]{1,0:T(8,128)(2,1)S(1)}) custom-call(bf16[256,512]{1,0:T(8,128)(2,1)S(1)} %shard_map.106.grad, bf16[128,512]{1,0:T(8,128)(2,1)S(1)} %collective-permute-done.18.peer, bf16[1792,512]{1,0:T(8,128)(2,1)S(1)} %copy-done, bf16[1792,512]{1,0:T(8,128)(2,1)S(1)} %collective-permute-done.3.refs_3_.weight_peer), custom_call_target="tpu_custom_call" | custom-call | flops 1 | bytes 1 | tf_op jit(solution)/shard_map/pallas_call | solution.py:83
  53.8 1.6 %collective-permute-start.19 = (bf16[64,1792]{1,0:T(8,128)(2,1)S(1)}, bf16[64,1792]{1,0:T(8,128)(2,1)S(1)}, u32[]{:S(2)}, u32[]{:S(2)}) collective-permute-start(bf16[64,1792]{1,0:T(8,128)(2,1)S(1)} %get-tuple-element.41.refs_0_), channel_id=1, source_target_pairs={{0,2},{1,3},{2,0},{3,1},{4,6},{5,7},{6,4},{7,5},{8,10},{9,11},{10,... | collective-permute-start | bytes 688136 | tf_op jit(solution)/shard_map/ppermute | solution.py:46
  55.4 1.3 %shard_map.114 = (f32[64,1792]{1,0:T(8,128)S(1)}, bf16[64,1792]{1,0:T(8,128)(2,1)S(1)}) custom-call(bf16[256,512]{1,0:T(8,128)(2,1)S(1)} %shard_map.113.grad, bf16[128,512]{1,0:T(8,128)(2,1)S(1)} %collective-permute-done.21.peer, bf16[1792,512]{1,0:T(8,128)(2,1)S(1)} %copy-done, bf16[1792,512]{1,0:T(8,128)(2,1)S(1)} %collective-permute-done.3.refs_3_.weight_peer), custom_call_target="tpu_custom_call" | custom-call | flops 1 | bytes 1 | tf_op jit(solution)/shard_map/pallas_call | solution.py:83
  56.7 2.0 %collective-permute-done.17 = bf16[64,1792]{1,0:T(8,128)(2,1)S(1)} collective-permute-done((bf16[64,1792]{1,0:T(8,128)(2,1)S(1)}, bf16[64,1792]{1,0:T(8,128)(2,1)S(1)}, u32[]{:S(2)}, u32[]{:S(2)}) %collective-permute-start.17) | collective-permute-done | bytes 229408 | tf_op jit(solution)/shard_map/ppermute | solution.py:46
  58.9 1.2 %collective-permute-start.20 = (bf16[64,1792]{1,0:T(8,128)(2,1)S(1)}, bf16[64,1792]{1,0:T(8,128)(2,1)S(1)}, u32[]{:S(2)}, u32[]{:S(2)}) collective-permute-start(bf16[64,1792]{1,0:T(8,128)(2,1)S(1)} %shard_map.108.refs_0_.refs_4_), channel_id=1, source_target_pairs={{0,4},{1,5},{2,6},{3,7},{4,0},{5,1},{6,2},{7,3},{8,12},{9,13},{10,... | collective-permute-start | bytes 688136 | tf_op jit(solution)/shard_map/ppermute | solution.py:46
  62.3 2.0 %collective-permute-start.23 = (bf16[64,1792]{1,0:T(8,128)(2,1)S(1)}, bf16[64,1792]{1,0:T(8,128)(2,1)S(1)}, u32[]{:S(2)}, u32[]{:S(2)}) collective-permute-start(bf16[64,1792]{1,0:T(8,128)(2,1)S(1)} %shard_map.126.refs_0_), channel_id=1, source_target_pairs={{0,2},{1,3},{2,0},{3,1},{4,6},{5,7},{6,4},{7,5},{8,10},{9,11},{10,... | collective-permute-start | bytes 688136 | tf_op jit(solution)/shard_map/ppermute | solution.py:46
  64.3 1.3 %shard_map.130 = (f32[64,1792]{1,0:T(8,128)S(1)}, bf16[64,1792]{1,0:T(8,128)(2,1)S(1)}) custom-call(bf16[256,512]{1,0:T(8,128)(2,1)S(1)} %get-tuple-element.58.refs_9_.grad, bf16[128,512]{1,0:T(8,128)(2,1)S(1)} %collective-permute-done.27.peer, bf16[1792,512]{1,0:T(8,128)(2,1)S(1)} %copy-done, bf16[1792,512]{1,0:T(8,128)(2,1)S(1)} %collective-permute-done.3.refs_3_.weight_peer), custom_call_target="tpu_custom_call" | custom-call | flops 1 | bytes 1 | tf_op jit(solution)/shard_map/pallas_call | solution.py:83
  65.7 1.4 %collective-permute-start.28 = (bf16[64,1792]{1,0:T(8,128)(2,1)S(1)}, bf16[64,1792]{1,0:T(8,128)(2,1)S(1)}, u32[]{:S(2)}, u32[]{:S(2)}) collective-permute-start(bf16[64,1792]{1,0:T(8,128)(2,1)S(1)} %get-tuple-element.67), channel_id=1, source_target_pairs={{0,2},{1,3},{2,0},{3,1},{4,6},{5,7},{6,4},{7,5},{8,10},{9,11},{10,... | collective-permute-start | bytes 688136 | tf_op jit(solution)/shard_map/ppermute | solution.py:46
  67.1 2.2 %collective-permute-start.31 = (bf16[64,1792]{1,0:T(8,128)(2,1)S(1)}, bf16[64,1792]{1,0:T(8,128)(2,1)S(1)}, u32[]{:S(2)}, u32[]{:S(2)}) collective-permute-start(bf16[64,1792]{1,0:T(8,128)(2,1)S(1)} %shard_map.115.refs_0_), channel_id=1, source_target_pairs={{0,12},{1,13},{2,14},{3,15},{4,8},{5,9},{6,10},{7,11},{8,4},{9,5},... | collective-permute-start | bytes 688136 | tf_op jit(solution)/shard_map/ppermute | solution.py:46
  71.6 4.4 %shard_map.123 = (f32[512,1792]{1,0:T(8,128)S(1)}, f32[1792,512]{1,0:T(8,128)S(1)}) custom-call(bf16[256,512]{1,0:T(8,128)(2,1)S(1)} %get-tuple-element.49.refs_0_, bf16[256,512]{1,0:T(8,128)(2,1)S(1)} %get-tuple-element.50.refs_1_.refs_0_, bf16[256,512]{1,0:T(8,128)(2,1)S(1)} %get-tuple-element.51.refs_2_, bf16[256,1792]{1,0:T(8,128)(2,1)S(1)} %get-tuple-element.52.refs_3_, ...), custom_call_target="tpu_custom_call" | custom-call | flops 1 | bytes 1 | tf_op jit(solution)/shard_map/pallas_call | solution.py:83
  77.4 2.0 %shard_map.125 = f32[1024,512]{1,0:T(8,128)} custom-call(s32[16]{0:T(128)S(1)} %stack.67.refs_0_, f32[256,512]{1,0:T(8,128)S(1)} %get-tuple-element.42.refs_1_, f32[256,512]{1,0:T(8,128)S(1)} %get-tuple-element.43.refs_2_, f32[256,512]{1,0:T(8,128)S(1)} %get-tuple-element.44.refs_3_, f32[256,512]{1,0:T(8,128)S(1)} %shard_map.124.refs_4_), custom_call_target="tpu_custom_call" | custom-call | flops 1 | bytes 1 | tf_op jit(solution)/shard_map/pallas_call | solution.py:83
  80.1 5.3 %shard_map.129 = (f32[512,1792]{1,0:T(8,128)}, f32[1792,512]{1,0:T(8,128)}, f32[8,128]{1,0:T(8,128)S(1)}) custom-call(bf16[256,512]{1,0:T(8,128)(2,1)S(1)} %get-tuple-element.60.refs_0_, bf16[256,1792]{1,0:T(8,128)(2,1)S(1)} %get-tuple-element.61.refs_1_, bf16[256,1792]{1,0:T(8,128)(2,1)S(1)} %get-tuple-element.62.refs_2_, ...), custom_call_target="tpu_custom_call" | custom-call | flops 1 | bytes 1 | tf_op jit(solution)/shard_map/pallas_call | solution.py:83
  85.4 0.8 shard_map.133
  (98 shorter events, 12.9 us)
Async XLA Ops:
  0.6 16.8 %collective-permute-start.3 = (bf16[1792,512]{1,0:T(8,128)(2,1)}, bf16[1792,512]{1,0:T(8,128)(2,1)S(1)}, u32[]{:S(2)}, u32[]{:S(2)}) collective-permute-start(bf16[1792,512]{1,0:T(8,128)(2,1)} %weight.7), channel_id=1, source_target_pairs={{0,1},{1,0},{2,3},{3,2},{4,5},{5,4},{6,7},{7,6},{8,9},{9,8},{10,11... | collective-permute-start | bytes 5505032 | tf_op jit(solution)/shard_map/ppermute | solution.py:46
  1.1 11.9 %collective-permute-start.2 = (bf16[64,1792]{1,0:T(8,128)(2,1)}, bf16[64,1792]{1,0:T(8,128)(2,1)S(1)}, u32[]{:S(2)}, u32[]{:S(2)}) collective-permute-start(bf16[64,1792]{1,0:T(8,128)(2,1)} %bitcast.24), channel_id=1, source_target_pairs={{0,4},{1,5},{2,6},{3,7},{4,0},{5,1},{6,2},{7,3},{8,12},{9,13},{10,... | collective-permute-start | bytes 688136 | tf_op jit(solution)/shard_map/ppermute | solution.py:46
  3.8 13.6 %collective-permute-start.1 = (bf16[64,1792]{1,0:T(8,128)(2,1)}, bf16[64,1792]{1,0:T(8,128)(2,1)S(1)}, u32[]{:S(2)}, u32[]{:S(2)}) collective-permute-start(bf16[64,1792]{1,0:T(8,128)(2,1)} %bitcast.25), channel_id=1, source_target_pairs={{0,12},{1,13},{2,14},{3,15},{4,8},{5,9},{6,10},{7,11},{8,4},{9,5},... | collective-permute-start | bytes 688136 | tf_op jit(solution)/shard_map/ppermute | solution.py:46
  6.3 11.2 %collective-permute-start = (bf16[64,1792]{1,0:T(8,128)(2,1)}, bf16[64,1792]{1,0:T(8,128)(2,1)S(1)}, u32[]{:S(2)}, u32[]{:S(2)}) collective-permute-start(bf16[64,1792]{1,0:T(8,128)(2,1)} %bitcast.26), channel_id=1, source_target_pairs={{0,2},{1,3},{2,0},{3,1},{4,6},{5,7},{6,4},{7,5},{8,10},{9,11},{10,... | collective-permute-start | bytes 688136 | tf_op jit(solution)/shard_map/ppermute | solution.py:46
  17.5 8.6 %collective-permute-start.5 = (bf16[64,1792]{1,0:T(8,128)(2,1)S(1)}, bf16[64,1792]{1,0:T(8,128)(2,1)S(1)}, u32[]{:S(2)}, u32[]{:S(2)}) collective-permute-start(bf16[64,1792]{1,0:T(8,128)(2,1)S(1)} %shard_map.94.refs_0_.refs_1_), channel_id=1, source_target_pairs={{0,2},{1,3},{2,0},{3,1},{4,6},{5,7},{6,4},{7,5},{8,10},{9,11},{10,... | collective-permute-start | bytes 688136 | tf_op jit(solution)/shard_map/ppermute | solution.py:46
  19.1 12.3 %collective-permute-start.10 = (bf16[64,1792]{1,0:T(8,128)(2,1)S(1)}, bf16[64,1792]{1,0:T(8,128)(2,1)S(1)}, u32[]{:S(2)}, u32[]{:S(2)}) collective-permute-start(bf16[64,1792]{1,0:T(8,128)(2,1)S(1)} %shard_map.95.refs_2_), channel_id=1, source_target_pairs={{0,4},{1,5},{2,6},{3,7},{4,0},{5,1},{6,2},{7,3},{8,12},{9,13},{10,... | collective-permute-start | bytes 688136 | tf_op jit(solution)/shard_map/ppermute | solution.py:46
  19.7 11.6 %collective-permute-start.4 = (bf16[64,1792]{1,0:T(8,128)(2,1)S(1)}, bf16[64,1792]{1,0:T(8,128)(2,1)S(1)}, u32[]{:S(2)}, u32[]{:S(2)}) collective-permute-start(bf16[64,1792]{1,0:T(8,128)(2,1)S(1)} %copy-done.3), channel_id=1, source_target_pairs={{0,2},{1,3},{2,0},{3,1},{4,6},{5,7},{6,4},{7,5},{8,10},{9,11},{10,... | collective-permute-start | bytes 688136 | tf_op jit(solution)/shard_map/ppermute | solution.py:46
  20.2 13.6 %collective-permute-start.9 = (bf16[64,1792]{1,0:T(8,128)(2,1)S(1)}, bf16[64,1792]{1,0:T(8,128)(2,1)S(1)}, u32[]{:S(2)}, u32[]{:S(2)}) collective-permute-start(bf16[64,1792]{1,0:T(8,128)(2,1)S(1)} %shard_map.95.refs_2_), channel_id=1, source_target_pairs={{0,12},{1,13},{2,14},{3,15},{4,8},{5,9},{6,10},{7,11},{8,4},{9,5},... | collective-permute-start | bytes 688136 | tf_op jit(solution)/shard_map/ppermute | solution.py:46
  22.9 14.6 %collective-permute-start.7 = (bf16[64,1792]{1,0:T(8,128)(2,1)S(1)}, bf16[64,1792]{1,0:T(8,128)(2,1)S(1)}, u32[]{:S(2)}, u32[]{:S(2)}) collective-permute-start(bf16[64,1792]{1,0:T(8,128)(2,1)S(1)} %shard_map.94.refs_0_.refs_1_), channel_id=1, source_target_pairs={{0,4},{1,5},{2,6},{3,7},{4,0},{5,1},{6,2},{7,3},{8,12},{9,13},{10,... | collective-permute-start | bytes 688136 | tf_op jit(solution)/shard_map/ppermute | solution.py:46
  26.1 13.3 %collective-permute-start.6 = (bf16[64,1792]{1,0:T(8,128)(2,1)S(1)}, bf16[64,1792]{1,0:T(8,128)(2,1)S(1)}, u32[]{:S(2)}, u32[]{:S(2)}) collective-permute-start(bf16[64,1792]{1,0:T(8,128)(2,1)S(1)} %shard_map.97), channel_id=1, source_target_pairs={{0,2},{1,3},{2,0},{3,1},{4,6},{5,7},{6,4},{7,5},{8,10},{9,11},{10,... | collective-permute-start | bytes 688136 | tf_op jit(solution)/shard_map/ppermute | solution.py:46
  31.4 8.0 %collective-permute-start.11 = (bf16[64,1792]{1,0:T(8,128)(2,1)S(1)}, bf16[64,1792]{1,0:T(8,128)(2,1)S(1)}, u32[]{:S(2)}, u32[]{:S(2)}) collective-permute-start(bf16[64,1792]{1,0:T(8,128)(2,1)S(1)} %collective-permute-done.10.refs_2_), channel_id=1, source_target_pairs={{0,2},{1,3},{2,0},{3,1},{4,6},{5,7},{6,4},{7,5},{8,10},{9,11},{10,... | collective-permute-start | bytes 688136 | tf_op jit(solution)/shard_map/ppermute | solution.py:46
  31.4 9.4 %collective-permute-start.8 = (bf16[64,1792]{1,0:T(8,128)(2,1)S(1)}, bf16[64,1792]{1,0:T(8,128)(2,1)S(1)}, u32[]{:S(2)}, u32[]{:S(2)}) collective-permute-start(bf16[64,1792]{1,0:T(8,128)(2,1)S(1)} %collective-permute-done.5.refs_4_.refs_0_.refs_2_), channel_id=1, source_target_pairs={{0,4},{1,5},{2,6},{3,7},{4,0},{5,1},{6,2},{7,3},{8,12},{9,13},{10,... | collective-permute-start | bytes 688136 | tf_op jit(solution)/shard_map/ppermute | solution.py:46
  40.9 5.4 %collective-permute-start.12 = (bf16[512,1792]{1,0:T(8,128)(2,1)S(1)}, bf16[512,1792]{1,0:T(8,128)(2,1)S(1)}, u32[]{:S(2)}, u32[]{:S(2)}) collective-permute-start(bf16[512,1792]{1,0:T(8,128)(2,1)S(1)} %shard_map.99), channel_id=1, source_target_pairs={{0,1},{1,0},{2,3},{3,2},{4,5},{5,4},{6,7},{7,6},{8,9},{9,8},{10,11... | collective-permute-start | bytes 5505032 | tf_op jit(solution)/shard_map/ppermute | solution.py:46
  41.0 8.1 %collective-permute-start.16 = (bf16[64,1792]{1,0:T(8,128)(2,1)S(1)}, bf16[64,1792]{1,0:T(8,128)(2,1)S(1)}, u32[]{:S(2)}, u32[]{:S(2)}) collective-permute-start(bf16[64,1792]{1,0:T(8,128)(2,1)S(1)} %shard_map.103.refs_0_), channel_id=1, source_target_pairs={{0,4},{1,5},{2,6},{3,7},{4,0},{5,1},{6,2},{7,3},{8,12},{9,13},{10,... | collective-permute-start | bytes 688136 | tf_op jit(solution)/shard_map/ppermute | solution.py:46
  41.3 7.8 %collective-permute-start.15 = (bf16[64,1792]{1,0:T(8,128)(2,1)S(1)}, bf16[64,1792]{1,0:T(8,128)(2,1)S(1)}, u32[]{:S(2)}, u32[]{:S(2)}) collective-permute-start(bf16[64,1792]{1,0:T(8,128)(2,1)S(1)} %shard_map.103.refs_0_), channel_id=1, source_target_pairs={{0,2},{1,3},{2,0},{3,1},{4,6},{5,7},{6,4},{7,5},{8,10},{9,11},{10,... | collective-permute-start | bytes 688136 | tf_op jit(solution)/shard_map/ppermute | solution.py:46
  41.9 3.5 %collective-permute-start.13 = (bf16[128,1792]{1,0:T(8,128)(2,1)S(1)}, bf16[128,1792]{1,0:T(8,128)(2,1)S(1)}, u32[]{:S(2)}, u32[]{:S(2)}) collective-permute-start(bf16[128,1792]{1,0:T(8,128)(2,1)S(1)} %shard_map.98.refs_5_.refs_0_), channel_id=1, source_target_pairs={{0,1},{1,0},{2,3},{3,2},{4,5},{5,4},{6,7},{7,6},{8,9},{9,8},{10,11... | collective-permute-start | bytes 1376264 | tf_op jit(solution)/shard_map/ppermute | solution.py:46
  46.1 3.0 %collective-permute-start.14 = (bf16[128,512]{1,0:T(8,128)(2,1)S(1)}, bf16[128,512]{1,0:T(8,128)(2,1)S(1)}, u32[]{:S(2)}, u32[]{:S(2)}) collective-permute-start(bf16[128,512]{1,0:T(8,128)(2,1)S(1)} %slice.59), channel_id=1, source_target_pairs={{0,1},{1,0},{2,3},{3,2},{4,5},{5,4},{6,7},{7,6},{8,9},{9,8},{10,11... | collective-permute-start | bytes 393224 | tf_op jit(solution)/shard_map/ppermute | solution.py:46
  50.5 8.2 %collective-permute-start.17 = (bf16[64,1792]{1,0:T(8,128)(2,1)S(1)}, bf16[64,1792]{1,0:T(8,128)(2,1)S(1)}, u32[]{:S(2)}, u32[]{:S(2)}) collective-permute-start(bf16[64,1792]{1,0:T(8,128)(2,1)S(1)} %get-tuple-element.40.refs_0_), channel_id=1, source_target_pairs={{0,2},{1,3},{2,0},{3,1},{4,6},{5,7},{6,4},{7,5},{8,10},{9,11},{10,... | collective-permute-start | bytes 688136 | tf_op jit(solution)/shard_map/ppermute | solution.py:46
  51.1 1.4 %collective-permute-start.18 = (bf16[128,512]{1,0:T(8,128)(2,1)S(1)}, bf16[128,512]{1,0:T(8,128)(2,1)S(1)}, u32[]{:S(2)}, u32[]{:S(2)}) collective-permute-start(bf16[128,512]{1,0:T(8,128)(2,1)S(1)} %slice.62), channel_id=1, source_target_pairs={{0,1},{1,0},{2,3},{3,2},{4,5},{5,4},{6,7},{7,6},{8,9},{9,8},{10,11... | collective-permute-start | bytes 393224 | tf_op jit(solution)/shard_map/ppermute | solution.py:46
  51.9 3.5 %collective-permute-start.21 = (bf16[128,512]{1,0:T(8,128)(2,1)S(1)}, bf16[128,512]{1,0:T(8,128)(2,1)S(1)}, u32[]{:S(2)}, u32[]{:S(2)}) collective-permute-start(bf16[128,512]{1,0:T(8,128)(2,1)S(1)} %slice.67), channel_id=1, source_target_pairs={{0,1},{1,0},{2,3},{3,2},{4,5},{5,4},{6,7},{7,6},{8,9},{9,8},{10,11... | collective-permute-start | bytes 393224 | tf_op jit(solution)/shard_map/ppermute | solution.py:46
  53.8 11.8 %collective-permute-start.19 = (bf16[64,1792]{1,0:T(8,128)(2,1)S(1)}, bf16[64,1792]{1,0:T(8,128)(2,1)S(1)}, u32[]{:S(2)}, u32[]{:S(2)}) collective-permute-start(bf16[64,1792]{1,0:T(8,128)(2,1)S(1)} %get-tuple-element.41.refs_0_), channel_id=1, source_target_pairs={{0,2},{1,3},{2,0},{3,1},{4,6},{5,7},{6,4},{7,5},{8,10},{9,11},{10,... | collective-permute-start | bytes 688136 | tf_op jit(solution)/shard_map/ppermute | solution.py:46
  58.8 12.1 %collective-permute-start.29 = (bf16[64,1792]{1,0:T(8,128)(2,1)S(1)}, bf16[64,1792]{1,0:T(8,128)(2,1)S(1)}, u32[]{:S(2)}, u32[]{:S(2)}) collective-permute-start(bf16[64,1792]{1,0:T(8,128)(2,1)S(1)} %get-tuple-element.48.refs_1_), channel_id=1, source_target_pairs={{0,2},{1,3},{2,0},{3,1},{4,6},{5,7},{6,4},{7,5},{8,10},{9,11},{10,... | collective-permute-start | bytes 688136 | tf_op jit(solution)/shard_map/ppermute | solution.py:46
  58.9 6.7 %collective-permute-start.20 = (bf16[64,1792]{1,0:T(8,128)(2,1)S(1)}, bf16[64,1792]{1,0:T(8,128)(2,1)S(1)}, u32[]{:S(2)}, u32[]{:S(2)}) collective-permute-start(bf16[64,1792]{1,0:T(8,128)(2,1)S(1)} %shard_map.108.refs_0_.refs_4_), channel_id=1, source_target_pairs={{0,4},{1,5},{2,6},{3,7},{4,0},{5,1},{6,2},{7,3},{8,12},{9,13},{10,... | collective-permute-start | bytes 688136 | tf_op jit(solution)/shard_map/ppermute | solution.py:46
  60.8 1.4 %collective-permute-start.27 = (bf16[128,512]{1,0:T(8,128)(2,1)S(1)}, bf16[128,512]{1,0:T(8,128)(2,1)S(1)}, u32[]{:S(2)}, u32[]{:S(2)}) collective-permute-start(bf16[128,512]{1,0:T(8,128)(2,1)S(1)} %slice.75), channel_id=1, source_target_pairs={{0,1},{1,0},{2,3},{3,2},{4,5},{5,4},{6,7},{7,6},{8,9},{9,8},{10,11... | collective-permute-start | bytes 393224 | tf_op jit(solution)/shard_map/ppermute | solution.py:46
  61.0 9.0 %collective-permute-start.22 = (bf16[256,1792]{1,0:T(8,128)(2,1)S(1)}, bf16[256,1792]{1,0:T(8,128)(2,1)S(1)}, u32[]{:S(2)}, u32[]{:S(2)}) collective-permute-start(bf16[256,1792]{1,0:T(8,128)(2,1)S(1)} %shard_map.118), channel_id=1, source_target_pairs={{0,1},{1,0},{2,3},{3,2},{4,5},{5,4},{6,7},{7,6},{8,9},{9,8},{10,11... | collective-permute-start | bytes 2752520 | tf_op jit(solution)/shard_map/ppermute | solution.py:46
  62.3 13.8 %collective-permute-start.23 = (bf16[64,1792]{1,0:T(8,128)(2,1)S(1)}, bf16[64,1792]{1,0:T(8,128)(2,1)S(1)}, u32[]{:S(2)}, u32[]{:S(2)}) collective-permute-start(bf16[64,1792]{1,0:T(8,128)(2,1)S(1)} %shard_map.126.refs_0_), channel_id=1, source_target_pairs={{0,2},{1,3},{2,0},{3,1},{4,6},{5,7},{6,4},{7,5},{8,10},{9,11},{10,... | collective-permute-start | bytes 688136 | tf_op jit(solution)/shard_map/ppermute | solution.py:46
  65.7 11.7 %collective-permute-start.28 = (bf16[64,1792]{1,0:T(8,128)(2,1)S(1)}, bf16[64,1792]{1,0:T(8,128)(2,1)S(1)}, u32[]{:S(2)}, u32[]{:S(2)}) collective-permute-start(bf16[64,1792]{1,0:T(8,128)(2,1)S(1)} %get-tuple-element.67), channel_id=1, source_target_pairs={{0,2},{1,3},{2,0},{3,1},{4,6},{5,7},{6,4},{7,5},{8,10},{9,11},{10,... | collective-permute-start | bytes 688136 | tf_op jit(solution)/shard_map/ppermute | solution.py:46
  67.1 18.3 %collective-permute-start.31 = (bf16[64,1792]{1,0:T(8,128)(2,1)S(1)}, bf16[64,1792]{1,0:T(8,128)(2,1)S(1)}, u32[]{:S(2)}, u32[]{:S(2)}) collective-permute-start(bf16[64,1792]{1,0:T(8,128)(2,1)S(1)} %shard_map.115.refs_0_), channel_id=1, source_target_pairs={{0,12},{1,13},{2,14},{3,15},{4,8},{5,9},{6,10},{7,11},{8,4},{9,5},... | collective-permute-start | bytes 688136 | tf_op jit(solution)/shard_map/ppermute | solution.py:46
  70.9 14.5 %collective-permute-start.30 = (bf16[64,1792]{1,0:T(8,128)(2,1)S(1)}, bf16[64,1792]{1,0:T(8,128)(2,1)S(1)}, u32[]{:S(2)}, u32[]{:S(2)}) collective-permute-start(bf16[64,1792]{1,0:T(8,128)(2,1)S(1)} %shard_map.132), channel_id=1, source_target_pairs={{0,4},{1,5},{2,6},{3,7},{4,0},{5,1},{6,2},{7,3},{8,12},{9,13},{10,... | collective-permute-start | bytes 688136 | tf_op jit(solution)/shard_map/ppermute | solution.py:46
  76.1 3.4 %collective-permute-start.25 = (bf16[48,1792]{1,0:T(8,128)(2,1)S(1)}, bf16[48,1792]{1,0:T(8,128)(2,1)S(1)}, u32[]{:S(2)}, u32[]{:S(2)}) collective-permute-start(bf16[48,1792]{1,0:T(8,128)(2,1)S(1)} %get-tuple-element.82), channel_id=1, source_target_pairs={{0,1},{1,0},{2,3},{3,2},{4,5},{5,4},{6,7},{7,6},{8,9},{9,8},{10,11... | collective-permute-start | bytes 516104 | tf_op jit(solution)/shard_map/ppermute | solution.py:46
  76.2 3.3 %collective-permute-start.24 = (bf16[48,1792]{1,0:T(8,128)(2,1)S(1)}, bf16[48,1792]{1,0:T(8,128)(2,1)S(1)}, u32[]{:S(2)}, u32[]{:S(2)}) collective-permute-start(bf16[48,1792]{1,0:T(8,128)(2,1)S(1)} %get-tuple-element.83), channel_id=1, source_target_pairs={{0,1},{1,0},{2,3},{3,2},{4,5},{5,4},{6,7},{7,6},{8,9},{9,8},{10,11... | collective-permute-start | bytes 516104 | tf_op jit(solution)/shard_map/ppermute | solution.py:46
  77.3 2.1 %collective-permute-start.26 = (bf16[32,1792]{1,0:T(8,128)(2,1)S(1)}, bf16[32,1792]{1,0:T(8,128)(2,1)S(1)}, u32[]{:S(2)}, u32[]{:S(2)}) collective-permute-start(bf16[32,1792]{1,0:T(8,128)(2,1)S(1)} %slice.90), channel_id=1, source_target_pairs={{0,1},{1,0},{2,3},{3,2},{4,5},{5,4},{6,7},{7,6},{8,9},{9,8},{10,11... | collective-permute-start | bytes 344072 | tf_op jit(solution)/shard_map/ppermute | solution.py:46
  (6 other events, 36.8 us)

commit v4 on v3

--- a/solution.py
+++ b/solution.py
@@ -232,7 +232,7 @@
     count = (len(refs) - 3) // 4
     codes, errs, srcs, grads = (refs[count * k : count * (k + 1)] for k in range(4))
     dec_grad, enc_grad, turned = refs[4 * count :]
-    n, tile = codes[0].shape[0], 256
+    n, tile = codes[0].shape[0], 896
     for j in range(count):
         turned[:, j * n : (j + 1) * n] = codes[j][...].T
 
@@ -381,20 +381,20 @@
     m = after(m, y0, p, flags, weight_peer)
     y1, q = over_y(m), over_pair(m)
     s = after(s, m)
-    s_p, s_m = over_pair(s), over_mirror(s)
+    s_m = over_mirror(s)
     q1, y2 = over_pair(y1), over_y(after(p, y1))
-    s_y2 = over_y(s_p)
-    half0 = pack([x, y0, s, s_y0], y1)
-    half3 = pack([q, q1], s_m, s_y2, y2)
+    s_p = over_pair(after(s, y1))
+    half3 = pack([q, q1], s_m, y2)
     other3 = over_core(half3)
-    halves = pack([half0, m, y1, p, y2], half3)
+    halves = pack([x, y0, s, s_y0, m, y1, p, y2], half3)
     others = over_core(halves)
     s_m = after(s_m, half3)
-    s_y1, s_q = over_y(s_m), over_pair(s_m)
+    s_y1 = over_y(s_m)
+    s_q, s_p1 = over_pair(s_m), over_pair(after(s_y0, half3))
     errs3, total3, grad3 = code(3, half3, [other3])
     peer3 = across(grad3)
     errs1, total1, grad1 = code(1, halves[4 * rows : 6 * rows], [after(others[4 * rows : 6 * rows], grad3)])
-    keep3, send3 = term(grad3, after(peer3, grad1, s_y1, s_q))
+    keep3, send3 = term(grad3, after(peer3, grad1, s_y1, s_p))
     back3 = over_y(send3)
     errs2, total2, grad2 = code(2, halves[6 * rows :], [after(others[6 * rows :], send3)])
     peer1, peer2 = across(grad1), across(grad2)
@@ -402,22 +402,22 @@
     back1 = over_y(send1)
     keep2, send2 = term(after(grad2, send1), peer2)
     back2 = over_y(send2)
-    sum3 = after((keep3 + back3.astype(F32)).astype(BF), send1)
+    sum3 = after((keep3 + back3.astype(F32)).astype(BF), send1, s_q)
     pair3 = over_pair(sum3)
     s_q = after(s_q, sum3)
     s_y3 = over_y(s_q)
-    s_mp = pack([s_m, s_y1, s_p, s_y2], sum3)
+    s_mp = pack([s_m, s_y1, s_p, s_p1], sum3)
     s_other = over_core(s_mp)
     errs0, total0, grad0 = code(0, halves[: 2 * rows], [after(others[: 2 * rows], sum3)])
     keep0, send0 = term(grad0, across(grad0))
     back0 = over_y(send0)
     far = pack([(keep1 + back1.astype(F32) + pair3.astype(F32)).astype(BF)], send2)
     far_in = over_mirror(far)
-    srcs0, codes0 = pre(0, halves[2 * rows : 4 * rows], [after(others[2 * rows : 4 * rows], far)])
-    srcs1, codes1 = pre(1, s_mp[: 2 * rows], [after(s_other[: 2 * rows], far)])
-    srcs2, codes2 = pre(2, s_mp[2 * rows :], [after(s_other[2 * rows :], far)])
+    srcs0, codes0 = pre(0, halves[2 * rows : 4 * rows], [after(others[2 * rows : 4 * rows], sum3)])
+    srcs1, codes1 = pre(1, s_mp[: 2 * rows], [after(s_other[: 2 * rows], sum3)])
+    srcs2, codes2 = pre(2, s_mp[2 * rows :], [after(s_other[2 * rows :], sum3)])
     dec_part, enc_part = early_step(
-        (codes0, codes1, codes2), (errs0, errs1, errs2), (srcs0, srcs1, srcs2), (grad0, grad1, grad2)
+        (after(codes0, far), codes1, codes2), (errs0, errs1, errs2), (srcs0, srcs1, srcs2), (grad0, grad1, grad2)
     )
     sum2 = add(keep2, back2, BF, codes1)
     pair2 = over_pair(sum2)
@@ -428,7 +428,7 @@
     srcs3, codes3 = pre(3, s_q, q_other)
     code_grad = place_rows(place, (total0, total1, total2, after(total3, dec_part)), rows)
     dec_grad, enc_grad, token = late_step(
-        (codes3,), (errs3,), (srcs3,), (grad3,), dec_part, enc_part
+        (codes3,), (errs3,), (srcs3,), (grad3,), dec_part, enc_part, 896
     )
     input_grad = call(
         finish_kernel, [like(x.shape, F32)], 0, own, pair2, far_in, token

time: 86.4 us -> 83.4 us (0.965)
  waiting for transfers between devices: 29.2 us -> 25.1 us
  starting transfers between devices: 26.3 us -> 29.7 us
  Pallas kernels: 27.3 us -> 25 us
    ppermute x32, waiting for transfers between devices: 29.2 us -> 25.1 us  [swap(): return lax.ppermute(x, 'lat', pairs)]
    ppermute x32, starting transfers between devices: 26.3 us -> 29.7 us  [swap(): return lax.ppermute(x, 'lat', pairs)]
    pallas_call x41 -> x43, Pallas kernels: 27.3 us -> 25 us  [call(): pl.pallas_call(kernel, out_shape=outs, in_specs=options.pop('in_specs', [...]
  transfers between devices with their start and end apart: 32 -> 32, of which waited for: 13 -> 11; matrix products, arithmetic and copies ran while one was open for 1% -> 1% of each run, Pallas kernels for 29% -> 27%
where the time goes in v4:
time: 83.4 us; the launch traced here: 83.2 us
  starting transfers between devices  29.7 us (36%)
  waiting for transfers between devices  25.1 us (30%)
  Pallas kernels  25 us (30%)
  local copies, waits for them, and re-layouts  2.14 us (3%)
  between operations  1.19 us (1%)
    ppermute x32, starting transfers between devices, swap(): return lax.ppermute(x, 'lat', pairs)  29.7 us
    ppermute x32, waiting for transfers between devices, swap(): return lax.ppermute(x, 'lat', pairs)  25.1 us
    pallas_call x43, Pallas kernels, call(): pl.pallas_call(kernel, out_shape=outs, in_specs=options.pop('in_specs', [...  25 us
  transfers between devices with their start and end apart: 32, of which 11 were waited for; matrix products, arithmetic and copies ran while one was open for 1% of the time, Pallas kernels for 27%

profile of v4, /device:TPU:0, one launch (start us, length us, event | category | flops | bytes accessed | tf_op | source)
XLA Modules:
  0.0 83.2 jit_solution(7955971004345761367)
XLA Ops:
  1.1 2.7 %collective-permute-start.2 = (bf16[64,1792]{1,0:T(8,128)(2,1)}, bf16[64,1792]{1,0:T(8,128)(2,1)S(1)}, u32[]{:S(2)}, u32[]{:S(2)}) collective-permute-start(bf16[64,1792]{1,0:T(8,128)(2,1)} %bitcast.24), channel_id=1, source_target_pairs={{0,4},{1,5},{2,6},{3,7},{4,0},{5,1},{6,2},{7,3},{8,12},{9,13},{10,... | collective-permute-start | bytes 688136 | tf_op jit(solution)/shard_map/ppermute | solution.py:46
  3.8 2.5 %collective-permute-start.1 = (bf16[64,1792]{1,0:T(8,128)(2,1)}, bf16[64,1792]{1,0:T(8,128)(2,1)S(1)}, u32[]{:S(2)}, u32[]{:S(2)}) collective-permute-start(bf16[64,1792]{1,0:T(8,128)(2,1)} %bitcast.25), channel_id=1, source_target_pairs={{0,12},{1,13},{2,14},{3,15},{4,8},{5,9},{6,10},{7,11},{8,4},{9,5},... | collective-permute-start | bytes 688136 | tf_op jit(solution)/shard_map/ppermute | solution.py:46
  6.3 1.5 %collective-permute-start = (bf16[64,1792]{1,0:T(8,128)(2,1)}, bf16[64,1792]{1,0:T(8,128)(2,1)S(1)}, u32[]{:S(2)}, u32[]{:S(2)}) collective-permute-start(bf16[64,1792]{1,0:T(8,128)(2,1)} %bitcast.26), channel_id=1, source_target_pairs={{0,2},{1,3},{2,0},{3,1},{4,6},{5,7},{6,4},{7,5},{8,10},{9,11},{10,... | collective-permute-start | bytes 688136 | tf_op jit(solution)/shard_map/ppermute | solution.py:46
  7.9 1.6 %copy-done.2 = s32[1024,512]{1,0:T(8,128)S(1)} copy-done((s32[1024,512]{1,0:T(8,128)S(1)}, s32[1024,512]{1,0:T(8,128)}, u32[]{:S(2)}) %copy-start.2) | copy-done | bytes 2097176
  9.5 3.6 %shard_map.93.refs_2_.refs_3_.refs_4_.refs_6_ = f32[1024,512]{1,0:T(8,128)S(1)} custom-call(s32[16]{0:T(128)S(1)} %stack.67.refs_0_, s32[1024,512]{1,0:T(8,128)S(1)} %copy-done.2), custom_call_target="tpu_custom_call" | custom-call | flops 1 | bytes 1 | tf_op jit(solution)/shard_map/pallas_call | solution.py:83
  13.1 4.3 %collective-permute-done.1.x = bf16[64,1792]{1,0:T(8,128)(2,1)S(1)} collective-permute-done((bf16[64,1792]{1,0:T(8,128)(2,1)}, bf16[64,1792]{1,0:T(8,128)(2,1)S(1)}, u32[]{:S(2)}, u32[]{:S(2)}) %collective-permute-start.1) | collective-permute-done | bytes 229408 | tf_op jit(solution)/shard_map/ppermute | solution.py:46
  17.5 1.6 %collective-permute-start.5 = (bf16[64,1792]{1,0:T(8,128)(2,1)S(1)}, bf16[64,1792]{1,0:T(8,128)(2,1)S(1)}, u32[]{:S(2)}, u32[]{:S(2)}) collective-permute-start(bf16[64,1792]{1,0:T(8,128)(2,1)S(1)} %shard_map.94.refs_0_.refs_4_), channel_id=1, source_target_pairs={{0,2},{1,3},{2,0},{3,1},{4,6},{5,7},{6,4},{7,5},{8,10},{9,11},{10,... | collective-permute-start | bytes 688136 | tf_op jit(solution)/shard_map/ppermute | solution.py:46
  19.7 2.7 %collective-permute-start.9 = (bf16[64,1792]{1,0:T(8,128)(2,1)S(1)}, bf16[64,1792]{1,0:T(8,128)(2,1)S(1)}, u32[]{:S(2)}, u32[]{:S(2)}) collective-permute-start(bf16[64,1792]{1,0:T(8,128)(2,1)S(1)} %shard_map.95.refs_2_.x), channel_id=1, source_target_pairs={{0,12},{1,13},{2,14},{3,15},{4,8},{5,9},{6,10},{7,11},{8,4},{9,5},... | collective-permute-start | bytes 688136 | tf_op jit(solution)/shard_map/ppermute | solution.py:46
  22.4 2.3 %collective-permute-done.5.refs_0_.refs_5_ = bf16[64,1792]{1,0:T(8,128)(2,1)S(1)} collective-permute-done((bf16[64,1792]{1,0:T(8,128)(2,1)S(1)}, bf16[64,1792]{1,0:T(8,128)(2,1)S(1)}, u32[]{:S(2)}, u32[]{:S(2)}) %collective-permute-start.5) | collective-permute-done | bytes 229408 | tf_op jit(solution)/shard_map/ppermute | solution.py:46
  24.7 1.6 %collective-permute-start.6 = (bf16[64,1792]{1,0:T(8,128)(2,1)S(1)}, bf16[64,1792]{1,0:T(8,128)(2,1)S(1)}, u32[]{:S(2)}, u32[]{:S(2)}) collective-permute-start(bf16[64,1792]{1,0:T(8,128)(2,1)S(1)} %shard_map.96), channel_id=1, source_target_pairs={{0,2},{1,3},{2,0},{3,1},{4,6},{5,7},{6,4},{7,5},{8,10},{9,11},{10,... | collective-permute-start | bytes 688136 | tf_op jit(solution)/shard_map/ppermute | solution.py:46
  26.8 7.0 %collective-permute-done.9.refs_2_.x = bf16[64,1792]{1,0:T(8,128)(2,1)S(1)} collective-permute-done((bf16[64,1792]{1,0:T(8,128)(2,1)S(1)}, bf16[64,1792]{1,0:T(8,128)(2,1)S(1)}, u32[]{:S(2)}, u32[]{:S(2)}) %collective-permute-start.9) | collective-permute-done | bytes 229408 | tf_op jit(solution)/shard_map/ppermute | solution.py:46
  33.8 2.1 %collective-permute-done.8.refs_1_ = bf16[64,1792]{1,0:T(8,128)(2,1)S(1)} collective-permute-done((bf16[64,1792]{1,0:T(8,128)(2,1)S(1)}, bf16[64,1792]{1,0:T(8,128)(2,1)S(1)}, u32[]{:S(2)}, u32[]{:S(2)}) %collective-permute-start.8) | collective-permute-done | bytes 229408 | tf_op jit(solution)/shard_map/ppermute | solution.py:46
  36.8 1.5 %collective-permute-start.13 = (bf16[64,1792]{1,0:T(8,128)(2,1)S(1)}, bf16[64,1792]{1,0:T(8,128)(2,1)S(1)}, u32[]{:S(2)}, u32[]{:S(2)}) collective-permute-start(bf16[64,1792]{1,0:T(8,128)(2,1)S(1)} %shard_map.102.refs_0_), channel_id=1, source_target_pairs={{0,2},{1,3},{2,0},{3,1},{4,6},{5,7},{6,4},{7,5},{8,10},{9,11},{10,... | collective-permute-start | bytes 688136 | tf_op jit(solution)/shard_map/ppermute | solution.py:46
  38.5 2.1 %collective-permute-done.11.refs_1_ = bf16[128,1792]{1,0:T(8,128)(2,1)S(1)} collective-permute-done((bf16[128,1792]{1,0:T(8,128)(2,1)S(1)}, bf16[128,1792]{1,0:T(8,128)(2,1)S(1)}, u32[]{:S(2)}, u32[]{:S(2)}) %collective-permute-start.11) | collective-permute-done | bytes 458784 | tf_op jit(solution)/shard_map/ppermute | solution.py:46
  42.3 1.9 %collective-permute-done.14.refs_2_ = bf16[64,1792]{1,0:T(8,128)(2,1)S(1)} collective-permute-done((bf16[64,1792]{1,0:T(8,128)(2,1)S(1)}, bf16[64,1792]{1,0:T(8,128)(2,1)S(1)}, u32[]{:S(2)}, u32[]{:S(2)}) %collective-permute-start.14) | collective-permute-done | bytes 229408 | tf_op jit(solution)/shard_map/ppermute | solution.py:46
  44.5 1.3 %shard_map.105 = (f32[64,1792]{1,0:T(8,128)S(1)}, bf16[64,1792]{1,0:T(8,128)(2,1)S(1)}) custom-call(bf16[256,512]{1,0:T(8,128)(2,1)S(1)} %get-tuple-element.37.refs_0_.grad.refs_3_, bf16[128,512]{1,0:T(8,128)(2,1)S(1)} %shard_map.104.peer, bf16[1792,512]{1,0:T(8,128)(2,1)S(1)} %copy-done, bf16[1792,512]{1,0:T(8,128)(2,1)S(1)} %collective-permute-done.3.refs_3_.weight_peer), custom_call_target="tpu_custom_call" | custom-call | flops 1 | bytes 1 | tf_op jit(solution)/shard_map/pallas_call | solution.py:83
  45.8 1.4 %collective-permute-start.15 = (bf16[64,1792]{1,0:T(8,128)(2,1)S(1)}, bf16[64,1792]{1,0:T(8,128)(2,1)S(1)}, u32[]{:S(2)}, u32[]{:S(2)}) collective-permute-start(bf16[64,1792]{1,0:T(8,128)(2,1)S(1)} %get-tuple-element.40.refs_0_), channel_id=1, source_target_pairs={{0,2},{1,3},{2,0},{3,1},{4,6},{5,7},{6,4},{7,5},{8,10},{9,11},{10,... | collective-permute-start | bytes 688136 | tf_op jit(solution)/shard_map/ppermute | solution.py:46
  48.6 2.0 %collective-permute-start.17 = (bf16[64,1792]{1,0:T(8,128)(2,1)S(1)}, bf16[64,1792]{1,0:T(8,128)(2,1)S(1)}, u32[]{:S(2)}, u32[]{:S(2)}) collective-permute-start(bf16[64,1792]{1,0:T(8,128)(2,1)S(1)} %shard_map.102.refs_0_), channel_id=1, source_target_pairs={{0,4},{1,5},{2,6},{3,7},{4,0},{5,1},{6,2},{7,3},{8,12},{9,13},{10,... | collective-permute-start | bytes 688136 | tf_op jit(solution)/shard_map/ppermute | solution.py:46
  50.8 1.3 %shard_map.107 = (f32[64,1792]{1,0:T(8,128)S(1)}, bf16[64,1792]{1,0:T(8,128)(2,1)S(1)}) custom-call(bf16[256,512]{1,0:T(8,128)(2,1)S(1)} %shard_map.106.grad, bf16[128,512]{1,0:T(8,128)(2,1)S(1)} %collective-permute-done.16.peer, bf16[1792,512]{1,0:T(8,128)(2,1)S(1)} %copy-done, bf16[1792,512]{1,0:T(8,128)(2,1)S(1)} %collective-permute-done.3.refs_3_.weight_peer), custom_call_target="tpu_custom_call" | custom-call | flops 1 | bytes 1 | tf_op jit(solution)/shard_map/pallas_call | solution.py:83
  52.9 1.3 %shard_map.116 = (f32[64,1792]{1,0:T(8,128)S(1)}, bf16[64,1792]{1,0:T(8,128)(2,1)S(1)}) custom-call(bf16[256,512]{1,0:T(8,128)(2,1)S(1)} %shard_map.115.grad, bf16[128,512]{1,0:T(8,128)(2,1)S(1)} %collective-permute-done.20.peer, bf16[1792,512]{1,0:T(8,128)(2,1)S(1)} %copy-done, bf16[1792,512]{1,0:T(8,128)(2,1)S(1)} %collective-permute-done.3.refs_3_.weight_peer), custom_call_target="tpu_custom_call" | custom-call | flops 1 | bytes 1 | tf_op jit(solution)/shard_map/pallas_call | solution.py:83
  54.2 1.4 %collective-permute-start.29 = (bf16[64,1792]{1,0:T(8,128)(2,1)S(1)}, bf16[64,1792]{1,0:T(8,128)(2,1)S(1)}, u32[]{:S(2)}, u32[]{:S(2)}) collective-permute-start(bf16[64,1792]{1,0:T(8,128)(2,1)S(1)} %get-tuple-element.49.refs_1_), channel_id=1, source_target_pairs={{0,2},{1,3},{2,0},{3,1},{4,6},{5,7},{6,4},{7,5},{8,10},{9,11},{10,... | collective-permute-start | bytes 688136 | tf_op jit(solution)/shard_map/ppermute | solution.py:46
  55.7 1.4 %collective-permute-done.17.refs_1_.x = bf16[64,1792]{1,0:T(8,128)(2,1)S(1)} collective-permute-done((bf16[64,1792]{1,0:T(8,128)(2,1)S(1)}, bf16[64,1792]{1,0:T(8,128)(2,1)S(1)}, u32[]{:S(2)}, u32[]{:S(2)}) %collective-permute-start.17) | collective-permute-done | bytes 229408 | tf_op jit(solution)/shard_map/ppermute | solution.py:46
  57.1 2.1 %collective-permute-start.19 = (bf16[64,1792]{1,0:T(8,128)(2,1)S(1)}, bf16[64,1792]{1,0:T(8,128)(2,1)S(1)}, u32[]{:S(2)}, u32[]{:S(2)}) collective-permute-start(bf16[64,1792]{1,0:T(8,128)(2,1)S(1)} %shard_map.108.refs_0_.refs_4_), channel_id=1, source_target_pairs={{0,4},{1,5},{2,6},{3,7},{4,0},{5,1},{6,2},{7,3},{8,12},{9,13},{10,... | collective-permute-start | bytes 688136 | tf_op jit(solution)/shard_map/ppermute | solution.py:46
  60.0 2.0 %collective-permute-done.21.refs_3_ = bf16[64,1792]{1,0:T(8,128)(2,1)S(1)} collective-permute-done((bf16[64,1792]{1,0:T(8,128)(2,1)S(1)}, bf16[64,1792]{1,0:T(8,128)(2,1)S(1)}, u32[]{:S(2)}, u32[]{:S(2)}) %collective-permute-start.21) | collective-permute-done | bytes 229408 | tf_op jit(solution)/shard_map/ppermute | solution.py:46
  62.9 0.7 collective-permute-start.23
  63.7 1.3 %shard_map.132 = (f32[64,1792]{1,0:T(8,128)S(1)}, bf16[64,1792]{1,0:T(8,128)(2,1)S(1)}) custom-call(bf16[256,512]{1,0:T(8,128)(2,1)S(1)} %get-tuple-element.58.refs_9_.grad, bf16[128,512]{1,0:T(8,128)(2,1)S(1)} %collective-permute-done.27.peer, bf16[1792,512]{1,0:T(8,128)(2,1)S(1)} %copy-done, bf16[1792,512]{1,0:T(8,128)(2,1)S(1)} %collective-permute-done.3.refs_3_.weight_peer), custom_call_target="tpu_custom_call" | custom-call | flops 1 | bytes 1 | tf_op jit(solution)/shard_map/pallas_call | solution.py:83
  65.0 1.3 %collective-permute-done.19 = bf16[64,1792]{1,0:T(8,128)(2,1)S(1)} collective-permute-done((bf16[64,1792]{1,0:T(8,128)(2,1)S(1)}, bf16[64,1792]{1,0:T(8,128)(2,1)S(1)}, u32[]{:S(2)}, u32[]{:S(2)}) %collective-permute-start.19) | collective-permute-done | bytes 229408 | tf_op jit(solution)/shard_map/ppermute | solution.py:46
  67.0 2.6 %collective-permute-start.31 = (bf16[64,1792]{1,0:T(8,128)(2,1)S(1)}, bf16[64,1792]{1,0:T(8,128)(2,1)S(1)}, u32[]{:S(2)}, u32[]{:S(2)}) collective-permute-start(bf16[64,1792]{1,0:T(8,128)(2,1)S(1)} %shard_map.117.refs_0_), channel_id=1, source_target_pairs={{0,12},{1,13},{2,14},{3,15},{4,8},{5,9},{6,10},{7,11},{8,4},{9,5},... | collective-permute-start | bytes 688136 | tf_op jit(solution)/shard_map/ppermute | solution.py:46
  71.3 3.7 %shard_map.125 = (f32[512,1792]{1,0:T(8,128)S(1)}, f32[1792,512]{1,0:T(8,128)S(1)}) custom-call(bf16[256,512]{1,0:T(8,128)(2,1)S(1)} %shard_map.118.refs_0_, bf16[256,512]{1,0:T(8,128)(2,1)S(1)} %get-tuple-element.50.refs_1_.refs_0_, bf16[256,512]{1,0:T(8,128)(2,1)S(1)} %get-tuple-element.51.refs_2_, bf16[256,1792]{1,0:T(8,128)(2,1)S(1)} %get-tuple-element.52.refs_3_, ...), custom_call_target="tpu_custom_call" | custom-call | flops 1 | bytes 1 | tf_op jit(solution)/shard_map/pallas_call | solution.py:83
  76.0 2.0 %shard_map.127 = f32[1024,512]{1,0:T(8,128)} custom-call(s32[16]{0:T(128)S(1)} %stack.67.refs_0_, f32[256,512]{1,0:T(8,128)S(1)} %get-tuple-element.42.refs_1_, f32[256,512]{1,0:T(8,128)S(1)} %get-tuple-element.43.refs_2_, f32[256,512]{1,0:T(8,128)S(1)} %get-tuple-element.44.refs_3_, f32[256,512]{1,0:T(8,128)S(1)} %shard_map.126.refs_4_), custom_call_target="tpu_custom_call" | custom-call | flops 1 | bytes 1 | tf_op jit(solution)/shard_map/pallas_call | solution.py:83
  78.7 3.7 %shard_map.131 = (f32[512,1792]{1,0:T(8,128)}, f32[1792,512]{1,0:T(8,128)}, f32[8,128]{1,0:T(8,128)S(1)}) custom-call(bf16[256,512]{1,0:T(8,128)(2,1)S(1)} %get-tuple-element.60.refs_0_, bf16[256,1792]{1,0:T(8,128)(2,1)S(1)} %get-tuple-element.61.refs_1_, bf16[256,1792]{1,0:T(8,128)(2,1)S(1)} %get-tuple-element.62.refs_2_, ...), custom_call_target="tpu_custom_call" | custom-call | flops 1 | bytes 1 | tf_op jit(solution)/shard_map/pallas_call | solution.py:83
  82.4 0.8 %shard_map.135 = f32[64,1792]{1,0:T(8,128)} custom-call(f32[64,1792]{1,0:T(8,128)S(1)} %shard_map.133.own, bf16[64,1792]{1,0:T(8,128)(2,1)S(1)} %collective-permute-done.30.pair, bf16[64,1792]{1,0:T(8,128)(2,1)S(1)} %collective-permute-done.31.far, f32[8,128]{1,0:T(8,128)S(1)} %get-tuple-element.69.token), custom_call_target="tpu_custom_call" | custom-call | flops 1 | bytes 1 | tf_op jit(solution)/shard_map/pallas_call | solution.py:83
  (100 shorter events, 12.8 us)
Async XLA Ops:
  0.6 16.8 %collective-permute-start.3 = (bf16[1792,512]{1,0:T(8,128)(2,1)}, bf16[1792,512]{1,0:T(8,128)(2,1)S(1)}, u32[]{:S(2)}, u32[]{:S(2)}) collective-permute-start(bf16[1792,512]{1,0:T(8,128)(2,1)} %weight.7), channel_id=1, source_target_pairs={{0,1},{1,0},{2,3},{3,2},{4,5},{5,4},{6,7},{7,6},{8,9},{9,8},{10,11... | collective-permute-start | bytes 5505032 | tf_op jit(solution)/shard_map/ppermute | solution.py:46
  1.1 11.9 %collective-permute-start.2 = (bf16[64,1792]{1,0:T(8,128)(2,1)}, bf16[64,1792]{1,0:T(8,128)(2,1)S(1)}, u32[]{:S(2)}, u32[]{:S(2)}) collective-permute-start(bf16[64,1792]{1,0:T(8,128)(2,1)} %bitcast.24), channel_id=1, source_target_pairs={{0,4},{1,5},{2,6},{3,7},{4,0},{5,1},{6,2},{7,3},{8,12},{9,13},{10,... | collective-permute-start | bytes 688136 | tf_op jit(solution)/shard_map/ppermute | solution.py:46
  3.8 13.6 %collective-permute-start.1 = (bf16[64,1792]{1,0:T(8,128)(2,1)}, bf16[64,1792]{1,0:T(8,128)(2,1)S(1)}, u32[]{:S(2)}, u32[]{:S(2)}) collective-permute-start(bf16[64,1792]{1,0:T(8,128)(2,1)} %bitcast.25), channel_id=1, source_target_pairs={{0,12},{1,13},{2,14},{3,15},{4,8},{5,9},{6,10},{7,11},{8,4},{9,5},... | collective-permute-start | bytes 688136 | tf_op jit(solution)/shard_map/ppermute | solution.py:46
  6.3 11.2 %collective-permute-start = (bf16[64,1792]{1,0:T(8,128)(2,1)}, bf16[64,1792]{1,0:T(8,128)(2,1)S(1)}, u32[]{:S(2)}, u32[]{:S(2)}) collective-permute-start(bf16[64,1792]{1,0:T(8,128)(2,1)} %bitcast.26), channel_id=1, source_target_pairs={{0,2},{1,3},{2,0},{3,1},{4,6},{5,7},{6,4},{7,5},{8,10},{9,11},{10,... | collective-permute-start | bytes 688136 | tf_op jit(solution)/shard_map/ppermute | solution.py:46
  17.5 7.2 %collective-permute-start.5 = (bf16[64,1792]{1,0:T(8,128)(2,1)S(1)}, bf16[64,1792]{1,0:T(8,128)(2,1)S(1)}, u32[]{:S(2)}, u32[]{:S(2)}) collective-permute-start(bf16[64,1792]{1,0:T(8,128)(2,1)S(1)} %shard_map.94.refs_0_.refs_4_), channel_id=1, source_target_pairs={{0,2},{1,3},{2,0},{3,1},{4,6},{5,7},{6,4},{7,5},{8,10},{9,11},{10,... | collective-permute-start | bytes 688136 | tf_op jit(solution)/shard_map/ppermute | solution.py:46
  19.1 14.7 %collective-permute-start.7 = (bf16[64,1792]{1,0:T(8,128)(2,1)S(1)}, bf16[64,1792]{1,0:T(8,128)(2,1)S(1)}, u32[]{:S(2)}, u32[]{:S(2)}) collective-permute-start(bf16[64,1792]{1,0:T(8,128)(2,1)S(1)} %shard_map.94.refs_0_.refs_4_), channel_id=1, source_target_pairs={{0,4},{1,5},{2,6},{3,7},{4,0},{5,1},{6,2},{7,3},{8,12},{9,13},{10,... | collective-permute-start | bytes 688136 | tf_op jit(solution)/shard_map/ppermute | solution.py:46
  19.7 14.1 %collective-permute-start.9 = (bf16[64,1792]{1,0:T(8,128)(2,1)S(1)}, bf16[64,1792]{1,0:T(8,128)(2,1)S(1)}, u32[]{:S(2)}, u32[]{:S(2)}) collective-permute-start(bf16[64,1792]{1,0:T(8,128)(2,1)S(1)} %shard_map.95.refs_2_.x), channel_id=1, source_target_pairs={{0,12},{1,13},{2,14},{3,15},{4,8},{5,9},{6,10},{7,11},{8,4},{9,5},... | collective-permute-start | bytes 688136 | tf_op jit(solution)/shard_map/ppermute | solution.py:46
  24.7 9.1 %collective-permute-start.6 = (bf16[64,1792]{1,0:T(8,128)(2,1)S(1)}, bf16[64,1792]{1,0:T(8,128)(2,1)S(1)}, u32[]{:S(2)}, u32[]{:S(2)}) collective-permute-start(bf16[64,1792]{1,0:T(8,128)(2,1)S(1)} %shard_map.96), channel_id=1, source_target_pairs={{0,2},{1,3},{2,0},{3,1},{4,6},{5,7},{6,4},{7,5},{8,10},{9,11},{10,... | collective-permute-start | bytes 688136 | tf_op jit(solution)/shard_map/ppermute | solution.py:46
  26.3 9.6 %collective-permute-start.8 = (bf16[64,1792]{1,0:T(8,128)(2,1)S(1)}, bf16[64,1792]{1,0:T(8,128)(2,1)S(1)}, u32[]{:S(2)}, u32[]{:S(2)}) collective-permute-start(bf16[64,1792]{1,0:T(8,128)(2,1)S(1)} %collective-permute-done.5.refs_0_.refs_5_), channel_id=1, source_target_pairs={{0,4},{1,5},{2,6},{3,7},{4,0},{5,1},{6,2},{7,3},{8,12},{9,13},{10,... | collective-permute-start | bytes 688136 | tf_op jit(solution)/shard_map/ppermute | solution.py:46
  26.3 9.7 %collective-permute-start.4 = (bf16[64,1792]{1,0:T(8,128)(2,1)S(1)}, bf16[64,1792]{1,0:T(8,128)(2,1)S(1)}, u32[]{:S(2)}, u32[]{:S(2)}) collective-permute-start(bf16[64,1792]{1,0:T(8,128)(2,1)S(1)} %copy-done.3), channel_id=1, source_target_pairs={{0,2},{1,3},{2,0},{3,1},{4,6},{5,7},{6,4},{7,5},{8,10},{9,11},{10,... | collective-permute-start | bytes 688136 | tf_op jit(solution)/shard_map/ppermute | solution.py:46
  36.1 5.4 %collective-permute-start.10 = (bf16[512,1792]{1,0:T(8,128)(2,1)S(1)}, bf16[512,1792]{1,0:T(8,128)(2,1)S(1)}, u32[]{:S(2)}, u32[]{:S(2)}) collective-permute-start(bf16[512,1792]{1,0:T(8,128)(2,1)S(1)} %shard_map.98), channel_id=1, source_target_pairs={{0,1},{1,0},{2,3},{3,2},{4,5},{5,4},{6,7},{7,6},{8,9},{9,8},{10,11... | collective-permute-start | bytes 5505032 | tf_op jit(solution)/shard_map/ppermute | solution.py:46
  36.2 8.1 %collective-permute-start.14 = (bf16[64,1792]{1,0:T(8,128)(2,1)S(1)}, bf16[64,1792]{1,0:T(8,128)(2,1)S(1)}, u32[]{:S(2)}, u32[]{:S(2)}) collective-permute-start(bf16[64,1792]{1,0:T(8,128)(2,1)S(1)} %shard_map.103), channel_id=1, source_target_pairs={{0,4},{1,5},{2,6},{3,7},{4,0},{5,1},{6,2},{7,3},{8,12},{9,13},{10,... | collective-permute-start | bytes 688136 | tf_op jit(solution)/shard_map/ppermute | solution.py:46
  36.4 4.2 %collective-permute-start.11 = (bf16[128,1792]{1,0:T(8,128)(2,1)S(1)}, bf16[128,1792]{1,0:T(8,128)(2,1)S(1)}, u32[]{:S(2)}, u32[]{:S(2)}) collective-permute-start(bf16[128,1792]{1,0:T(8,128)(2,1)S(1)} %shard_map.97.refs_8_.refs_0_), channel_id=1, source_target_pairs={{0,1},{1,0},{2,3},{3,2},{4,5},{5,4},{6,7},{7,6},{8,9},{9,8},{10,11... | collective-permute-start | bytes 1376264 | tf_op jit(solution)/shard_map/ppermute | solution.py:46
  36.8 7.6 %collective-permute-start.13 = (bf16[64,1792]{1,0:T(8,128)(2,1)S(1)}, bf16[64,1792]{1,0:T(8,128)(2,1)S(1)}, u32[]{:S(2)}, u32[]{:S(2)}) collective-permute-start(bf16[64,1792]{1,0:T(8,128)(2,1)S(1)} %shard_map.102.refs_0_), channel_id=1, source_target_pairs={{0,2},{1,3},{2,0},{3,1},{4,6},{5,7},{6,4},{7,5},{8,10},{9,11},{10,... | collective-permute-start | bytes 688136 | tf_op jit(solution)/shard_map/ppermute | solution.py:46
  41.3 3.2 %collective-permute-start.12 = (bf16[128,512]{1,0:T(8,128)(2,1)S(1)}, bf16[128,512]{1,0:T(8,128)(2,1)S(1)}, u32[]{:S(2)}, u32[]{:S(2)}) collective-permute-start(bf16[128,512]{1,0:T(8,128)(2,1)S(1)} %slice.59), channel_id=1, source_target_pairs={{0,1},{1,0},{2,3},{3,2},{4,5},{5,4},{6,7},{7,6},{8,9},{9,8},{10,11... | collective-permute-start | bytes 393224 | tf_op jit(solution)/shard_map/ppermute | solution.py:46
  45.8 9.8 %collective-permute-start.15 = (bf16[64,1792]{1,0:T(8,128)(2,1)S(1)}, bf16[64,1792]{1,0:T(8,128)(2,1)S(1)}, u32[]{:S(2)}, u32[]{:S(2)}) collective-permute-start(bf16[64,1792]{1,0:T(8,128)(2,1)S(1)} %get-tuple-element.40.refs_0_), channel_id=1, source_target_pairs={{0,2},{1,3},{2,0},{3,1},{4,6},{5,7},{6,4},{7,5},{8,10},{9,11},{10,... | collective-permute-start | bytes 688136 | tf_op jit(solution)/shard_map/ppermute | solution.py:46
  47.3 3.5 %collective-permute-start.16 = (bf16[128,512]{1,0:T(8,128)(2,1)S(1)}, bf16[128,512]{1,0:T(8,128)(2,1)S(1)}, u32[]{:S(2)}, u32[]{:S(2)}) collective-permute-start(bf16[128,512]{1,0:T(8,128)(2,1)S(1)} %slice.62), channel_id=1, source_target_pairs={{0,1},{1,0},{2,3},{3,2},{4,5},{5,4},{6,7},{7,6},{8,9},{9,8},{10,11... | collective-permute-start | bytes 393224 | tf_op jit(solution)/shard_map/ppermute | solution.py:46
  48.1 4.8 %collective-permute-start.20 = (bf16[128,512]{1,0:T(8,128)(2,1)S(1)}, bf16[128,512]{1,0:T(8,128)(2,1)S(1)}, u32[]{:S(2)}, u32[]{:S(2)}) collective-permute-start(bf16[128,512]{1,0:T(8,128)(2,1)S(1)} %slice.67), channel_id=1, source_target_pairs={{0,1},{1,0},{2,3},{3,2},{4,5},{5,4},{6,7},{7,6},{8,9},{9,8},{10,11... | collective-permute-start | bytes 393224 | tf_op jit(solution)/shard_map/ppermute | solution.py:46
  48.6 8.4 %collective-permute-start.17 = (bf16[64,1792]{1,0:T(8,128)(2,1)S(1)}, bf16[64,1792]{1,0:T(8,128)(2,1)S(1)}, u32[]{:S(2)}, u32[]{:S(2)}) collective-permute-start(bf16[64,1792]{1,0:T(8,128)(2,1)S(1)} %shard_map.102.refs_0_), channel_id=1, source_target_pairs={{0,4},{1,5},{2,6},{3,7},{4,0},{5,1},{6,2},{7,3},{8,12},{9,13},{10,... | collective-permute-start | bytes 688136 | tf_op jit(solution)/shard_map/ppermute | solution.py:46
  50.6 11.4 %collective-permute-start.21 = (bf16[64,1792]{1,0:T(8,128)(2,1)S(1)}, bf16[64,1792]{1,0:T(8,128)(2,1)S(1)}, u32[]{:S(2)}, u32[]{:S(2)}) collective-permute-start(bf16[64,1792]{1,0:T(8,128)(2,1)S(1)} %shard_map.119), channel_id=1, source_target_pairs={{0,4},{1,5},{2,6},{3,7},{4,0},{5,1},{6,2},{7,3},{8,12},{9,13},{10,... | collective-permute-start | bytes 688136 | tf_op jit(solution)/shard_map/ppermute | solution.py:46
  52.1 12.9 %collective-permute-start.18 = (bf16[64,1792]{1,0:T(8,128)(2,1)S(1)}, bf16[64,1792]{1,0:T(8,128)(2,1)S(1)}, u32[]{:S(2)}, u32[]{:S(2)}) collective-permute-start(bf16[64,1792]{1,0:T(8,128)(2,1)S(1)} %get-tuple-element.41.refs_0_), channel_id=1, source_target_pairs={{0,2},{1,3},{2,0},{3,1},{4,6},{5,7},{6,4},{7,5},{8,10},{9,11},{10,... | collective-permute-start | bytes 688136 | tf_op jit(solution)/shard_map/ppermute | solution.py:46
  54.2 16.3 %collective-permute-start.29 = (bf16[64,1792]{1,0:T(8,128)(2,1)S(1)}, bf16[64,1792]{1,0:T(8,128)(2,1)S(1)}, u32[]{:S(2)}, u32[]{:S(2)}) collective-permute-start(bf16[64,1792]{1,0:T(8,128)(2,1)S(1)} %get-tuple-element.49.refs_1_), channel_id=1, source_target_pairs={{0,2},{1,3},{2,0},{3,1},{4,6},{5,7},{6,4},{7,5},{8,10},{9,11},{10,... | collective-permute-start | bytes 688136 | tf_op jit(solution)/shard_map/ppermute | solution.py:46
  57.1 9.2 %collective-permute-start.19 = (bf16[64,1792]{1,0:T(8,128)(2,1)S(1)}, bf16[64,1792]{1,0:T(8,128)(2,1)S(1)}, u32[]{:S(2)}, u32[]{:S(2)}) collective-permute-start(bf16[64,1792]{1,0:T(8,128)(2,1)S(1)} %shard_map.108.refs_0_.refs_4_), channel_id=1, source_target_pairs={{0,4},{1,5},{2,6},{3,7},{4,0},{5,1},{6,2},{7,3},{8,12},{9,13},{10,... | collective-permute-start | bytes 688136 | tf_op jit(solution)/shard_map/ppermute | solution.py:46
  59.9 3.0 %collective-permute-start.27 = (bf16[128,512]{1,0:T(8,128)(2,1)S(1)}, bf16[128,512]{1,0:T(8,128)(2,1)S(1)}, u32[]{:S(2)}, u32[]{:S(2)}) collective-permute-start(bf16[128,512]{1,0:T(8,128)(2,1)S(1)} %slice.75), channel_id=1, source_target_pairs={{0,1},{1,0},{2,3},{3,2},{4,5},{5,4},{6,7},{7,6},{8,9},{9,8},{10,11... | collective-permute-start | bytes 393224 | tf_op jit(solution)/shard_map/ppermute | solution.py:46
  62.1 7.6 %collective-permute-start.22 = (bf16[256,1792]{1,0:T(8,128)(2,1)S(1)}, bf16[256,1792]{1,0:T(8,128)(2,1)S(1)}, u32[]{:S(2)}, u32[]{:S(2)}) collective-permute-start(bf16[256,1792]{1,0:T(8,128)(2,1)S(1)} %shard_map.120), channel_id=1, source_target_pairs={{0,1},{1,0},{2,3},{3,2},{4,5},{5,4},{6,7},{7,6},{8,9},{9,8},{10,11... | collective-permute-start | bytes 2752520 | tf_op jit(solution)/shard_map/ppermute | solution.py:46
  62.9 12.0 %collective-permute-start.23 = (bf16[64,1792]{1,0:T(8,128)(2,1)S(1)}, bf16[64,1792]{1,0:T(8,128)(2,1)S(1)}, u32[]{:S(2)}, u32[]{:S(2)}) collective-permute-start(bf16[64,1792]{1,0:T(8,128)(2,1)S(1)} %shard_map.128.refs_0_), channel_id=1, source_target_pairs={{0,2},{1,3},{2,0},{3,1},{4,6},{5,7},{6,4},{7,5},{8,10},{9,11},{10,... | collective-permute-start | bytes 688136 | tf_op jit(solution)/shard_map/ppermute | solution.py:46
  66.4 9.6 %collective-permute-start.28 = (bf16[64,1792]{1,0:T(8,128)(2,1)S(1)}, bf16[64,1792]{1,0:T(8,128)(2,1)S(1)}, u32[]{:S(2)}, u32[]{:S(2)}) collective-permute-start(bf16[64,1792]{1,0:T(8,128)(2,1)S(1)} %get-tuple-element.67), channel_id=1, source_target_pairs={{0,2},{1,3},{2,0},{3,1},{4,6},{5,7},{6,4},{7,5},{8,10},{9,11},{10,... | collective-permute-start | bytes 688136 | tf_op jit(solution)/shard_map/ppermute | solution.py:46
  67.0 15.3 %collective-permute-start.31 = (bf16[64,1792]{1,0:T(8,128)(2,1)S(1)}, bf16[64,1792]{1,0:T(8,128)(2,1)S(1)}, u32[]{:S(2)}, u32[]{:S(2)}) collective-permute-start(bf16[64,1792]{1,0:T(8,128)(2,1)S(1)} %shard_map.117.refs_0_), channel_id=1, source_target_pairs={{0,12},{1,13},{2,14},{3,15},{4,8},{5,9},{6,10},{7,11},{8,4},{9,5},... | collective-permute-start | bytes 688136 | tf_op jit(solution)/shard_map/ppermute | solution.py:46
  70.5 11.8 %collective-permute-start.30 = (bf16[64,1792]{1,0:T(8,128)(2,1)S(1)}, bf16[64,1792]{1,0:T(8,128)(2,1)S(1)}, u32[]{:S(2)}, u32[]{:S(2)}) collective-permute-start(bf16[64,1792]{1,0:T(8,128)(2,1)S(1)} %shard_map.134), channel_id=1, source_target_pairs={{0,4},{1,5},{2,6},{3,7},{4,0},{5,1},{6,2},{7,3},{8,12},{9,13},{10,... | collective-permute-start | bytes 688136 | tf_op jit(solution)/shard_map/ppermute | solution.py:46
  75.0 3.0 %collective-permute-start.25 = (bf16[48,1792]{1,0:T(8,128)(2,1)S(1)}, bf16[48,1792]{1,0:T(8,128)(2,1)S(1)}, u32[]{:S(2)}, u32[]{:S(2)}) collective-permute-start(bf16[48,1792]{1,0:T(8,128)(2,1)S(1)} %get-tuple-element.82), channel_id=1, source_target_pairs={{0,1},{1,0},{2,3},{3,2},{4,5},{5,4},{6,7},{7,6},{8,9},{9,8},{10,11... | collective-permute-start | bytes 516104 | tf_op jit(solution)/shard_map/ppermute | solution.py:46
  75.1 2.9 %collective-permute-start.24 = (bf16[48,1792]{1,0:T(8,128)(2,1)S(1)}, bf16[48,1792]{1,0:T(8,128)(2,1)S(1)}, u32[]{:S(2)}, u32[]{:S(2)}) collective-permute-start(bf16[48,1792]{1,0:T(8,128)(2,1)S(1)} %get-tuple-element.83), channel_id=1, source_target_pairs={{0,1},{1,0},{2,3},{3,2},{4,5},{5,4},{6,7},{7,6},{8,9},{9,8},{10,11... | collective-permute-start | bytes 516104 | tf_op jit(solution)/shard_map/ppermute | solution.py:46
  75.9 2.1 %collective-permute-start.26 = (bf16[32,1792]{1,0:T(8,128)(2,1)S(1)}, bf16[32,1792]{1,0:T(8,128)(2,1)S(1)}, u32[]{:S(2)}, u32[]{:S(2)}) collective-permute-start(bf16[32,1792]{1,0:T(8,128)(2,1)S(1)} %slice.90), channel_id=1, source_target_pairs={{0,1},{1,0},{2,3},{3,2},{4,5},{5,4},{6,7},{7,6},{8,9},{9,8},{10,11... | collective-permute-start | bytes 344072 | tf_op jit(solution)/shard_map/ppermute | solution.py:46
  (6 other events, 36.3 us)

commit v5 on v4

--- a/solution.py
+++ b/solution.py
@@ -394,7 +394,8 @@
     errs3, total3, grad3 = code(3, half3, [other3])
     peer3 = across(grad3)
     errs1, total1, grad1 = code(1, halves[4 * rows : 6 * rows], [after(others[4 * rows : 6 * rows], grad3)])
-    keep3, send3 = term(grad3, after(peer3, grad1, s_y1, s_p))
+    errs0, total0, grad0 = code(0, halves[: 2 * rows], [after(others[: 2 * rows], grad1)])
+    keep3, send3 = term(grad3, after(peer3, grad0, s_y1, s_p))
     back3 = over_y(send3)
     errs2, total2, grad2 = code(2, halves[6 * rows :], [after(others[6 * rows :], send3)])
     peer1, peer2 = across(grad1), across(grad2)
@@ -408,8 +409,7 @@
     s_y3 = over_y(s_q)
     s_mp = pack([s_m, s_y1, s_p, s_p1], sum3)
     s_other = over_core(s_mp)
-    errs0, total0, grad0 = code(0, halves[: 2 * rows], [after(others[: 2 * rows], sum3)])
-    keep0, send0 = term(grad0, across(grad0))
+    keep0, send0 = term(after(grad0, sum3), across(grad0))
     back0 = over_y(send0)
     far = pack([(keep1 + back1.astype(F32) + pair3.astype(F32)).astype(BF)], send2)
     far_in = over_mirror(far)

time: 83.4 us -> 83 us (level)
  waiting for transfers between devices: 25.1 us -> 23.9 us
    ppermute x32, waiting for transfers between devices: 25.1 us -> 23.9 us  [swap(): return lax.ppermute(x, 'lat', pairs)]
    pallas_call x43 -> x44, Pallas kernels: 25 us -> 25 us  [call(): pl.pallas_call(kernel, out_shape=outs, in_specs=options.pop('in_specs', [...]
  transfers between devices with their start and end apart: 32 -> 32, of which waited for: 11 -> 10; matrix products, arithmetic and copies ran while one was open for 1% -> 1% of each run, Pallas kernels for 27% -> 27%
where the time goes in v5:
time: 83 us; the launch traced here: 82.9 us
  starting transfers between devices  30.4 us (37%)
  Pallas kernels  25 us (30%)
  waiting for transfers between devices  23.9 us (29%)
  local copies, waits for them, and re-layouts  2.14 us (3%)
  between operations  1.22 us (1%)
    ppermute x32, starting transfers between devices, swap(): return lax.ppermute(x, 'lat', pairs)  30.4 us
    pallas_call x44, Pallas kernels, call(): pl.pallas_call(kernel, out_shape=outs, in_specs=options.pop('in_specs', [...  25 us
    ppermute x32, waiting for transfers between devices, swap(): return lax.ppermute(x, 'lat', pairs)  23.9 us
  transfers between devices with their start and end apart: 32, of which 10 were waited for; matrix products, arithmetic and copies ran while one was open for 1% of the time, Pallas kernels for 27%

profile of v5, /device:TPU:0, one launch (start us, length us, event | category | flops | bytes accessed | tf_op | source)
XLA Modules:
  0.0 82.9 jit_solution(7915362931172500366)
XLA Ops:
  1.1 2.7 %collective-permute-start.2 = (bf16[64,1792]{1,0:T(8,128)(2,1)}, bf16[64,1792]{1,0:T(8,128)(2,1)S(1)}, u32[]{:S(2)}, u32[]{:S(2)}) collective-permute-start(bf16[64,1792]{1,0:T(8,128)(2,1)} %bitcast.24), channel_id=1, source_target_pairs={{0,4},{1,5},{2,6},{3,7},{4,0},{5,1},{6,2},{7,3},{8,12},{9,13},{10,... | collective-permute-start | bytes 688136 | tf_op jit(solution)/shard_map/ppermute | solution.py:46
  3.8 2.5 %collective-permute-start.1 = (bf16[64,1792]{1,0:T(8,128)(2,1)}, bf16[64,1792]{1,0:T(8,128)(2,1)S(1)}, u32[]{:S(2)}, u32[]{:S(2)}) collective-permute-start(bf16[64,1792]{1,0:T(8,128)(2,1)} %bitcast.25), channel_id=1, source_target_pairs={{0,12},{1,13},{2,14},{3,15},{4,8},{5,9},{6,10},{7,11},{8,4},{9,5},... | collective-permute-start | bytes 688136 | tf_op jit(solution)/shard_map/ppermute | solution.py:46
  6.3 1.5 %collective-permute-start = (bf16[64,1792]{1,0:T(8,128)(2,1)}, bf16[64,1792]{1,0:T(8,128)(2,1)S(1)}, u32[]{:S(2)}, u32[]{:S(2)}) collective-permute-start(bf16[64,1792]{1,0:T(8,128)(2,1)} %bitcast.26), channel_id=1, source_target_pairs={{0,2},{1,3},{2,0},{3,1},{4,6},{5,7},{6,4},{7,5},{8,10},{9,11},{10,... | collective-permute-start | bytes 688136 | tf_op jit(solution)/shard_map/ppermute | solution.py:46
  7.9 1.6 %copy-done.2 = s32[1024,512]{1,0:T(8,128)S(1)} copy-done((s32[1024,512]{1,0:T(8,128)S(1)}, s32[1024,512]{1,0:T(8,128)}, u32[]{:S(2)}) %copy-start.2) | copy-done | bytes 2097176
  9.5 3.6 %shard_map.93.refs_2_.refs_3_.refs_4_.refs_6_ = f32[1024,512]{1,0:T(8,128)S(1)} custom-call(s32[16]{0:T(128)S(1)} %stack.67.refs_0_, s32[1024,512]{1,0:T(8,128)S(1)} %copy-done.2), custom_call_target="tpu_custom_call" | custom-call | flops 1 | bytes 1 | tf_op jit(solution)/shard_map/pallas_call | solution.py:83
  13.1 4.3 %collective-permute-done.1.x = bf16[64,1792]{1,0:T(8,128)(2,1)S(1)} collective-permute-done((bf16[64,1792]{1,0:T(8,128)(2,1)}, bf16[64,1792]{1,0:T(8,128)(2,1)S(1)}, u32[]{:S(2)}, u32[]{:S(2)}) %collective-permute-start.1) | collective-permute-done | bytes 229408 | tf_op jit(solution)/shard_map/ppermute | solution.py:46
  17.5 1.6 %collective-permute-start.5 = (bf16[64,1792]{1,0:T(8,128)(2,1)S(1)}, bf16[64,1792]{1,0:T(8,128)(2,1)S(1)}, u32[]{:S(2)}, u32[]{:S(2)}) collective-permute-start(bf16[64,1792]{1,0:T(8,128)(2,1)S(1)} %shard_map.94.refs_0_.refs_4_), channel_id=1, source_target_pairs={{0,2},{1,3},{2,0},{3,1},{4,6},{5,7},{6,4},{7,5},{8,10},{9,11},{10,... | collective-permute-start | bytes 688136 | tf_op jit(solution)/shard_map/ppermute | solution.py:46
  19.7 2.7 %collective-permute-start.9 = (bf16[64,1792]{1,0:T(8,128)(2,1)S(1)}, bf16[64,1792]{1,0:T(8,128)(2,1)S(1)}, u32[]{:S(2)}, u32[]{:S(2)}) collective-permute-start(bf16[64,1792]{1,0:T(8,128)(2,1)S(1)} %shard_map.95.refs_2_.x), channel_id=1, source_target_pairs={{0,12},{1,13},{2,14},{3,15},{4,8},{5,9},{6,10},{7,11},{8,4},{9,5},... | collective-permute-start | bytes 688136 | tf_op jit(solution)/shard_map/ppermute | solution.py:46
  22.4 2.3 %collective-permute-done.5.refs_0_.refs_5_ = bf16[64,1792]{1,0:T(8,128)(2,1)S(1)} collective-permute-done((bf16[64,1792]{1,0:T(8,128)(2,1)S(1)}, bf16[64,1792]{1,0:T(8,128)(2,1)S(1)}, u32[]{:S(2)}, u32[]{:S(2)}) %collective-permute-start.5) | collective-permute-done | bytes 229408 | tf_op jit(solution)/shard_map/ppermute | solution.py:46
  24.7 1.6 %collective-permute-start.6 = (bf16[64,1792]{1,0:T(8,128)(2,1)S(1)}, bf16[64,1792]{1,0:T(8,128)(2,1)S(1)}, u32[]{:S(2)}, u32[]{:S(2)}) collective-permute-start(bf16[64,1792]{1,0:T(8,128)(2,1)S(1)} %shard_map.96), channel_id=1, source_target_pairs={{0,2},{1,3},{2,0},{3,1},{4,6},{5,7},{6,4},{7,5},{8,10},{9,11},{10,... | collective-permute-start | bytes 688136 | tf_op jit(solution)/shard_map/ppermute | solution.py:46
  26.8 7.0 %collective-permute-done.9.refs_2_.x = bf16[64,1792]{1,0:T(8,128)(2,1)S(1)} collective-permute-done((bf16[64,1792]{1,0:T(8,128)(2,1)S(1)}, bf16[64,1792]{1,0:T(8,128)(2,1)S(1)}, u32[]{:S(2)}, u32[]{:S(2)}) %collective-permute-start.9) | collective-permute-done | bytes 229408 | tf_op jit(solution)/shard_map/ppermute | solution.py:46
  33.8 2.1 %collective-permute-done.8.refs_1_ = bf16[64,1792]{1,0:T(8,128)(2,1)S(1)} collective-permute-done((bf16[64,1792]{1,0:T(8,128)(2,1)S(1)}, bf16[64,1792]{1,0:T(8,128)(2,1)S(1)}, u32[]{:S(2)}, u32[]{:S(2)}) %collective-permute-start.8) | collective-permute-done | bytes 229408 | tf_op jit(solution)/shard_map/ppermute | solution.py:46
  36.8 1.5 %collective-permute-start.13 = (bf16[64,1792]{1,0:T(8,128)(2,1)S(1)}, bf16[64,1792]{1,0:T(8,128)(2,1)S(1)}, u32[]{:S(2)}, u32[]{:S(2)}) collective-permute-start(bf16[64,1792]{1,0:T(8,128)(2,1)S(1)} %shard_map.104.refs_0_), channel_id=1, source_target_pairs={{0,2},{1,3},{2,0},{3,1},{4,6},{5,7},{6,4},{7,5},{8,10},{9,11},{10,... | collective-permute-start | bytes 688136 | tf_op jit(solution)/shard_map/ppermute | solution.py:46
  38.5 2.1 %collective-permute-done.11.refs_1_ = bf16[128,1792]{1,0:T(8,128)(2,1)S(1)} collective-permute-done((bf16[128,1792]{1,0:T(8,128)(2,1)S(1)}, bf16[128,1792]{1,0:T(8,128)(2,1)S(1)}, u32[]{:S(2)}, u32[]{:S(2)}) %collective-permute-start.11) | collective-permute-done | bytes 458784 | tf_op jit(solution)/shard_map/ppermute | solution.py:46
  43.1 1.2 %collective-permute-done.14.refs_2_ = bf16[64,1792]{1,0:T(8,128)(2,1)S(1)} collective-permute-done((bf16[64,1792]{1,0:T(8,128)(2,1)S(1)}, bf16[64,1792]{1,0:T(8,128)(2,1)S(1)}, u32[]{:S(2)}, u32[]{:S(2)}) %collective-permute-start.14) | collective-permute-done | bytes 229408 | tf_op jit(solution)/shard_map/ppermute | solution.py:46
  44.5 1.3 %shard_map.107 = (f32[64,1792]{1,0:T(8,128)S(1)}, bf16[64,1792]{1,0:T(8,128)(2,1)S(1)}) custom-call(bf16[256,512]{1,0:T(8,128)(2,1)S(1)} %get-tuple-element.37.refs_0_.grad.refs_3_, bf16[128,512]{1,0:T(8,128)(2,1)S(1)} %shard_map.106.peer, bf16[1792,512]{1,0:T(8,128)(2,1)S(1)} %copy-done, bf16[1792,512]{1,0:T(8,128)(2,1)S(1)} %collective-permute-done.3.refs_3_.weight_peer), custom_call_target="tpu_custom_call" | custom-call | flops 1 | bytes 1 | tf_op jit(solution)/shard_map/pallas_call | solution.py:83
  45.8 1.4 %collective-permute-start.15 = (bf16[64,1792]{1,0:T(8,128)(2,1)S(1)}, bf16[64,1792]{1,0:T(8,128)(2,1)S(1)}, u32[]{:S(2)}, u32[]{:S(2)}) collective-permute-start(bf16[64,1792]{1,0:T(8,128)(2,1)S(1)} %get-tuple-element.42.refs_0_), channel_id=1, source_target_pairs={{0,2},{1,3},{2,0},{3,1},{4,6},{5,7},{6,4},{7,5},{8,10},{9,11},{10,... | collective-permute-start | bytes 688136 | tf_op jit(solution)/shard_map/ppermute | solution.py:46
  48.6 2.0 %collective-permute-start.17 = (bf16[64,1792]{1,0:T(8,128)(2,1)S(1)}, bf16[64,1792]{1,0:T(8,128)(2,1)S(1)}, u32[]{:S(2)}, u32[]{:S(2)}) collective-permute-start(bf16[64,1792]{1,0:T(8,128)(2,1)S(1)} %shard_map.104.refs_0_), channel_id=1, source_target_pairs={{0,4},{1,5},{2,6},{3,7},{4,0},{5,1},{6,2},{7,3},{8,12},{9,13},{10,... | collective-permute-start | bytes 688136 | tf_op jit(solution)/shard_map/ppermute | solution.py:46
  50.9 1.3 %shard_map.111 = (f32[64,1792]{1,0:T(8,128)S(1)}, bf16[64,1792]{1,0:T(8,128)(2,1)S(1)}) custom-call(bf16[256,512]{1,0:T(8,128)(2,1)S(1)} %shard_map.110.grad, bf16[128,512]{1,0:T(8,128)(2,1)S(1)} %collective-permute-done.16.peer, bf16[1792,512]{1,0:T(8,128)(2,1)S(1)} %copy-done, bf16[1792,512]{1,0:T(8,128)(2,1)S(1)} %collective-permute-done.3.refs_3_.weight_peer), custom_call_target="tpu_custom_call" | custom-call | flops 1 | bytes 1 | tf_op jit(solution)/shard_map/pallas_call | solution.py:83
  53.0 1.3 %shard_map.116 = (f32[64,1792]{1,0:T(8,128)S(1)}, bf16[64,1792]{1,0:T(8,128)(2,1)S(1)}) custom-call(bf16[256,512]{1,0:T(8,128)(2,1)S(1)} %shard_map.115.grad, bf16[128,512]{1,0:T(8,128)(2,1)S(1)} %collective-permute-done.20.peer, bf16[1792,512]{1,0:T(8,128)(2,1)S(1)} %copy-done, bf16[1792,512]{1,0:T(8,128)(2,1)S(1)} %collective-permute-done.3.refs_3_.weight_peer), custom_call_target="tpu_custom_call" | custom-call | flops 1 | bytes 1 | tf_op jit(solution)/shard_map/pallas_call | solution.py:83
  54.3 1.4 %collective-permute-start.29 = (bf16[64,1792]{1,0:T(8,128)(2,1)S(1)}, bf16[64,1792]{1,0:T(8,128)(2,1)S(1)}, u32[]{:S(2)}, u32[]{:S(2)}) collective-permute-start(bf16[64,1792]{1,0:T(8,128)(2,1)S(1)} %get-tuple-element.50.refs_1_), channel_id=1, source_target_pairs={{0,2},{1,3},{2,0},{3,1},{4,6},{5,7},{6,4},{7,5},{8,10},{9,11},{10,... | collective-permute-start | bytes 688136 | tf_op jit(solution)/shard_map/ppermute | solution.py:46
  55.8 1.3 %collective-permute-done.17.refs_1_.x = bf16[64,1792]{1,0:T(8,128)(2,1)S(1)} collective-permute-done((bf16[64,1792]{1,0:T(8,128)(2,1)S(1)}, bf16[64,1792]{1,0:T(8,128)(2,1)S(1)}, u32[]{:S(2)}, u32[]{:S(2)}) %collective-permute-start.17) | collective-permute-done | bytes 229408 | tf_op jit(solution)/shard_map/ppermute | solution.py:46
  57.1 2.1 %collective-permute-start.19 = (bf16[64,1792]{1,0:T(8,128)(2,1)S(1)}, bf16[64,1792]{1,0:T(8,128)(2,1)S(1)}, u32[]{:S(2)}, u32[]{:S(2)}) collective-permute-start(bf16[64,1792]{1,0:T(8,128)(2,1)S(1)} %shard_map.112.refs_0_.refs_4_), channel_id=1, source_target_pairs={{0,4},{1,5},{2,6},{3,7},{4,0},{5,1},{6,2},{7,3},{8,12},{9,13},{10,... | collective-permute-start | bytes 688136 | tf_op jit(solution)/shard_map/ppermute | solution.py:46
  59.1 2.8 %collective-permute-done.21.refs_3_ = bf16[64,1792]{1,0:T(8,128)(2,1)S(1)} collective-permute-done((bf16[64,1792]{1,0:T(8,128)(2,1)S(1)}, bf16[64,1792]{1,0:T(8,128)(2,1)S(1)}, u32[]{:S(2)}, u32[]{:S(2)}) %collective-permute-start.21) | collective-permute-done | bytes 229408 | tf_op jit(solution)/shard_map/ppermute | solution.py:46
  62.3 0.7 collective-permute-start.23
  63.0 1.3 %shard_map.133 = (f32[64,1792]{1,0:T(8,128)S(1)}, bf16[64,1792]{1,0:T(8,128)(2,1)S(1)}) custom-call(bf16[256,512]{1,0:T(8,128)(2,1)S(1)} %shard_map.132.grad, bf16[128,512]{1,0:T(8,128)(2,1)S(1)} %collective-permute-done.27.peer, bf16[1792,512]{1,0:T(8,128)(2,1)S(1)} %copy-done, bf16[1792,512]{1,0:T(8,128)(2,1)S(1)} %collective-permute-done.3.refs_3_.weight_peer), custom_call_target="tpu_custom_call" | custom-call | flops 1 | bytes 1 | tf_op jit(solution)/shard_map/pallas_call | solution.py:83
  64.4 1.4 %collective-permute-start.28 = (bf16[64,1792]{1,0:T(8,128)(2,1)S(1)}, bf16[64,1792]{1,0:T(8,128)(2,1)S(1)}, u32[]{:S(2)}, u32[]{:S(2)}) collective-permute-start(bf16[64,1792]{1,0:T(8,128)(2,1)S(1)} %get-tuple-element.67), channel_id=1, source_target_pairs={{0,2},{1,3},{2,0},{3,1},{4,6},{5,7},{6,4},{7,5},{8,10},{9,11},{10,... | collective-permute-start | bytes 688136 | tf_op jit(solution)/shard_map/ppermute | solution.py:46
  67.0 2.5 %collective-permute-start.31 = (bf16[64,1792]{1,0:T(8,128)(2,1)S(1)}, bf16[64,1792]{1,0:T(8,128)(2,1)S(1)}, u32[]{:S(2)}, u32[]{:S(2)}) collective-permute-start(bf16[64,1792]{1,0:T(8,128)(2,1)S(1)} %shard_map.117.refs_0_), channel_id=1, source_target_pairs={{0,12},{1,13},{2,14},{3,15},{4,8},{5,9},{6,10},{7,11},{8,4},{9,5},... | collective-permute-start | bytes 688136 | tf_op jit(solution)/shard_map/ppermute | solution.py:46
  71.1 3.7 %shard_map.125 = (f32[512,1792]{1,0:T(8,128)S(1)}, f32[1792,512]{1,0:T(8,128)S(1)}) custom-call(bf16[256,512]{1,0:T(8,128)(2,1)S(1)} %shard_map.118.refs_0_, bf16[256,512]{1,0:T(8,128)(2,1)S(1)} %get-tuple-element.51.refs_1_.refs_0_, bf16[256,512]{1,0:T(8,128)(2,1)S(1)} %get-tuple-element.52.refs_2_, bf16[256,1792]{1,0:T(8,128)(2,1)S(1)} %get-tuple-element.53.refs_3_, ...), custom_call_target="tpu_custom_call" | custom-call | flops 1 | bytes 1 | tf_op jit(solution)/shard_map/pallas_call | solution.py:83
  75.6 2.0 %shard_map.127 = f32[1024,512]{1,0:T(8,128)} custom-call(s32[16]{0:T(128)S(1)} %stack.67.refs_0_, f32[256,512]{1,0:T(8,128)S(1)} %get-tuple-element.39.refs_1_, f32[256,512]{1,0:T(8,128)S(1)} %get-tuple-element.40.refs_2_, f32[256,512]{1,0:T(8,128)S(1)} %get-tuple-element.43.refs_3_, f32[256,512]{1,0:T(8,128)S(1)} %shard_map.126.refs_4_), custom_call_target="tpu_custom_call" | custom-call | flops 1 | bytes 1 | tf_op jit(solution)/shard_map/pallas_call | solution.py:83
  78.4 3.7 %shard_map.131 = (f32[512,1792]{1,0:T(8,128)}, f32[1792,512]{1,0:T(8,128)}, f32[8,128]{1,0:T(8,128)S(1)}) custom-call(bf16[256,512]{1,0:T(8,128)(2,1)S(1)} %get-tuple-element.60.refs_0_, bf16[256,1792]{1,0:T(8,128)(2,1)S(1)} %get-tuple-element.61.refs_1_, bf16[256,1792]{1,0:T(8,128)(2,1)S(1)} %get-tuple-element.62.refs_2_, ...), custom_call_target="tpu_custom_call" | custom-call | flops 1 | bytes 1 | tf_op jit(solution)/shard_map/pallas_call | solution.py:83
  82.0 0.8 %shard_map.136 = f32[64,1792]{1,0:T(8,128)} custom-call(f32[64,1792]{1,0:T(8,128)S(1)} %shard_map.134.own, bf16[64,1792]{1,0:T(8,128)(2,1)S(1)} %collective-permute-done.30.pair, bf16[64,1792]{1,0:T(8,128)(2,1)S(1)} %collective-permute-done.31.far, f32[8,128]{1,0:T(8,128)S(1)} %get-tuple-element.69.token), custom_call_target="tpu_custom_call" | custom-call | flops 1 | bytes 1 | tf_op jit(solution)/shard_map/pallas_call | solution.py:83
  (101 shorter events, 12.5 us)
Async XLA Ops:
  0.6 16.8 %collective-permute-start.3 = (bf16[1792,512]{1,0:T(8,128)(2,1)}, bf16[1792,512]{1,0:T(8,128)(2,1)S(1)}, u32[]{:S(2)}, u32[]{:S(2)}) collective-permute-start(bf16[1792,512]{1,0:T(8,128)(2,1)} %weight.7), channel_id=1, source_target_pairs={{0,1},{1,0},{2,3},{3,2},{4,5},{5,4},{6,7},{7,6},{8,9},{9,8},{10,11... | collective-permute-start | bytes 5505032 | tf_op jit(solution)/shard_map/ppermute | solution.py:46
  1.1 11.9 %collective-permute-start.2 = (bf16[64,1792]{1,0:T(8,128)(2,1)}, bf16[64,1792]{1,0:T(8,128)(2,1)S(1)}, u32[]{:S(2)}, u32[]{:S(2)}) collective-permute-start(bf16[64,1792]{1,0:T(8,128)(2,1)} %bitcast.24), channel_id=1, source_target_pairs={{0,4},{1,5},{2,6},{3,7},{4,0},{5,1},{6,2},{7,3},{8,12},{9,13},{10,... | collective-permute-start | bytes 688136 | tf_op jit(solution)/shard_map/ppermute | solution.py:46
  3.8 13.6 %collective-permute-start.1 = (bf16[64,1792]{1,0:T(8,128)(2,1)}, bf16[64,1792]{1,0:T(8,128)(2,1)S(1)}, u32[]{:S(2)}, u32[]{:S(2)}) collective-permute-start(bf16[64,1792]{1,0:T(8,128)(2,1)} %bitcast.25), channel_id=1, source_target_pairs={{0,12},{1,13},{2,14},{3,15},{4,8},{5,9},{6,10},{7,11},{8,4},{9,5},... | collective-permute-start | bytes 688136 | tf_op jit(solution)/shard_map/ppermute | solution.py:46
  6.3 11.2 %collective-permute-start = (bf16[64,1792]{1,0:T(8,128)(2,1)}, bf16[64,1792]{1,0:T(8,128)(2,1)S(1)}, u32[]{:S(2)}, u32[]{:S(2)}) collective-permute-start(bf16[64,1792]{1,0:T(8,128)(2,1)} %bitcast.26), channel_id=1, source_target_pairs={{0,2},{1,3},{2,0},{3,1},{4,6},{5,7},{6,4},{7,5},{8,10},{9,11},{10,... | collective-permute-start | bytes 688136 | tf_op jit(solution)/shard_map/ppermute | solution.py:46
  17.5 7.2 %collective-permute-start.5 = (bf16[64,1792]{1,0:T(8,128)(2,1)S(1)}, bf16[64,1792]{1,0:T(8,128)(2,1)S(1)}, u32[]{:S(2)}, u32[]{:S(2)}) collective-permute-start(bf16[64,1792]{1,0:T(8,128)(2,1)S(1)} %shard_map.94.refs_0_.refs_4_), channel_id=1, source_target_pairs={{0,2},{1,3},{2,0},{3,1},{4,6},{5,7},{6,4},{7,5},{8,10},{9,11},{10,... | collective-permute-start | bytes 688136 | tf_op jit(solution)/shard_map/ppermute | solution.py:46
  19.1 14.7 %collective-permute-start.7 = (bf16[64,1792]{1,0:T(8,128)(2,1)S(1)}, bf16[64,1792]{1,0:T(8,128)(2,1)S(1)}, u32[]{:S(2)}, u32[]{:S(2)}) collective-permute-start(bf16[64,1792]{1,0:T(8,128)(2,1)S(1)} %shard_map.94.refs_0_.refs_4_), channel_id=1, source_target_pairs={{0,4},{1,5},{2,6},{3,7},{4,0},{5,1},{6,2},{7,3},{8,12},{9,13},{10,... | collective-permute-start | bytes 688136 | tf_op jit(solution)/shard_map/ppermute | solution.py:46
  19.7 14.1 %collective-permute-start.9 = (bf16[64,1792]{1,0:T(8,128)(2,1)S(1)}, bf16[64,1792]{1,0:T(8,128)(2,1)S(1)}, u32[]{:S(2)}, u32[]{:S(2)}) collective-permute-start(bf16[64,1792]{1,0:T(8,128)(2,1)S(1)} %shard_map.95.refs_2_.x), channel_id=1, source_target_pairs={{0,12},{1,13},{2,14},{3,15},{4,8},{5,9},{6,10},{7,11},{8,4},{9,5},... | collective-permute-start | bytes 688136 | tf_op jit(solution)/shard_map/ppermute | solution.py:46
  24.7 9.1 %collective-permute-start.6 = (bf16[64,1792]{1,0:T(8,128)(2,1)S(1)}, bf16[64,1792]{1,0:T(8,128)(2,1)S(1)}, u32[]{:S(2)}, u32[]{:S(2)}) collective-permute-start(bf16[64,1792]{1,0:T(8,128)(2,1)S(1)} %shard_map.96), channel_id=1, source_target_pairs={{0,2},{1,3},{2,0},{3,1},{4,6},{5,7},{6,4},{7,5},{8,10},{9,11},{10,... | collective-permute-start | bytes 688136 | tf_op jit(solution)/shard_map/ppermute | solution.py:46
  26.3 9.6 %collective-permute-start.8 = (bf16[64,1792]{1,0:T(8,128)(2,1)S(1)}, bf16[64,1792]{1,0:T(8,128)(2,1)S(1)}, u32[]{:S(2)}, u32[]{:S(2)}) collective-permute-start(bf16[64,1792]{1,0:T(8,128)(2,1)S(1)} %collective-permute-done.5.refs_0_.refs_5_), channel_id=1, source_target_pairs={{0,4},{1,5},{2,6},{3,7},{4,0},{5,1},{6,2},{7,3},{8,12},{9,13},{10,... | collective-permute-start | bytes 688136 | tf_op jit(solution)/shard_map/ppermute | solution.py:46
  26.3 9.7 %collective-permute-start.4 = (bf16[64,1792]{1,0:T(8,128)(2,1)S(1)}, bf16[64,1792]{1,0:T(8,128)(2,1)S(1)}, u32[]{:S(2)}, u32[]{:S(2)}) collective-permute-start(bf16[64,1792]{1,0:T(8,128)(2,1)S(1)} %copy-done.3), channel_id=1, source_target_pairs={{0,2},{1,3},{2,0},{3,1},{4,6},{5,7},{6,4},{7,5},{8,10},{9,11},{10,... | collective-permute-start | bytes 688136 | tf_op jit(solution)/shard_map/ppermute | solution.py:46
  36.1 5.4 %collective-permute-start.10 = (bf16[512,1792]{1,0:T(8,128)(2,1)S(1)}, bf16[512,1792]{1,0:T(8,128)(2,1)S(1)}, u32[]{:S(2)}, u32[]{:S(2)}) collective-permute-start(bf16[512,1792]{1,0:T(8,128)(2,1)S(1)} %shard_map.98), channel_id=1, source_target_pairs={{0,1},{1,0},{2,3},{3,2},{4,5},{5,4},{6,7},{7,6},{8,9},{9,8},{10,11... | collective-permute-start | bytes 5505032 | tf_op jit(solution)/shard_map/ppermute | solution.py:46
  36.2 8.1 %collective-permute-start.14 = (bf16[64,1792]{1,0:T(8,128)(2,1)S(1)}, bf16[64,1792]{1,0:T(8,128)(2,1)S(1)}, u32[]{:S(2)}, u32[]{:S(2)}) collective-permute-start(bf16[64,1792]{1,0:T(8,128)(2,1)S(1)} %shard_map.105), channel_id=1, source_target_pairs={{0,4},{1,5},{2,6},{3,7},{4,0},{5,1},{6,2},{7,3},{8,12},{9,13},{10,... | collective-permute-start | bytes 688136 | tf_op jit(solution)/shard_map/ppermute | solution.py:46
  36.4 4.2 %collective-permute-start.11 = (bf16[128,1792]{1,0:T(8,128)(2,1)S(1)}, bf16[128,1792]{1,0:T(8,128)(2,1)S(1)}, u32[]{:S(2)}, u32[]{:S(2)}) collective-permute-start(bf16[128,1792]{1,0:T(8,128)(2,1)S(1)} %shard_map.97.refs_8_.refs_0_), channel_id=1, source_target_pairs={{0,1},{1,0},{2,3},{3,2},{4,5},{5,4},{6,7},{7,6},{8,9},{9,8},{10,11... | collective-permute-start | bytes 1376264 | tf_op jit(solution)/shard_map/ppermute | solution.py:46
  36.8 7.6 %collective-permute-start.13 = (bf16[64,1792]{1,0:T(8,128)(2,1)S(1)}, bf16[64,1792]{1,0:T(8,128)(2,1)S(1)}, u32[]{:S(2)}, u32[]{:S(2)}) collective-permute-start(bf16[64,1792]{1,0:T(8,128)(2,1)S(1)} %shard_map.104.refs_0_), channel_id=1, source_target_pairs={{0,2},{1,3},{2,0},{3,1},{4,6},{5,7},{6,4},{7,5},{8,10},{9,11},{10,... | collective-permute-start | bytes 688136 | tf_op jit(solution)/shard_map/ppermute | solution.py:46
  41.3 3.2 %collective-permute-start.12 = (bf16[128,512]{1,0:T(8,128)(2,1)S(1)}, bf16[128,512]{1,0:T(8,128)(2,1)S(1)}, u32[]{:S(2)}, u32[]{:S(2)}) collective-permute-start(bf16[128,512]{1,0:T(8,128)(2,1)S(1)} %slice.63), channel_id=1, source_target_pairs={{0,1},{1,0},{2,3},{3,2},{4,5},{5,4},{6,7},{7,6},{8,9},{9,8},{10,11... | collective-permute-start | bytes 393224 | tf_op jit(solution)/shard_map/ppermute | solution.py:46
  45.8 8.5 %collective-permute-start.15 = (bf16[64,1792]{1,0:T(8,128)(2,1)S(1)}, bf16[64,1792]{1,0:T(8,128)(2,1)S(1)}, u32[]{:S(2)}, u32[]{:S(2)}) collective-permute-start(bf16[64,1792]{1,0:T(8,128)(2,1)S(1)} %get-tuple-element.42.refs_0_), channel_id=1, source_target_pairs={{0,2},{1,3},{2,0},{3,1},{4,6},{5,7},{6,4},{7,5},{8,10},{9,11},{10,... | collective-permute-start | bytes 688136 | tf_op jit(solution)/shard_map/ppermute | solution.py:46
  47.3 3.5 %collective-permute-start.16 = (bf16[128,512]{1,0:T(8,128)(2,1)S(1)}, bf16[128,512]{1,0:T(8,128)(2,1)S(1)}, u32[]{:S(2)}, u32[]{:S(2)}) collective-permute-start(bf16[128,512]{1,0:T(8,128)(2,1)S(1)} %slice.66), channel_id=1, source_target_pairs={{0,1},{1,0},{2,3},{3,2},{4,5},{5,4},{6,7},{7,6},{8,9},{9,8},{10,11... | collective-permute-start | bytes 393224 | tf_op jit(solution)/shard_map/ppermute | solution.py:46
  48.1 4.1 %collective-permute-start.20 = (bf16[128,512]{1,0:T(8,128)(2,1)S(1)}, bf16[128,512]{1,0:T(8,128)(2,1)S(1)}, u32[]{:S(2)}, u32[]{:S(2)}) collective-permute-start(bf16[128,512]{1,0:T(8,128)(2,1)S(1)} %slice.67), channel_id=1, source_target_pairs={{0,1},{1,0},{2,3},{3,2},{4,5},{5,4},{6,7},{7,6},{8,9},{9,8},{10,11... | collective-permute-start | bytes 393224 | tf_op jit(solution)/shard_map/ppermute | solution.py:46
  48.6 8.4 %collective-permute-start.17 = (bf16[64,1792]{1,0:T(8,128)(2,1)S(1)}, bf16[64,1792]{1,0:T(8,128)(2,1)S(1)}, u32[]{:S(2)}, u32[]{:S(2)}) collective-permute-start(bf16[64,1792]{1,0:T(8,128)(2,1)S(1)} %shard_map.104.refs_0_), channel_id=1, source_target_pairs={{0,4},{1,5},{2,6},{3,7},{4,0},{5,1},{6,2},{7,3},{8,12},{9,13},{10,... | collective-permute-start | bytes 688136 | tf_op jit(solution)/shard_map/ppermute | solution.py:46
  50.6 11.4 %collective-permute-start.21 = (bf16[64,1792]{1,0:T(8,128)(2,1)S(1)}, bf16[64,1792]{1,0:T(8,128)(2,1)S(1)}, u32[]{:S(2)}, u32[]{:S(2)}) collective-permute-start(bf16[64,1792]{1,0:T(8,128)(2,1)S(1)} %shard_map.119), channel_id=1, source_target_pairs={{0,4},{1,5},{2,6},{3,7},{4,0},{5,1},{6,2},{7,3},{8,12},{9,13},{10,... | collective-permute-start | bytes 688136 | tf_op jit(solution)/shard_map/ppermute | solution.py:46
  50.8 11.5 %collective-permute-start.27 = (bf16[128,512]{1,0:T(8,128)(2,1)S(1)}, bf16[128,512]{1,0:T(8,128)(2,1)S(1)}, u32[]{:S(2)}, u32[]{:S(2)}) collective-permute-start(bf16[128,512]{1,0:T(8,128)(2,1)S(1)} %slice.75), channel_id=1, source_target_pairs={{0,1},{1,0},{2,3},{3,2},{4,5},{5,4},{6,7},{7,6},{8,9},{9,8},{10,11... | collective-permute-start | bytes 393224 | tf_op jit(solution)/shard_map/ppermute | solution.py:46
  52.2 12.1 %collective-permute-start.18 = (bf16[64,1792]{1,0:T(8,128)(2,1)S(1)}, bf16[64,1792]{1,0:T(8,128)(2,1)S(1)}, u32[]{:S(2)}, u32[]{:S(2)}) collective-permute-start(bf16[64,1792]{1,0:T(8,128)(2,1)S(1)} %get-tuple-element.46.refs_0_), channel_id=1, source_target_pairs={{0,2},{1,3},{2,0},{3,1},{4,6},{5,7},{6,4},{7,5},{8,10},{9,11},{10,... | collective-permute-start | bytes 688136 | tf_op jit(solution)/shard_map/ppermute | solution.py:46
  54.3 16.1 %collective-permute-start.29 = (bf16[64,1792]{1,0:T(8,128)(2,1)S(1)}, bf16[64,1792]{1,0:T(8,128)(2,1)S(1)}, u32[]{:S(2)}, u32[]{:S(2)}) collective-permute-start(bf16[64,1792]{1,0:T(8,128)(2,1)S(1)} %get-tuple-element.50.refs_1_), channel_id=1, source_target_pairs={{0,2},{1,3},{2,0},{3,1},{4,6},{5,7},{6,4},{7,5},{8,10},{9,11},{10,... | collective-permute-start | bytes 688136 | tf_op jit(solution)/shard_map/ppermute | solution.py:46
  57.1 9.2 %collective-permute-start.19 = (bf16[64,1792]{1,0:T(8,128)(2,1)S(1)}, bf16[64,1792]{1,0:T(8,128)(2,1)S(1)}, u32[]{:S(2)}, u32[]{:S(2)}) collective-permute-start(bf16[64,1792]{1,0:T(8,128)(2,1)S(1)} %shard_map.112.refs_0_.refs_4_), channel_id=1, source_target_pairs={{0,4},{1,5},{2,6},{3,7},{4,0},{5,1},{6,2},{7,3},{8,12},{9,13},{10,... | collective-permute-start | bytes 688136 | tf_op jit(solution)/shard_map/ppermute | solution.py:46
  62.1 7.5 %collective-permute-start.22 = (bf16[256,1792]{1,0:T(8,128)(2,1)S(1)}, bf16[256,1792]{1,0:T(8,128)(2,1)S(1)}, u32[]{:S(2)}, u32[]{:S(2)}) collective-permute-start(bf16[256,1792]{1,0:T(8,128)(2,1)S(1)} %shard_map.120), channel_id=1, source_target_pairs={{0,1},{1,0},{2,3},{3,2},{4,5},{5,4},{6,7},{7,6},{8,9},{9,8},{10,11... | collective-permute-start | bytes 2752520 | tf_op jit(solution)/shard_map/ppermute | solution.py:46
  62.3 12.5 %collective-permute-start.23 = (bf16[64,1792]{1,0:T(8,128)(2,1)S(1)}, bf16[64,1792]{1,0:T(8,128)(2,1)S(1)}, u32[]{:S(2)}, u32[]{:S(2)}) collective-permute-start(bf16[64,1792]{1,0:T(8,128)(2,1)S(1)} %shard_map.128.refs_0_), channel_id=1, source_target_pairs={{0,2},{1,3},{2,0},{3,1},{4,6},{5,7},{6,4},{7,5},{8,10},{9,11},{10,... | collective-permute-start | bytes 688136 | tf_op jit(solution)/shard_map/ppermute | solution.py:46
  64.4 11.1 %collective-permute-start.28 = (bf16[64,1792]{1,0:T(8,128)(2,1)S(1)}, bf16[64,1792]{1,0:T(8,128)(2,1)S(1)}, u32[]{:S(2)}, u32[]{:S(2)}) collective-permute-start(bf16[64,1792]{1,0:T(8,128)(2,1)S(1)} %get-tuple-element.67), channel_id=1, source_target_pairs={{0,2},{1,3},{2,0},{3,1},{4,6},{5,7},{6,4},{7,5},{8,10},{9,11},{10,... | collective-permute-start | bytes 688136 | tf_op jit(solution)/shard_map/ppermute | solution.py:46
  67.0 15.0 %collective-permute-start.31 = (bf16[64,1792]{1,0:T(8,128)(2,1)S(1)}, bf16[64,1792]{1,0:T(8,128)(2,1)S(1)}, u32[]{:S(2)}, u32[]{:S(2)}) collective-permute-start(bf16[64,1792]{1,0:T(8,128)(2,1)S(1)} %shard_map.117.refs_0_), channel_id=1, source_target_pairs={{0,12},{1,13},{2,14},{3,15},{4,8},{5,9},{6,10},{7,11},{8,4},{9,5},... | collective-permute-start | bytes 688136 | tf_op jit(solution)/shard_map/ppermute | solution.py:46
  70.4 11.7 %collective-permute-start.30 = (bf16[64,1792]{1,0:T(8,128)(2,1)S(1)}, bf16[64,1792]{1,0:T(8,128)(2,1)S(1)}, u32[]{:S(2)}, u32[]{:S(2)}) collective-permute-start(bf16[64,1792]{1,0:T(8,128)(2,1)S(1)} %shard_map.135), channel_id=1, source_target_pairs={{0,4},{1,5},{2,6},{3,7},{4,0},{5,1},{6,2},{7,3},{8,12},{9,13},{10,... | collective-permute-start | bytes 688136 | tf_op jit(solution)/shard_map/ppermute | solution.py:46
  74.9 2.8 %collective-permute-start.25 = (bf16[48,1792]{1,0:T(8,128)(2,1)S(1)}, bf16[48,1792]{1,0:T(8,128)(2,1)S(1)}, u32[]{:S(2)}, u32[]{:S(2)}) collective-permute-start(bf16[48,1792]{1,0:T(8,128)(2,1)S(1)} %get-tuple-element.82), channel_id=1, source_target_pairs={{0,1},{1,0},{2,3},{3,2},{4,5},{5,4},{6,7},{7,6},{8,9},{9,8},{10,11... | collective-permute-start | bytes 516104 | tf_op jit(solution)/shard_map/ppermute | solution.py:46
  74.9 2.8 %collective-permute-start.24 = (bf16[48,1792]{1,0:T(8,128)(2,1)S(1)}, bf16[48,1792]{1,0:T(8,128)(2,1)S(1)}, u32[]{:S(2)}, u32[]{:S(2)}) collective-permute-start(bf16[48,1792]{1,0:T(8,128)(2,1)S(1)} %get-tuple-element.83), channel_id=1, source_target_pairs={{0,1},{1,0},{2,3},{3,2},{4,5},{5,4},{6,7},{7,6},{8,9},{9,8},{10,11... | collective-permute-start | bytes 516104 | tf_op jit(solution)/shard_map/ppermute | solution.py:46
  75.5 2.2 %collective-permute-start.26 = (bf16[32,1792]{1,0:T(8,128)(2,1)S(1)}, bf16[32,1792]{1,0:T(8,128)(2,1)S(1)}, u32[]{:S(2)}, u32[]{:S(2)}) collective-permute-start(bf16[32,1792]{1,0:T(8,128)(2,1)S(1)} %slice.90), channel_id=1, source_target_pairs={{0,1},{1,0},{2,3},{3,2},{4,5},{5,4},{6,7},{7,6},{8,9},{9,8},{10,11... | collective-permute-start | bytes 344072 | tf_op jit(solution)/shard_map/ppermute | solution.py:46
  (6 other events, 37.3 us)
